TPU v7x, 32 devices: a whole 2x2x4 slice. The times are simulated.
32 devices in a mesh: seq: 8 (over y, x, core), head: 4 (over z).
Axes of the slice: x: 2, y: 2, z: 4, core: 2. Of those that a mesh axis runs over, the one named last changes fastest.
Arguments:
- query_new: bfloat16 [1024, 6144], P('seq', 'head'), may hold values from -18 to 18
- key_new: bfloat16 [1024, 6144], P('seq', 'head'), may hold values from -4 to 4
- value_new: bfloat16 [1024, 6144], P('seq', 'head'), may hold values from -6 to 6
- cache_keys: bfloat16 [512, 6144], P(('seq', 'head')), may hold values from -448 to 448
- cache_values: bfloat16 [512, 6144], P(('seq', 'head')), may hold values from -448 to 448
- key_exponent: int32 [128, 48], P(('seq', 'head')), may hold values from -9 to -6
- value_exponent: int32 [128, 48], P(('seq', 'head')), may hold values from -9 to -6
- block_mask: int32 [16, 16], replicated, may hold values 0 or 1
Outputs:
- attended: bfloat16 [1024, 6144], P('seq', 'head')
All inputs are finite; a program needn't handle non-finite values.
Results may differ from a plain program's by a relative error of at most 0.0065.
Values may be sent and summed in bfloat16 or wider, within the bound.
No kernel may reach another device: no remote copies, remote signals or barrier semaphores. Data moves between devices by JAX's collectives and lax.ppermute only.
A program may use at most 64 MiB of HBM per device.

v0:
```python
import functools
import math

import jax
import jax.numpy as jnp
from jax import lax
from jax.experimental import pallas as pl
from jax.experimental.pallas import tpu as pltpu
from jax.sharding import PartitionSpec as P

DH = 128
QBLK = 64
CBLK = 32
SBLK = 4
MASKED = -1e30
SMALL = 8 * 2**20
LARGE = 16 * 2**20


def partner(index, step, count):
    if count & (count - 1) == 0:
        return index ^ step
    return (index + step) % count


def origin(index, step, count):
    if count & (count - 1) == 0:
        return index ^ step
    return (index + count - step) % count


def columns(chunk, width):
    return pl.ds(pl.multiple_of(chunk * width, DH), width)


def vmem(count):
    return [pl.BlockSpec(memory_space=pltpu.VMEM)] * count


def prepare_kernel(groups, gather, shards, *refs):
    new_refs, cache_refs, outs, scratch = refs[:3], refs[3:7], refs[7:-6], refs[-6:]
    pieces, cached = outs[:groups], outs[groups:]
    ck_buf, cv_buf, ke_buf, ve_buf, cache_sems, new_sems = scratch
    group, shard = lax.axis_index("seq") // gather, lax.axis_index("head")

    loads = [
        pltpu.make_async_copy(src, dst, cache_sems.at[i])
        for i, (src, dst) in enumerate(zip(cache_refs, (ck_buf, cv_buf, ke_buf, ve_buf)))
    ]
    rows, width = pieces[0].shape[0] // 3, pieces[0].shape[1]
    copies = []
    for t in range(groups):
        cols = columns(partner(group, t, groups), width)
        for i, src in enumerate(new_refs):
            dst = pieces[t].at[pl.ds(i * rows, rows)]
            copies.append(pltpu.make_async_copy(src.at[:, cols], dst, new_sems.at[t, i]))
    for copy in loads + copies:
        copy.start()
    for copy in loads:
        copy.wait()

    blocks, heads = ke_buf.shape
    cache_rows = ck_buf.shape[0]
    exponent = jnp.concatenate(
        [
            jnp.broadcast_to(ref[i : i + 1], (SBLK, heads))
            for ref in (ke_buf, ve_buf)
            for i in range(blocks)
        ],
        axis=0,
    )
    power = jnp.left_shift(1, exponent + 16).astype(jnp.float32) * 2.0**-16
    power = power.astype(jnp.bfloat16)
    head = lax.broadcasted_iota(jnp.int32, (heads, width), 0)
    head -= lax.broadcasted_iota(jnp.int32, (heads, width), 1) // DH
    for t in range(groups):
        for s in range(shards):
            part = partner(shard, s, shards) * groups + partner(group, t, groups)
            spread = (head == part * (width // DH)).astype(jnp.float32).astype(jnp.bfloat16)
            factor = jnp.dot(power, spread, preferred_element_type=jnp.float32)
            for which, buf in enumerate((ck_buf, cv_buf)):
                mantissa = buf[:, columns(part, width)].astype(jnp.float32)
                scaled = mantissa * factor[which * cache_rows : (which + 1) * cache_rows]
                cached[s][t, which] = scaled.astype(jnp.bfloat16)
    for copy in copies:
        copy.wait()


def prepare(q, k, v, ck, cv, ke, ve, groups, gather, shards):
    rows, width = q.shape[0], q.shape[1] // groups
    operands = (k, v, q, ck, cv, ke, ve)
    outs = pl.pallas_call(
        functools.partial(prepare_kernel, groups, gather, shards),
        out_shape=[jax.ShapeDtypeStruct((3 * rows, width), jnp.bfloat16)] * groups
        + [jax.ShapeDtypeStruct((groups, 2, ck.shape[0], width), jnp.bfloat16)] * shards,
        in_specs=[pl.BlockSpec(memory_space=pltpu.HBM)] * len(operands),
        out_specs=vmem(groups + shards),
        scratch_shapes=[pltpu.VMEM(x.shape, x.dtype) for x in (ck, cv, ke, ve)]
        + [pltpu.SemaphoreType.DMA((4,)), pltpu.SemaphoreType.DMA((groups, 3))],
        compiler_params=pltpu.CompilerParams(vmem_limit_bytes=SMALL),
        cost_estimate=pl.CostEstimate(
            flops=4 * ck.size, bytes_accessed=12 * q.size + 8 * ck.size, transcendentals=0
        ),
        name="prepare",
    )(*[pltpu.with_memory_space_constraint(x, pltpu.HBM) for x in operands])
    return list(outs[:groups]), list(outs[groups:])


def interleave_kernel(*refs):
    rows = refs[0].shape[1]
    for which in range(2):
        for s, ref in enumerate(refs[:-1]):
            refs[-1][pl.ds((which * len(refs[:-1]) + s) * rows, rows)] = ref[which]


def interleave(pieces):
    _, rows, width = pieces[0].shape
    count = len(pieces)
    if rows % 16:
        return jnp.stack(pieces, axis=1).reshape(-1, width)
    return pl.pallas_call(
        interleave_kernel,
        out_shape=jax.ShapeDtypeStruct((2 * count * rows, width), jnp.bfloat16),
        in_specs=vmem(count),
        out_specs=vmem(1)[0],
        compiler_params=pltpu.CompilerParams(vmem_limit_bytes=SMALL),
        cost_estimate=pl.CostEstimate(
            flops=0, bytes_accessed=8 * count * rows * width, transcendentals=0
        ),
        name="interleave",
    )(*pieces)


def join_kernel(rows, *refs):
    for i, ref in enumerate(refs[:-1]):
        refs[-1][i] = ref[pl.ds(0, rows)]


def join(pieces, rows):
    shape = (len(pieces), rows, pieces[0].shape[1])
    return pl.pallas_call(
        functools.partial(join_kernel, rows),
        out_shape=jax.ShapeDtypeStruct(shape, jnp.bfloat16),
        in_specs=vmem(len(pieces)),
        out_specs=vmem(1)[0],
        compiler_params=pltpu.CompilerParams(vmem_limit_bytes=SMALL),
        cost_estimate=pl.CostEstimate(
            flops=0, bytes_accessed=4 * math.prod(shape), transcendentals=0
        ),
        name="join",
    )(*pieces)


def rows_of(refs, start, count, cols):
    parts = []
    for ref in refs:
        if len(ref.shape) == 2:
            parts.append(ref[start : start + count, cols])
        else:
            parts.append(ref[:, start : start + count, cols].reshape(-1, cols.stop - cols.start))
    return parts[0] if len(parts) == 1 else jnp.concatenate(parts, axis=0)


def attend_sets(queries, sets):
    scale = math.log2(math.e) / math.sqrt(DH)
    scores = []
    for keys, _, bias in sets:
        x = lax.dot_general(
            queries, keys, (((1,), (1,)), ((), ())), preferred_element_type=jnp.float32
        )
        scores.append(x * scale if bias is None else x * scale + bias)
    peak = functools.reduce(
        jnp.maximum, [jnp.max(x, axis=1, keepdims=True) for x in scores]
    )
    total, product = 0.0, 0.0
    for x, (_, values, _) in zip(scores, sets):
        raised = jnp.exp2(x - peak)
        total += jnp.sum(raised, axis=1, keepdims=True)
        product += jnp.dot(
            raised.astype(jnp.bfloat16), values, preferred_element_type=jnp.float32
        )
    return peak, total, product


def bias_rows(bias_ref, pieces, blocks):
    width = bias_ref.shape[1]
    return jnp.concatenate(
        [
            jnp.broadcast_to(bias_ref[row : row + 1], (QBLK, width))
            for t in pieces
            for row in range(t * blocks, (t + 1) * blocks)
        ],
        axis=0,
    )


def attend_kernel(pieces, counts, q_start, rows, merge, final, *refs):
    q_refs, refs = refs[: len(pieces)], refs[len(pieces) :]
    sets = []
    for count, masked in counts:
        bias = bias_rows(refs[count], pieces, rows // QBLK) if masked else None
        sets.append((refs[:count], refs[0].shape[-2] // 2 if masked else rows, bias))
        refs = refs[count + masked :]
    state, refs = (refs[:3], refs[3:]) if merge else (None, refs)
    width = q_refs[0].shape[1]
    for at in range(0, width, DH):
        cols = slice(at, at + DH)
        queries = rows_of(q_refs, q_start, rows, cols)
        peak, total, product = attend_sets(
            queries,
            [
                (rows_of(k_refs, 0, half, cols), rows_of(k_refs, half, half, cols), bias)
                for k_refs, half, bias in sets
            ],
        )
        if merge:
            peak_1, total_1, product_1 = [ref[:, cols] for ref in state]
            top = jnp.maximum(peak, peak_1)
            share, share_1 = jnp.exp2(peak - top), jnp.exp2(peak_1 - top)
            total = total * share + total_1 * share_1
            product = product * share + product_1 * share_1
            peak = top
        if final:
            result = (product / total).astype(jnp.bfloat16)
            for i in range(len(pieces)):
                refs[i][:, cols] = result[i * rows : (i + 1) * rows]
        else:
            for ref, x in zip(refs, (peak, total, product)):
                ref[:, cols] = jnp.broadcast_to(x, product.shape)


def attend(q, pieces, sets, state=(), final=False):
    groups = len(pieces)
    rows, width = q[0].shape[0] // 3, q[0].shape[1]
    count = 0
    for arrays, bias in sets:
        for x in arrays:
            stacked = x.shape[0] if x.ndim == 3 else 1
            count += stacked * (rows if bias is None else x.shape[-2] // 2)
    if final:
        out_shape = [jax.ShapeDtypeStruct((rows, width), jnp.bfloat16)] * groups
    else:
        out_shape = [jax.ShapeDtypeStruct((groups * rows, width), jnp.float32)] * 3
    operands = [q[t] for t in pieces]
    for arrays, bias in sets:
        operands += [*arrays] if bias is None else [*arrays, bias]
    operands += state
    return pl.pallas_call(
        functools.partial(
            attend_kernel,
            tuple(pieces),
            tuple((len(arrays), bias is not None) for arrays, bias in sets),
            2 * rows,
            rows,
            bool(state),
            final,
        ),
        out_shape=out_shape,
        in_specs=vmem(len(operands)),
        out_specs=vmem(len(out_shape)),
        compiler_params=pltpu.CompilerParams(vmem_limit_bytes=LARGE),
        cost_estimate=pl.CostEstimate(
            flops=4 * groups * rows * count * width,
            bytes_accessed=4 * count * width,
            transcendentals=groups * rows * count * width // DH,
        ),
        name="attend",
    )(*operands)


def unpack_kernel(steps, gather, width, *refs):
    groups = len(steps)
    parts, out_ref, sems = refs[:groups], refs[groups], refs[groups + 1]
    me = lax.axis_index("seq") // gather
    copies = [
        pltpu.make_async_copy(
            parts[i], out_ref.at[:, columns(partner(me, t, groups), width)], sems.at[i]
        )
        for i, t in enumerate(steps)
    ]
    for copy in copies:
        copy.start()
    for copy in copies:
        copy.wait()


def unpack(parts, steps, gather):
    rows, width = parts[0].shape
    groups = len(steps)
    return pl.pallas_call(
        functools.partial(unpack_kernel, tuple(steps), gather, width),
        out_shape=jax.ShapeDtypeStruct((rows, groups * width), jnp.bfloat16),
        in_specs=vmem(groups),
        out_specs=pl.BlockSpec(memory_space=pl.ANY),
        scratch_shapes=[pltpu.SemaphoreType.DMA((groups,))],
        compiler_params=pltpu.CompilerParams(vmem_limit_bytes=SMALL),
        cost_estimate=pl.CostEstimate(
            flops=0, bytes_accessed=4 * groups * rows * width, transcendentals=0
        ),
        name="unpack_heads",
    )(*parts)


def per_device(
    seq_count,
    head_count,
    query_new,
    key_new,
    value_new,
    cache_keys,
    cache_values,
    key_exponent,
    value_exponent,
    block_mask,
):
    tok_rows, width_dev = query_new.shape
    groups = math.gcd(width_dev // DH, seq_count)
    gather = seq_count // groups
    width = width_dev // groups
    cache_rows = cache_keys.shape[0]
    seq_index = lax.axis_index("seq")
    head_index = lax.axis_index("head")
    group, member = seq_index // gather, seq_index % gather

    def to_group(x, t):
        if t == 0:
            return x
        pairs = [
            (s, partner(s // gather, t, groups) * gather + s % gather) for s in range(seq_count)
        ]
        return lax.ppermute(x, "seq", pairs)

    def from_group(x, t):
        if t == 0:
            return x
        pairs = [
            (s, origin(s // gather, t, groups) * gather + s % gather) for s in range(seq_count)
        ]
        return lax.ppermute(x, "seq", pairs)

    def to_member(x, t):
        pairs = [
            (s, s // gather * gather + partner(s % gather, t, gather)) for s in range(seq_count)
        ]
        return lax.ppermute(x, "seq", pairs)

    def to_head(x, t):
        if t == 0:
            return x
        return lax.ppermute(x, "head", [(h, partner(h, t, head_count)) for h in range(head_count)])

    members = range(1, gather)
    kv_own, stored = prepare(
        query_new,
        key_new,
        value_new,
        cache_keys,
        cache_values,
        key_exponent,
        value_exponent,
        groups,
        gather,
        head_count,
    )
    kv_other = [to_member(kv_own[0][: 2 * tok_rows], s) for s in members]
    if gather > 1:
        kv_own[1:-1], stored, kv_other[0] = lax.optimization_barrier(
            (kv_own[1:-1], stored, kv_other[0])
        )
    kv = [to_group(kv_own[t], t) for t in range(groups)]
    by_head = []
    for s in range(head_count):
        x = stored[s]
        if s > 2:
            x, by_head[s - 2] = lax.optimization_barrier((x, by_head[s - 2]))
        by_head.append(to_head(x, s))
    kv[1:] = [lax.optimization_barrier((x, by_head))[0] for x in kv[1:]]
    block_mask, group, member, head_index, _ = lax.optimization_barrier(
        (block_mask, group, member, head_index, kv[1:])
    )
    cache = [to_group(interleave([x[t] for x in by_head]), t) for t in range(groups)]
    if groups > 1:
        swap = join(kv[1:], 2 * tok_rows)
        kv_other += [to_member(swap, s) for s in members]

    q_source = jnp.stack([origin(group, t, groups) * gather + member for t in range(groups)])
    blocks = tok_rows // QBLK
    q_block = (q_source[:, None] * blocks + jnp.arange(blocks)[None, :]).reshape(-1)
    q_pick = (q_block[:, None] == jnp.arange(block_mask.shape[0])[None, :]).astype(jnp.float32)
    row_mask = jnp.dot(q_pick, block_mask.astype(jnp.float32))

    def bias_of(steps):
        device = jnp.stack(
            [
                (origin(group, t, groups) * gather + origin(member, s, gather)) * head_count
                + origin(head_index, z, head_count)
                for s in steps
                for t in range(groups)
                for z in range(head_count)
            ]
        )
        block = (device[:, None] * cache_rows + jnp.arange(cache_rows)[None, :]).reshape(-1)
        pick = jnp.arange(block_mask.shape[1])[:, None] == (block // CBLK)[None, :]
        seen = jnp.dot(row_mask, pick.astype(jnp.float32))
        return jnp.where(seen > 0.5, 0.0, MASKED).astype(jnp.float32)

    every = range(groups)
    steps = [*every[-1:], *every[1:-1], *every[:1]] if groups > 1 else [0]
    bias = [bias_of([0])] + ([bias_of(members)] if gather > 1 else [])
    away = steps[:-1]
    if groups > 1:
        state = attend(kv, away, [(kv, None)])
        cache, state, bias = lax.optimization_barrier((cache, state, bias))
    sets, last = [(cache, bias[0])], []
    if gather > 1:
        swap = join(cache, cache[0].shape[0])
        sets.append((kv_other, None))
        last = [([to_member(swap, s) for s in members], bias[1])]
    parts = {}
    if groups > 1:
        state = attend(kv, away, sets, state, not last)
        if last:
            state = attend(kv, away, last, state, True)
        parts.update(zip(away, state))
    parts[0] = attend(kv, [0], [(kv, None), *sets, *last], (), True)[0]
    return unpack([from_group(parts[t], t) for t in steps], steps, gather)


def solution(mesh):
    return jax.shard_map(
        functools.partial(per_device, mesh.shape["seq"], mesh.shape["head"]),
        mesh=mesh,
        in_specs=(
            P("seq", "head"),
            P("seq", "head"),
            P("seq", "head"),
            P(("seq", "head"), None),
            P(("seq", "head"), None),
            P(("seq", "head"), None),
            P(("seq", "head"), None),
            P(),
        ),
        out_specs=P("seq", "head"),
        check_vma=False,
    )
```

profile of v0, /device:TPU:0, one launch (start us, length us, event | category | flops | bytes accessed | tf_op | source)
XLA Modules:
  0.0 38.3 jit_solution(5750935340274041875)
XLA Ops:
  0.0 1.8 %prepare.1 = (bf16[384,384]{1,0:T(8,128)(2,1)S(1)}, bf16[384,384]{1,0:T(8,128)(2,1)S(1)}, bf16[384,384]{1,0:T(8,128)(2,1)S(1)}, bf16[384,384]{1,0:T(8,128)(2,1)S...) custom-call(bf16[128,1536]{1,0:T(8,128)(2,1)} %refs_0_.1, ...), custom_call_target="tpu_custom_call" | custom-call | flops 393216 | bytes 3145728 | tf_op jit(solution)/shard_map/prepare/pallas_call | solution.py:92
  1.8 0.5 %collective-permute-start.1 = (bf16[256,384]{1,0:T(8,128)(2,1)S(1)}, bf16[256,384]{1,0:T(8,128)(2,1)S(1)}, u32[]{:S(2)}, u32[]{:S(2)}) collective-permute-start(bf16[256,384]{1,0:T(8,128)(2,1)S(1)} %slice.51), channel_id=1, source_target_pairs={{0,4},{4,0},{8,12},{12,8},{16,20},{20,16},{24,28},{28,24},{1,5},{5... | collective-permute-start | bytes 589832 | tf_op jit(solution)/shard_map/ppermute | solution.py:345
  2.4 3.5 %collective-permute-start = (bf16[384,384]{1,0:T(8,128)(2,1)S(1)}, bf16[384,384]{1,0:T(8,128)(2,1)S(1)}, u32[]{:S(2)}, u32[]{:S(2)}) collective-permute-start(bf16[384,384]{1,0:T(8,128)(2,1)S(1)} %get-tuple-element.47), channel_id=1, source_target_pairs={{0,24},{4,28},{8,16},{12,20},{16,8},{20,12},{24,0},{28,4},{1,25},{... | collective-permute-start | bytes 884744 | tf_op jit(solution)/shard_map/ppermute | solution.py:331
  5.9 1.6 %collective-permute-start.2 = (bf16[4,2,16,384]{3,2,1,0:T(8,128)(2,1)S(1)}, bf16[4,2,16,384]{3,2,1,0:T(8,128)(2,1)S(1)}, u32[]{:S(2)}, u32[]{:S(2)}) collective-permute-start(bf16[4,2,16,384]{3,2,1,0:T(8,128)(2,1)S(1)} %get-tuple-element.57), channel_id=1, source_target_pairs={{0,1},{1,0},{2,3},{3,2},{4,5},{5,4},{6,7},{7,6},{8,9},{9,8},{10,11... | collective-permute-start | bytes 294920 | tf_op jit(solution)/shard_map/ppermute | solution.py:350
  7.5 2.7 %collective-permute-start.3 = (bf16[4,2,16,384]{3,2,1,0:T(8,128)(2,1)S(1)}, bf16[4,2,16,384]{3,2,1,0:T(8,128)(2,1)S(1)}, u32[]{:S(2)}, u32[]{:S(2)}) collective-permute-start(bf16[4,2,16,384]{3,2,1,0:T(8,128)(2,1)S(1)} %get-tuple-element.59), channel_id=1, source_target_pairs={{0,2},{1,3},{2,0},{3,1},{4,6},{5,7},{6,4},{7,5},{8,10},{9,11},{10,... | collective-permute-start | bytes 294920 | tf_op jit(solution)/shard_map/ppermute | solution.py:350
  10.1 0.5 %collective-permute-start.5 = (bf16[384,384]{1,0:T(8,128)(2,1)S(1)}, bf16[384,384]{1,0:T(8,128)(2,1)S(1)}, u32[]{:S(2)}, u32[]{:S(2)}) collective-permute-start(bf16[384,384]{1,0:T(8,128)(2,1)S(1)} %get-tuple-element.62), channel_id=1, source_target_pairs={{0,8},{4,12},{8,0},{12,4},{16,24},{20,28},{24,16},{28,20},{1,9},{5... | collective-permute-start | bytes 884744 | tf_op jit(solution)/shard_map/ppermute | solution.py:331
  10.7 1.4 %collective-permute-start.6 = (bf16[384,384]{1,0:T(8,128)(2,1)S(1)}, bf16[384,384]{1,0:T(8,128)(2,1)S(1)}, u32[]{:S(2)}, u32[]{:S(2)}) collective-permute-start(bf16[384,384]{1,0:T(8,128)(2,1)S(1)} %get-tuple-element.64), channel_id=1, source_target_pairs={{0,16},{4,20},{8,24},{12,28},{16,0},{20,4},{24,8},{28,12},{1,17},{... | collective-permute-start | bytes 884744 | tf_op jit(solution)/shard_map/ppermute | solution.py:331
  12.1 3.4 %collective-permute-start.4 = (bf16[4,2,16,384]{3,2,1,0:T(8,128)(2,1)S(1)}, bf16[4,2,16,384]{3,2,1,0:T(8,128)(2,1)S(1)}, u32[]{:S(2)}, u32[]{:S(2)}) collective-permute-start(bf16[4,2,16,384]{3,2,1,0:T(8,128)(2,1)S(1)} %get-tuple-element.60), channel_id=1, source_target_pairs={{0,3},{1,2},{2,1},{3,0},{4,7},{5,6},{6,5},{7,4},{8,11},{9,10},{10,... | collective-permute-start | bytes 294920 | tf_op jit(solution)/shard_map/ppermute | solution.py:350
  15.5 3.1 %collective-permute-done.4 = bf16[4,2,16,384]{3,2,1,0:T(8,128)(2,1)S(1)} collective-permute-done((bf16[4,2,16,384]{3,2,1,0:T(8,128)(2,1)S(1)}, bf16[4,2,16,384]{3,2,1,0:T(8,128)(2,1)S(1)}, u32[]{:S(2)}, u32[]{:S(2)}) %collective-permute-start.4) | collective-permute-done | bytes 98336 | tf_op jit(solution)/shard_map/ppermute | solution.py:350
  18.7 0.7 %collective-permute-start.7 = (bf16[128,384]{1,0:T(8,128)(2,1)S(1)}, bf16[128,384]{1,0:T(8,128)(2,1)S(1)}, u32[]{:S(2)}, u32[]{:S(2)}) collective-permute-start(bf16[128,384]{1,0:T(8,128)(2,1)S(1)} %interleave.5), channel_id=1, source_target_pairs={{0,8},{4,12},{8,0},{12,4},{16,24},{20,28},{24,16},{28,20},{1,9},{5... | collective-permute-start | bytes 294920 | tf_op jit(solution)/shard_map/ppermute | solution.py:331
  19.4 1.6 %collective-permute-start.8 = (bf16[128,384]{1,0:T(8,128)(2,1)S(1)}, bf16[128,384]{1,0:T(8,128)(2,1)S(1)}, u32[]{:S(2)}, u32[]{:S(2)}) collective-permute-start(bf16[128,384]{1,0:T(8,128)(2,1)S(1)} %interleave.6), channel_id=1, source_target_pairs={{0,16},{4,20},{8,24},{12,28},{16,0},{20,4},{24,8},{28,12},{1,17},{... | collective-permute-start | bytes 294920 | tf_op jit(solution)/shard_map/ppermute | solution.py:331
  21.0 1.4 %collective-permute-start.9 = (bf16[128,384]{1,0:T(8,128)(2,1)S(1)}, bf16[128,384]{1,0:T(8,128)(2,1)S(1)}, u32[]{:S(2)}, u32[]{:S(2)}) collective-permute-start(bf16[128,384]{1,0:T(8,128)(2,1)S(1)} %interleave.7), channel_id=1, source_target_pairs={{0,24},{4,28},{8,16},{12,20},{16,8},{20,12},{24,0},{28,4},{1,25},{... | collective-permute-start | bytes 294920 | tf_op jit(solution)/shard_map/ppermute | solution.py:331
  22.5 0.1 stack.155
  22.6 0.1 stack.138
  22.9 0.1 add.233
  23.3 0.1 add.277
  23.4 0.4 %copy-done = s32[16,16]{1,0:T(8,128)S(1)} copy-done((s32[16,16]{1,0:T(8,128)S(1)}, s32[16,16]{1,0:T(8,128)}, u32[]{:S(2)}) %copy-start) | copy-done | bytes 1048
  23.9 0.2 fusion.4
  24.1 0.1 fusion.1.refs_7_.refs_9_
  24.2 0.1 fusion.refs_4_.refs_13_
  24.3 1.1 %attend.4 = (f32[384,384]{1,0:T(8,128)S(1)}, f32[384,384]{1,0:T(8,128)S(1)}, f32[384,384]{1,0:T(8,128)S(1)}) custom-call(bf16[384,384]{1,0:T(8,128)(2,1)S(1)} %collective-permute-done.refs_0_.refs_6_.refs_2_.refs_4_, bf16[384,384]{1,0:T(8,128)(2,1)S(1)} %collective-permute-done.5.refs_1_.refs_4_.refs_0_.refs_2_, ...), custom_call_target="tpu_custom_call" | custom-call | flops 301989888 | bytes 786432 | tf_op jit(solution)/shard_map/attend/pallas_call | solution.py:248
  25.4 1.1 %collective-permute-done.9.refs_3_.refs_6_.refs_8_ = bf16[128,384]{1,0:T(8,128)(2,1)S(1)} collective-permute-done((bf16[128,384]{1,0:T(8,128)(2,1)S(1)}, bf16[128,384]{1,0:T(8,128)(2,1)S(1)}, u32[]{:S(2)}, u32[]{:S(2)}) %collective-permute-start.9) | collective-permute-done | bytes 98336 | tf_op jit(solution)/shard_map/ppermute | solution.py:331
  26.7 1.7 %attend.5 = (f32[384,384]{1,0:T(8,128)S(1)}, f32[384,384]{1,0:T(8,128)S(1)}, f32[384,384]{1,0:T(8,128)S(1)}) custom-call(bf16[384,384]{1,0:T(8,128)(2,1)S(1)} %collective-permute-done.refs_0_.refs_6_.refs_2_.refs_4_, bf16[384,384]{1,0:T(8,128)(2,1)S(1)} %collective-permute-done.5.refs_1_.refs_4_.refs_0_.refs_2_, ...), custom_call_target="tpu_custom_call" | custom-call | flops 452984832 | bytes 1179648 | tf_op jit(solution)/shard_map/attend/pallas_call | solution.py:248
  28.4 0.8 %attend.6 = (bf16[128,384]{1,0:T(8,128)(2,1)S(1)}, bf16[128,384]{1,0:T(8,128)(2,1)S(1)}, bf16[128,384]{1,0:T(8,128)(2,1)S(1)}) custom-call(bf16[384,384]{1,0:T(8,128)(2,1)S(1)} %collective-permute-done.refs_0_.refs_6_.refs_2_.refs_4_, bf16[384,384]{1,0:T(8,128)(2,1)S(1)} %collective-permute-done.5.refs_1_.refs_4_.refs_0_.refs_2_, ...), custom_call_target="tpu_custom_call" | custom-call | flops 150994944 | bytes 393216 | tf_op jit(solution)/shard_map/attend/pallas_call | solution.py:248
  29.2 1.4 %collective-permute-start.12 = (bf16[128,384]{1,0:T(8,128)(2,1)S(1)}, bf16[128,384]{1,0:T(8,128)(2,1)S(1)}, u32[]{:S(2)}, u32[]{:S(2)}) collective-permute-start(bf16[128,384]{1,0:T(8,128)(2,1)S(1)} %get-tuple-element.86), channel_id=1, source_target_pairs={{0,24},{4,28},{8,16},{12,20},{16,8},{20,12},{24,0},{28,4},{1,25},{... | collective-permute-start | bytes 294920 | tf_op jit(solution)/shard_map/ppermute | solution.py:339
  30.7 0.6 %collective-permute-start.13 = (bf16[128,384]{1,0:T(8,128)(2,1)S(1)}, bf16[128,384]{1,0:T(8,128)(2,1)S(1)}, u32[]{:S(2)}, u32[]{:S(2)}) collective-permute-start(bf16[128,384]{1,0:T(8,128)(2,1)S(1)} %get-tuple-element.87), channel_id=1, source_target_pairs={{0,8},{4,12},{8,0},{12,4},{16,24},{20,28},{24,16},{28,20},{1,9},{5... | collective-permute-start | bytes 294920 | tf_op jit(solution)/shard_map/ppermute | solution.py:339
  31.3 1.5 %collective-permute-start.14 = (bf16[128,384]{1,0:T(8,128)(2,1)S(1)}, bf16[128,384]{1,0:T(8,128)(2,1)S(1)}, u32[]{:S(2)}, u32[]{:S(2)}) collective-permute-start(bf16[128,384]{1,0:T(8,128)(2,1)S(1)} %get-tuple-element.88), channel_id=1, source_target_pairs={{0,16},{4,20},{8,24},{12,28},{16,0},{20,4},{24,8},{28,12},{1,17},{... | collective-permute-start | bytes 294920 | tf_op jit(solution)/shard_map/ppermute | solution.py:339
  32.8 1.4 %attend.7.refs_3_ = bf16[128,384]{1,0:T(8,128)(2,1)S(1)} custom-call(bf16[384,384]{1,0:T(8,128)(2,1)S(1)} %get-tuple-element.54.refs_3_.refs_0_.refs_1_, bf16[384,384]{1,0:T(8,128)(2,1)S(1)} %get-tuple-element.54.refs_3_.refs_0_.refs_1_, bf16[384,384]{1,0:T(8,128)(2,1)S(1)} %collective-permute-done.5.refs_1_.refs_4_.refs_0_.refs_2_, ...), custom_call_target="tpu_custom_call" | custom-call | flops 301989888 | bytes 2359296 | tf_op jit(solution)/shard_map/attend/pallas_call | solution.py:248
  34.3 1.6 %collective-permute-done.12.refs_0_ = bf16[128,384]{1,0:T(8,128)(2,1)S(1)} collective-permute-done((bf16[128,384]{1,0:T(8,128)(2,1)S(1)}, bf16[128,384]{1,0:T(8,128)(2,1)S(1)}, u32[]{:S(2)}, u32[]{:S(2)}) %collective-permute-start.12) | collective-permute-done | bytes 98336 | tf_op jit(solution)/shard_map/ppermute | solution.py:339
  35.8 0.7 %collective-permute-done.13.refs_1_ = bf16[128,384]{1,0:T(8,128)(2,1)S(1)} collective-permute-done((bf16[128,384]{1,0:T(8,128)(2,1)S(1)}, bf16[128,384]{1,0:T(8,128)(2,1)S(1)}, u32[]{:S(2)}, u32[]{:S(2)}) %collective-permute-start.13) | collective-permute-done | bytes 98336 | tf_op jit(solution)/shard_map/ppermute | solution.py:339
  36.5 1.0 %collective-permute-done.14.refs_2_ = bf16[128,384]{1,0:T(8,128)(2,1)S(1)} collective-permute-done((bf16[128,384]{1,0:T(8,128)(2,1)S(1)}, bf16[128,384]{1,0:T(8,128)(2,1)S(1)}, u32[]{:S(2)}, u32[]{:S(2)}) %collective-permute-start.14) | collective-permute-done | bytes 98336 | tf_op jit(solution)/shard_map/ppermute | solution.py:339
  37.5 0.8 %unpack_heads.1 = bf16[128,1536]{1,0:T(8,128)(2,1)} custom-call(bf16[128,384]{1,0:T(8,128)(2,1)S(1)} %collective-permute-done.12.refs_0_, bf16[128,384]{1,0:T(8,128)(2,1)S(1)} %collective-permute-done.13.refs_1_, bf16[128,384]{1,0:T(8,128)(2,1)S(1)} %collective-permute-done.14.refs_2_, bf16[128,384]{1,0:T(8,128)(2,1)S(1)} %attend.7.refs_3_), custom_call_target="tpu_custom_call" | custom-call | bytes 786432 | tf_op jit(solution)/shard_map/unpack_heads/pallas_call | solution.py:290
  (33 shorter events, 0.8 us)
Async XLA Ops:
  1.8 4.0 %collective-permute-start.1 = (bf16[256,384]{1,0:T(8,128)(2,1)S(1)}, bf16[256,384]{1,0:T(8,128)(2,1)S(1)}, u32[]{:S(2)}, u32[]{:S(2)}) collective-permute-start(bf16[256,384]{1,0:T(8,128)(2,1)S(1)} %slice.51), channel_id=1, source_target_pairs={{0,4},{4,0},{8,12},{12,8},{16,20},{20,16},{24,28},{28,24},{1,5},{5... | collective-permute-start | bytes 589832 | tf_op jit(solution)/shard_map/ppermute | solution.py:345
  2.4 18.6 %collective-permute-start = (bf16[384,384]{1,0:T(8,128)(2,1)S(1)}, bf16[384,384]{1,0:T(8,128)(2,1)S(1)}, u32[]{:S(2)}, u32[]{:S(2)}) collective-permute-start(bf16[384,384]{1,0:T(8,128)(2,1)S(1)} %get-tuple-element.47), channel_id=1, source_target_pairs={{0,24},{4,28},{8,16},{12,20},{16,8},{20,12},{24,0},{28,4},{1,25},{... | collective-permute-start | bytes 884744 | tf_op jit(solution)/shard_map/ppermute | solution.py:331
  5.9 6.2 %collective-permute-start.2 = (bf16[4,2,16,384]{3,2,1,0:T(8,128)(2,1)S(1)}, bf16[4,2,16,384]{3,2,1,0:T(8,128)(2,1)S(1)}, u32[]{:S(2)}, u32[]{:S(2)}) collective-permute-start(bf16[4,2,16,384]{3,2,1,0:T(8,128)(2,1)S(1)} %get-tuple-element.57), channel_id=1, source_target_pairs={{0,1},{1,0},{2,3},{3,2},{4,5},{5,4},{6,7},{7,6},{8,9},{9,8},{10,11... | collective-permute-start | bytes 294920 | tf_op jit(solution)/shard_map/ppermute | solution.py:350
  7.5 8.0 %collective-permute-start.3 = (bf16[4,2,16,384]{3,2,1,0:T(8,128)(2,1)S(1)}, bf16[4,2,16,384]{3,2,1,0:T(8,128)(2,1)S(1)}, u32[]{:S(2)}, u32[]{:S(2)}) collective-permute-start(bf16[4,2,16,384]{3,2,1,0:T(8,128)(2,1)S(1)} %get-tuple-element.59), channel_id=1, source_target_pairs={{0,2},{1,3},{2,0},{3,1},{4,6},{5,7},{6,4},{7,5},{8,10},{9,11},{10,... | collective-permute-start | bytes 294920 | tf_op jit(solution)/shard_map/ppermute | solution.py:350
  10.1 12.3 %collective-permute-start.5 = (bf16[384,384]{1,0:T(8,128)(2,1)S(1)}, bf16[384,384]{1,0:T(8,128)(2,1)S(1)}, u32[]{:S(2)}, u32[]{:S(2)}) collective-permute-start(bf16[384,384]{1,0:T(8,128)(2,1)S(1)} %get-tuple-element.62), channel_id=1, source_target_pairs={{0,8},{4,12},{8,0},{12,4},{16,24},{20,28},{24,16},{28,20},{1,9},{5... | collective-permute-start | bytes 884744 | tf_op jit(solution)/shard_map/ppermute | solution.py:331
  10.7 11.8 %collective-permute-start.6 = (bf16[384,384]{1,0:T(8,128)(2,1)S(1)}, bf16[384,384]{1,0:T(8,128)(2,1)S(1)}, u32[]{:S(2)}, u32[]{:S(2)}) collective-permute-start(bf16[384,384]{1,0:T(8,128)(2,1)S(1)} %get-tuple-element.64), channel_id=1, source_target_pairs={{0,16},{4,20},{8,24},{12,28},{16,0},{20,4},{24,8},{28,12},{1,17},{... | collective-permute-start | bytes 884744 | tf_op jit(solution)/shard_map/ppermute | solution.py:331
  12.1 6.6 %collective-permute-start.4 = (bf16[4,2,16,384]{3,2,1,0:T(8,128)(2,1)S(1)}, bf16[4,2,16,384]{3,2,1,0:T(8,128)(2,1)S(1)}, u32[]{:S(2)}, u32[]{:S(2)}) collective-permute-start(bf16[4,2,16,384]{3,2,1,0:T(8,128)(2,1)S(1)} %get-tuple-element.60), channel_id=1, source_target_pairs={{0,3},{1,2},{2,1},{3,0},{4,7},{5,6},{6,5},{7,4},{8,11},{9,10},{10,... | collective-permute-start | bytes 294920 | tf_op jit(solution)/shard_map/ppermute | solution.py:350
  18.7 6.7 %collective-permute-start.7 = (bf16[128,384]{1,0:T(8,128)(2,1)S(1)}, bf16[128,384]{1,0:T(8,128)(2,1)S(1)}, u32[]{:S(2)}, u32[]{:S(2)}) collective-permute-start(bf16[128,384]{1,0:T(8,128)(2,1)S(1)} %interleave.5), channel_id=1, source_target_pairs={{0,8},{4,12},{8,0},{12,4},{16,24},{20,28},{24,16},{28,20},{1,9},{5... | collective-permute-start | bytes 294920 | tf_op jit(solution)/shard_map/ppermute | solution.py:331
  19.4 6.0 %collective-permute-start.8 = (bf16[128,384]{1,0:T(8,128)(2,1)S(1)}, bf16[128,384]{1,0:T(8,128)(2,1)S(1)}, u32[]{:S(2)}, u32[]{:S(2)}) collective-permute-start(bf16[128,384]{1,0:T(8,128)(2,1)S(1)} %interleave.6), channel_id=1, source_target_pairs={{0,16},{4,20},{8,24},{12,28},{16,0},{20,4},{24,8},{28,12},{1,17},{... | collective-permute-start | bytes 294920 | tf_op jit(solution)/shard_map/ppermute | solution.py:331
  21.0 5.6 %collective-permute-start.9 = (bf16[128,384]{1,0:T(8,128)(2,1)S(1)}, bf16[128,384]{1,0:T(8,128)(2,1)S(1)}, u32[]{:S(2)}, u32[]{:S(2)}) collective-permute-start(bf16[128,384]{1,0:T(8,128)(2,1)S(1)} %interleave.7), channel_id=1, source_target_pairs={{0,24},{4,28},{8,16},{12,20},{16,8},{20,12},{24,0},{28,4},{1,25},{... | collective-permute-start | bytes 294920 | tf_op jit(solution)/shard_map/ppermute | solution.py:331
  23.2 0.7 %copy-start = (s32[16,16]{1,0:T(8,128)S(1)}, s32[16,16]{1,0:T(8,128)}, u32[]{:S(2)}) copy-start(s32[16,16]{1,0:T(8,128)} %param.15) | copy-start | bytes 3076
  23.4 3.3 %collective-permute-start.11 = (bf16[3,256,384]{2,1,0:T(8,128)(2,1)S(1)}, bf16[3,256,384]{2,1,0:T(8,128)(2,1)S(1)}, u32[]{:S(2)}, u32[]{:S(2)}) collective-permute-start(bf16[3,256,384]{2,1,0:T(8,128)(2,1)S(1)} %join.3), channel_id=1, source_target_pairs={{0,4},{4,0},{8,12},{12,8},{16,20},{20,16},{24,28},{28,24},{1,5},{5... | collective-permute-start | bytes 1769480 | tf_op jit(solution)/shard_map/ppermute | solution.py:345
  26.6 1.8 %collective-permute-start.10 = (bf16[4,128,384]{2,1,0:T(8,128)(2,1)S(1)}, bf16[4,128,384]{2,1,0:T(8,128)(2,1)S(1)}, u32[]{:S(2)}, u32[]{:S(2)}) collective-permute-start(bf16[4,128,384]{2,1,0:T(8,128)(2,1)S(1)} %join.2), channel_id=1, source_target_pairs={{0,4},{4,0},{8,12},{12,8},{16,20},{20,16},{24,28},{28,24},{1,5},{5... | collective-permute-start | bytes 1179656 | tf_op jit(solution)/shard_map/ppermute | solution.py:345
  29.2 6.6 %collective-permute-start.12 = (bf16[128,384]{1,0:T(8,128)(2,1)S(1)}, bf16[128,384]{1,0:T(8,128)(2,1)S(1)}, u32[]{:S(2)}, u32[]{:S(2)}) collective-permute-start(bf16[128,384]{1,0:T(8,128)(2,1)S(1)} %get-tuple-element.86), channel_id=1, source_target_pairs={{0,24},{4,28},{8,16},{12,20},{16,8},{20,12},{24,0},{28,4},{1,25},{... | collective-permute-start | bytes 294920 | tf_op jit(solution)/shard_map/ppermute | solution.py:339
  30.7 5.9 %collective-permute-start.13 = (bf16[128,384]{1,0:T(8,128)(2,1)S(1)}, bf16[128,384]{1,0:T(8,128)(2,1)S(1)}, u32[]{:S(2)}, u32[]{:S(2)}) collective-permute-start(bf16[128,384]{1,0:T(8,128)(2,1)S(1)} %get-tuple-element.87), channel_id=1, source_target_pairs={{0,8},{4,12},{8,0},{12,4},{16,24},{20,28},{24,16},{28,20},{1,9},{5... | collective-permute-start | bytes 294920 | tf_op jit(solution)/shard_map/ppermute | solution.py:339
  31.3 6.2 %collective-permute-start.14 = (bf16[128,384]{1,0:T(8,128)(2,1)S(1)}, bf16[128,384]{1,0:T(8,128)(2,1)S(1)}, u32[]{:S(2)}, u32[]{:S(2)}) collective-permute-start(bf16[128,384]{1,0:T(8,128)(2,1)S(1)} %get-tuple-element.88), channel_id=1, source_target_pairs={{0,16},{4,20},{8,24},{12,28},{16,0},{20,4},{24,8},{28,12},{1,17},{... | collective-permute-start | bytes 294920 | tf_op jit(solution)/shard_map/ppermute | solution.py:339
where the time goes:
time: 38.5 us; the launch traced here: 38.3 us
  starting transfers between devices  21 us (55%)
  Pallas kernels  7.77 us (20%)
  waiting for transfers between devices  7.55 us (20%)
  local copies, waits for them, and re-layouts  0.97 us (3%)
  matrix products  0.44 us (1%)
    ppermute x6, starting transfers between devices, to_group(): return lax.ppermute(x, 'seq', pairs)  9.13 us
    ppermute x3, starting transfers between devices, to_head(): lax.ppermute(x, 'head', [(h, partner(h, t, head_count)) for h in range(he...  7.66 us
    pallas_call x4, Pallas kernels, attend(): pl.pallas_call(functools.partial(attend_kernel, tuple(pieces), tuple(((le...  5.06 us
    ppermute x3, starting transfers between devices, from_group(): return lax.ppermute(x, 'seq', pairs)  3.55 us
    ppermute x3, waiting for transfers between devices, from_group(): return lax.ppermute(x, 'seq', pairs)  3.25 us
    ppermute x3, waiting for transfers between devices, to_head(): lax.ppermute(x, 'head', [(h, partner(h, t, head_count)) for h in range(he...  3.14 us
    pallas_call x1, Pallas kernels, prepare(): pl.pallas_call(functools.partial(prepare_kernel, groups, gather, shards),...  1.8 us
    ppermute x6, waiting for transfers between devices, to_group(): return lax.ppermute(x, 'seq', pairs)  1.15 us
  transfers between devices with their start and end apart: 15, of which 5 were waited for; matrix products, arithmetic and copies ran while one was open for 3% of the time, Pallas kernels for 11%

commit v1 on v0

--- a/solution.py
+++ b/solution.py
@@ -37,9 +37,45 @@
     return [pl.BlockSpec(memory_space=pltpu.VMEM)] * count
 
 
-def prepare_kernel(groups, gather, shards, *refs):
+def start_loads(new_refs, pieces, targets, sems):
+    rows, width = pieces[0].shape[0] // 3, pieces[0].shape[1]
+    copies = []
+    for n, (piece, target) in enumerate(zip(pieces, targets)):
+        cols = columns(target, width)
+        for i, src in enumerate(new_refs):
+            dst = piece.at[pl.ds(i * rows, rows)]
+            copies.append(pltpu.make_async_copy(src.at[:, cols], dst, sems.at[n, i]))
+    for copy in copies:
+        copy.start()
+    return copies
+
+
+def pack_kernel(steps, groups, gather, *refs):
+    group = lax.axis_index("seq") // gather
+    targets = [partner(group, t, groups) for t in steps]
+    for copy in start_loads(refs[:3], refs[3:-1], targets, refs[-1]):
+        copy.wait()
+
+
+def pack(new, steps, groups, gather):
+    rows, width = new[0].shape[0], new[0].shape[1] // groups
+    return pl.pallas_call(
+        functools.partial(pack_kernel, tuple(steps), groups, gather),
+        out_shape=[jax.ShapeDtypeStruct((3 * rows, width), jnp.bfloat16)] * len(steps),
+        in_specs=[pl.BlockSpec(memory_space=pltpu.HBM)] * 3,
+        out_specs=vmem(len(steps)),
+        scratch_shapes=[pltpu.SemaphoreType.DMA((len(steps), 3))],
+        compiler_params=pltpu.CompilerParams(vmem_limit_bytes=SMALL),
+        cost_estimate=pl.CostEstimate(
+            flops=0, bytes_accessed=12 * len(steps) * rows * width, transcendentals=0
+        ),
+        name="pack",
+    )(*[pltpu.with_memory_space_constraint(x, pltpu.HBM) for x in new])
+
+
+def prepare_kernel(steps, groups, gather, shards, *refs):
     new_refs, cache_refs, outs, scratch = refs[:3], refs[3:7], refs[7:-6], refs[-6:]
-    pieces, cached = outs[:groups], outs[groups:]
+    pieces, cached = outs[: len(steps)], outs[len(steps) :]
     ck_buf, cv_buf, ke_buf, ve_buf, cache_sems, new_sems = scratch
     group, shard = lax.axis_index("seq") // gather, lax.axis_index("head")
 
@@ -47,18 +83,14 @@
         pltpu.make_async_copy(src, dst, cache_sems.at[i])
         for i, (src, dst) in enumerate(zip(cache_refs, (ck_buf, cv_buf, ke_buf, ve_buf)))
     ]
-    rows, width = pieces[0].shape[0] // 3, pieces[0].shape[1]
-    copies = []
-    for t in range(groups):
-        cols = columns(partner(group, t, groups), width)
-        for i, src in enumerate(new_refs):
-            dst = pieces[t].at[pl.ds(i * rows, rows)]
-            copies.append(pltpu.make_async_copy(src.at[:, cols], dst, new_sems.at[t, i]))
-    for copy in loads + copies:
+    for copy in loads:
         copy.start()
+    targets = [partner(group, t, groups) for t in steps]
+    copies = start_loads(new_refs, pieces, targets, new_sems)
     for copy in loads:
         copy.wait()
 
+    width = cached[0].shape[-1]
     blocks, heads = ke_buf.shape
     cache_rows = ck_buf.shape[0]
     exponent = jnp.concatenate(
@@ -86,24 +118,27 @@
         copy.wait()
 
 
-def prepare(q, k, v, ck, cv, ke, ve, groups, gather, shards):
-    rows, width = q.shape[0], q.shape[1] // groups
-    operands = (k, v, q, ck, cv, ke, ve)
+def prepare(new, stored, steps, groups, gather, shards):
+    rows, width = new[0].shape[0], new[0].shape[1] // groups
+    cache_rows = stored[0].shape[0]
+    operands = (*new, *stored)
     outs = pl.pallas_call(
-        functools.partial(prepare_kernel, groups, gather, shards),
-        out_shape=[jax.ShapeDtypeStruct((3 * rows, width), jnp.bfloat16)] * groups
-        + [jax.ShapeDtypeStruct((groups, 2, ck.shape[0], width), jnp.bfloat16)] * shards,
+        functools.partial(prepare_kernel, tuple(steps), groups, gather, shards),
+        out_shape=[jax.ShapeDtypeStruct((3 * rows, width), jnp.bfloat16)] * len(steps)
+        + [jax.ShapeDtypeStruct((groups, 2, cache_rows, width), jnp.bfloat16)] * shards,
         in_specs=[pl.BlockSpec(memory_space=pltpu.HBM)] * len(operands),
-        out_specs=vmem(groups + shards),
-        scratch_shapes=[pltpu.VMEM(x.shape, x.dtype) for x in (ck, cv, ke, ve)]
-        + [pltpu.SemaphoreType.DMA((4,)), pltpu.SemaphoreType.DMA((groups, 3))],
+        out_specs=vmem(len(steps) + shards),
+        scratch_shapes=[pltpu.VMEM(x.shape, x.dtype) for x in stored]
+        + [pltpu.SemaphoreType.DMA((4,)), pltpu.SemaphoreType.DMA((len(steps), 3))],
         compiler_params=pltpu.CompilerParams(vmem_limit_bytes=SMALL),
         cost_estimate=pl.CostEstimate(
-            flops=4 * ck.size, bytes_accessed=12 * q.size + 8 * ck.size, transcendentals=0
+            flops=4 * stored[0].size,
+            bytes_accessed=12 * len(steps) * rows * width + 8 * stored[0].size,
+            transcendentals=0,
         ),
         name="prepare",
     )(*[pltpu.with_memory_space_constraint(x, pltpu.HBM) for x in operands])
-    return list(outs[:groups]), list(outs[groups:])
+    return list(outs[: len(steps)]), list(outs[len(steps) :])
 
 
 def interleave_kernel(*refs):
@@ -350,23 +385,18 @@
         return lax.ppermute(x, "head", [(h, partner(h, t, head_count)) for h in range(head_count)])
 
     members = range(1, gather)
-    kv_own, stored = prepare(
-        query_new,
-        key_new,
-        value_new,
-        cache_keys,
-        cache_values,
-        key_exponent,
-        value_exponent,
-        groups,
-        gather,
-        head_count,
-    )
+    every = range(groups)
+    steps = [*every[-1:], *every[1:-1], *every[:1]] if groups > 1 else [0]
+    new = (key_new, value_new, query_new)
+    stored = (cache_keys, cache_values, key_exponent, value_exponent)
+    first = sorted({steps[0], 0})
+    kv_own, stored = prepare(new, stored, first, groups, gather, head_count)
+    kv_own = dict(zip(first, kv_own))
     kv_other = [to_member(kv_own[0][: 2 * tok_rows], s) for s in members]
     if gather > 1:
-        kv_own[1:-1], stored, kv_other[0] = lax.optimization_barrier(
-            (kv_own[1:-1], stored, kv_other[0])
-        )
+        new, stored, kv_other[0] = lax.optimization_barrier((new, stored, kv_other[0]))
+    if groups > 2:
+        kv_own.update(zip(steps[1:-1], pack(new, steps[1:-1], groups, gather)))
     kv = [to_group(kv_own[t], t) for t in range(groups)]
     by_head = []
     for s in range(head_count):
@@ -378,7 +408,7 @@
     block_mask, group, member, head_index, _ = lax.optimization_barrier(
         (block_mask, group, member, head_index, kv[1:])
     )
-    cache = [to_group(interleave([x[t] for x in by_head]), t) for t in range(groups)]
+    cache = [to_group(interleave([x[t] for x in by_head]), t) for t in steps]
     if groups > 1:
         swap = join(kv[1:], 2 * tok_rows)
         kv_other += [to_member(swap, s) for s in members]
@@ -389,13 +419,13 @@
     q_pick = (q_block[:, None] == jnp.arange(block_mask.shape[0])[None, :]).astype(jnp.float32)
     row_mask = jnp.dot(q_pick, block_mask.astype(jnp.float32))
 
-    def bias_of(steps):
+    def bias_of(swaps):
         device = jnp.stack(
             [
                 (origin(group, t, groups) * gather + origin(member, s, gather)) * head_count
                 + origin(head_index, z, head_count)
-                for s in steps
-                for t in range(groups)
+                for s in swaps
+                for t in steps
                 for z in range(head_count)
             ]
         )
@@ -404,8 +434,6 @@
         seen = jnp.dot(row_mask, pick.astype(jnp.float32))
         return jnp.where(seen > 0.5, 0.0, MASKED).astype(jnp.float32)
 
-    every = range(groups)
-    steps = [*every[-1:], *every[1:-1], *every[:1]] if groups > 1 else [0]
     bias = [bias_of([0])] + ([bias_of(members)] if gather > 1 else [])
     away = steps[:-1]
     if groups > 1:

time: 38.5 us -> 38.5 us (level)
  starting transfers between devices: 21 us -> 19.8 us
  Pallas kernels: 7.77 us -> 8.59 us
    ppermute x3, waiting for transfers between devices: 3.14 us -> 4.4 us  [to_head(): lax.ppermute(x, 'head', [(h, partner(h, t, head_count)) for h in range(he...]
    ppermute x3, starting transfers between devices: 7.66 us -> 6.4 us  [to_head(): lax.ppermute(x, 'head', [(h, partner(h, t, head_count)) for h in range(he...]
    ppermute x6, waiting for transfers between devices: 1.15 us -> 0.21 us  [to_group(): return lax.ppermute(x, 'seq', pairs)]
    pallas_call x1 -> x2, Pallas kernels: 1.8 us -> 2.62 us  [the longest x1 1.43 us: prepare(): pl.pallas_call(functools.partial(prepare_kernel, tuple(steps), groups, ga...]
  transfers between devices with their start and end apart: 15 -> 15, of which waited for: 5 -> 5; matrix products, arithmetic and copies ran while one was open for 3% -> 3% of each run, Pallas kernels for 11% -> 15%
where the time goes in v1:
time: 38.5 us; the launch traced here: 38.2 us
  starting transfers between devices  19.8 us (51%)
  Pallas kernels  8.59 us (22%)
  waiting for transfers between devices  7.87 us (20%)
  local copies, waits for them, and re-layouts  0.97 us (3%)
  matrix products  0.44 us (1%)
    ppermute x6, starting transfers between devices, to_group(): return lax.ppermute(x, 'seq', pairs)  9.19 us
    ppermute x3, starting transfers between devices, to_head(): lax.ppermute(x, 'head', [(h, partner(h, t, head_count)) for h in range(he...  6.4 us
    pallas_call x4, Pallas kernels, attend(): pl.pallas_call(functools.partial(attend_kernel, tuple(pieces), tuple(((le...  5.06 us
    ppermute x3, waiting for transfers between devices, to_head(): lax.ppermute(x, 'head', [(h, partner(h, t, head_count)) for h in range(he...  4.4 us
    ppermute x3, starting transfers between devices, from_group(): return lax.ppermute(x, 'seq', pairs)  3.55 us
    ppermute x3, waiting for transfers between devices, from_group(): return lax.ppermute(x, 'seq', pairs)  3.25 us
    pallas_call x1, Pallas kernels, prepare(): pl.pallas_call(functools.partial(prepare_kernel, tuple(steps), groups, ga...  1.43 us
    pallas_call x1, Pallas kernels, pack(): pl.pallas_call(functools.partial(pack_kernel, tuple(steps), groups, gathe...  1.18 us
  transfers between devices with their start and end apart: 15, of which 5 were waited for; matrix products, arithmetic and copies ran while one was open for 3% of the time, Pallas kernels for 15%

profile of v1, /device:TPU:0, one launch (start us, length us, event | category | flops | bytes accessed | tf_op | source)
XLA Modules:
  0.0 38.2 jit_solution(18395770501112913379)
XLA Ops:
  0.0 1.4 %prepare.1 = (bf16[384,384]{1,0:T(8,128)(2,1)S(1)}, bf16[384,384]{1,0:T(8,128)(2,1)S(1)}, bf16[4,2,16,384]{3,2,1,0:T(8,128)(2,1)S(1)}, bf16[4,2,16,384]{3,2,1,0:...) custom-call(bf16[128,1536]{1,0:T(8,128)(2,1)} %refs_0_.2, ...), custom_call_target="tpu_custom_call" | custom-call | flops 393216 | bytes 1966080 | tf_op jit(solution)/shard_map/prepare/pallas_call | solution.py:125
  1.5 0.5 %collective-permute-start.1 = (bf16[256,384]{1,0:T(8,128)(2,1)S(1)}, bf16[256,384]{1,0:T(8,128)(2,1)S(1)}, u32[]{:S(2)}, u32[]{:S(2)}) collective-permute-start(bf16[256,384]{1,0:T(8,128)(2,1)S(1)} %slice.51), channel_id=1, source_target_pairs={{0,4},{4,0},{8,12},{12,8},{16,20},{20,16},{24,28},{28,24},{1,5},{5... | collective-permute-start | bytes 589832 | tf_op jit(solution)/shard_map/ppermute | solution.py:380
  2.0 3.5 %collective-permute-start = (bf16[384,384]{1,0:T(8,128)(2,1)S(1)}, bf16[384,384]{1,0:T(8,128)(2,1)S(1)}, u32[]{:S(2)}, u32[]{:S(2)}) collective-permute-start(bf16[384,384]{1,0:T(8,128)(2,1)S(1)} %get-tuple-element.48), channel_id=1, source_target_pairs={{0,24},{4,28},{8,16},{12,20},{16,8},{20,12},{24,0},{28,4},{1,25},{... | collective-permute-start | bytes 884744 | tf_op jit(solution)/shard_map/ppermute | solution.py:366
  5.5 1.6 %collective-permute-start.2 = (bf16[4,2,16,384]{3,2,1,0:T(8,128)(2,1)S(1)}, bf16[4,2,16,384]{3,2,1,0:T(8,128)(2,1)S(1)}, u32[]{:S(2)}, u32[]{:S(2)}) collective-permute-start(bf16[4,2,16,384]{3,2,1,0:T(8,128)(2,1)S(1)} %get-tuple-element.56), channel_id=1, source_target_pairs={{0,1},{1,0},{2,3},{3,2},{4,5},{5,4},{6,7},{7,6},{8,9},{9,8},{10,11... | collective-permute-start | bytes 294920 | tf_op jit(solution)/shard_map/ppermute | solution.py:385
  7.1 2.7 %collective-permute-start.3 = (bf16[4,2,16,384]{3,2,1,0:T(8,128)(2,1)S(1)}, bf16[4,2,16,384]{3,2,1,0:T(8,128)(2,1)S(1)}, u32[]{:S(2)}, u32[]{:S(2)}) collective-permute-start(bf16[4,2,16,384]{3,2,1,0:T(8,128)(2,1)S(1)} %get-tuple-element.58), channel_id=1, source_target_pairs={{0,2},{1,3},{2,0},{3,1},{4,6},{5,7},{6,4},{7,5},{8,10},{9,11},{10,... | collective-permute-start | bytes 294920 | tf_op jit(solution)/shard_map/ppermute | solution.py:385
  9.8 1.2 %pack.1 = (bf16[384,384]{1,0:T(8,128)(2,1)S(1)}, bf16[384,384]{1,0:T(8,128)(2,1)S(1)}) custom-call(bf16[128,1536]{1,0:T(8,128)(2,1)} %refs_0_.2, bf16[128,1536]{1,0:T(8,128)(2,1)} %refs_1_.2, bf16[128,1536]{1,0:T(8,128)(2,1)} %refs_2_.2), custom_call_target="tpu_custom_call" | custom-call | bytes 1179648 | tf_op jit(solution)/shard_map/pack/pallas_call | solution.py:62
  10.9 0.6 %collective-permute-start.5 = (bf16[384,384]{1,0:T(8,128)(2,1)S(1)}, bf16[384,384]{1,0:T(8,128)(2,1)S(1)}, u32[]{:S(2)}, u32[]{:S(2)}) collective-permute-start(bf16[384,384]{1,0:T(8,128)(2,1)S(1)} %get-tuple-element.64), channel_id=1, source_target_pairs={{0,8},{4,12},{8,0},{12,4},{16,24},{20,28},{24,16},{28,20},{1,9},{5... | collective-permute-start | bytes 884744 | tf_op jit(solution)/shard_map/ppermute | solution.py:366
  11.6 1.4 %collective-permute-start.6 = (bf16[384,384]{1,0:T(8,128)(2,1)S(1)}, bf16[384,384]{1,0:T(8,128)(2,1)S(1)}, u32[]{:S(2)}, u32[]{:S(2)}) collective-permute-start(bf16[384,384]{1,0:T(8,128)(2,1)S(1)} %get-tuple-element.66), channel_id=1, source_target_pairs={{0,16},{4,20},{8,24},{12,28},{16,0},{20,4},{24,8},{28,12},{1,17},{... | collective-permute-start | bytes 884744 | tf_op jit(solution)/shard_map/ppermute | solution.py:366
  13.0 2.2 %collective-permute-start.4 = (bf16[4,2,16,384]{3,2,1,0:T(8,128)(2,1)S(1)}, bf16[4,2,16,384]{3,2,1,0:T(8,128)(2,1)S(1)}, u32[]{:S(2)}, u32[]{:S(2)}) collective-permute-start(bf16[4,2,16,384]{3,2,1,0:T(8,128)(2,1)S(1)} %get-tuple-element.59), channel_id=1, source_target_pairs={{0,3},{1,2},{2,1},{3,0},{4,7},{5,6},{6,5},{7,4},{8,11},{9,10},{10,... | collective-permute-start | bytes 294920 | tf_op jit(solution)/shard_map/ppermute | solution.py:385
  15.1 4.4 %collective-permute-done.4 = bf16[4,2,16,384]{3,2,1,0:T(8,128)(2,1)S(1)} collective-permute-done((bf16[4,2,16,384]{3,2,1,0:T(8,128)(2,1)S(1)}, bf16[4,2,16,384]{3,2,1,0:T(8,128)(2,1)S(1)}, u32[]{:S(2)}, u32[]{:S(2)}) %collective-permute-start.4) | collective-permute-done | bytes 98336 | tf_op jit(solution)/shard_map/ppermute | solution.py:385
  19.6 1.6 %collective-permute-start.7 = (bf16[128,384]{1,0:T(8,128)(2,1)S(1)}, bf16[128,384]{1,0:T(8,128)(2,1)S(1)}, u32[]{:S(2)}, u32[]{:S(2)}) collective-permute-start(bf16[128,384]{1,0:T(8,128)(2,1)S(1)} %interleave.4), channel_id=1, source_target_pairs={{0,24},{4,28},{8,16},{12,20},{16,8},{20,12},{24,0},{28,4},{1,25},{... | collective-permute-start | bytes 294920 | tf_op jit(solution)/shard_map/ppermute | solution.py:366
  21.2 0.6 %collective-permute-start.8 = (bf16[128,384]{1,0:T(8,128)(2,1)S(1)}, bf16[128,384]{1,0:T(8,128)(2,1)S(1)}, u32[]{:S(2)}, u32[]{:S(2)}) collective-permute-start(bf16[128,384]{1,0:T(8,128)(2,1)S(1)} %interleave.5), channel_id=1, source_target_pairs={{0,8},{4,12},{8,0},{12,4},{16,24},{20,28},{24,16},{28,20},{1,9},{5... | collective-permute-start | bytes 294920 | tf_op jit(solution)/shard_map/ppermute | solution.py:366
  21.8 1.5 %collective-permute-start.9 = (bf16[128,384]{1,0:T(8,128)(2,1)S(1)}, bf16[128,384]{1,0:T(8,128)(2,1)S(1)}, u32[]{:S(2)}, u32[]{:S(2)}) collective-permute-start(bf16[128,384]{1,0:T(8,128)(2,1)S(1)} %interleave.6), channel_id=1, source_target_pairs={{0,16},{4,20},{8,24},{12,28},{16,0},{20,4},{24,8},{28,12},{1,17},{... | collective-permute-start | bytes 294920 | tf_op jit(solution)/shard_map/ppermute | solution.py:366
  23.4 0.1 stack.155
  23.5 0.1 stack.138
  23.8 0.1 add.233
  24.2 0.1 add.277
  24.3 0.4 %copy-done = s32[16,16]{1,0:T(8,128)S(1)} copy-done((s32[16,16]{1,0:T(8,128)S(1)}, s32[16,16]{1,0:T(8,128)}, u32[]{:S(2)}) %copy-start) | copy-done | bytes 1048
  24.8 0.2 fusion.4
  25.0 0.1 fusion.1.refs_7_.refs_9_
  25.1 0.1 fusion.refs_4_.refs_13_
  25.2 1.1 %attend.4 = (f32[384,384]{1,0:T(8,128)S(1)}, f32[384,384]{1,0:T(8,128)S(1)}, f32[384,384]{1,0:T(8,128)S(1)}) custom-call(bf16[384,384]{1,0:T(8,128)(2,1)S(1)} %collective-permute-done.refs_0_.refs_6_.refs_2_.refs_4_, bf16[384,384]{1,0:T(8,128)(2,1)S(1)} %collective-permute-done.5.refs_1_.refs_4_.refs_0_.refs_2_, ...), custom_call_target="tpu_custom_call" | custom-call | flops 301989888 | bytes 786432 | tf_op jit(solution)/shard_map/attend/pallas_call | solution.py:283
  26.3 0.2 collective-permute-done.9.refs_2_.refs_5_.refs_7_
  26.7 1.7 %attend.5 = (f32[384,384]{1,0:T(8,128)S(1)}, f32[384,384]{1,0:T(8,128)S(1)}, f32[384,384]{1,0:T(8,128)S(1)}) custom-call(bf16[384,384]{1,0:T(8,128)(2,1)S(1)} %collective-permute-done.refs_0_.refs_6_.refs_2_.refs_4_, bf16[384,384]{1,0:T(8,128)(2,1)S(1)} %collective-permute-done.5.refs_1_.refs_4_.refs_0_.refs_2_, ...), custom_call_target="tpu_custom_call" | custom-call | flops 452984832 | bytes 1179648 | tf_op jit(solution)/shard_map/attend/pallas_call | solution.py:283
  28.4 0.8 %attend.6 = (bf16[128,384]{1,0:T(8,128)(2,1)S(1)}, bf16[128,384]{1,0:T(8,128)(2,1)S(1)}, bf16[128,384]{1,0:T(8,128)(2,1)S(1)}) custom-call(bf16[384,384]{1,0:T(8,128)(2,1)S(1)} %collective-permute-done.refs_0_.refs_6_.refs_2_.refs_4_, bf16[384,384]{1,0:T(8,128)(2,1)S(1)} %collective-permute-done.5.refs_1_.refs_4_.refs_0_.refs_2_, ...), custom_call_target="tpu_custom_call" | custom-call | flops 150994944 | bytes 393216 | tf_op jit(solution)/shard_map/attend/pallas_call | solution.py:283
  29.2 1.5 %collective-permute-start.12 = (bf16[128,384]{1,0:T(8,128)(2,1)S(1)}, bf16[128,384]{1,0:T(8,128)(2,1)S(1)}, u32[]{:S(2)}, u32[]{:S(2)}) collective-permute-start(bf16[128,384]{1,0:T(8,128)(2,1)S(1)} %get-tuple-element.88), channel_id=1, source_target_pairs={{0,24},{4,28},{8,16},{12,20},{16,8},{20,12},{24,0},{28,4},{1,25},{... | collective-permute-start | bytes 294920 | tf_op jit(solution)/shard_map/ppermute | solution.py:374
  30.7 1.4 %collective-permute-start.13 = (bf16[128,384]{1,0:T(8,128)(2,1)S(1)}, bf16[128,384]{1,0:T(8,128)(2,1)S(1)}, u32[]{:S(2)}, u32[]{:S(2)}) collective-permute-start(bf16[128,384]{1,0:T(8,128)(2,1)S(1)} %get-tuple-element.89), channel_id=1, source_target_pairs={{0,8},{4,12},{8,0},{12,4},{16,24},{20,28},{24,16},{28,20},{1,9},{5... | collective-permute-start | bytes 294920 | tf_op jit(solution)/shard_map/ppermute | solution.py:374
  32.1 0.6 %collective-permute-start.14 = (bf16[128,384]{1,0:T(8,128)(2,1)S(1)}, bf16[128,384]{1,0:T(8,128)(2,1)S(1)}, u32[]{:S(2)}, u32[]{:S(2)}) collective-permute-start(bf16[128,384]{1,0:T(8,128)(2,1)S(1)} %get-tuple-element.90), channel_id=1, source_target_pairs={{0,16},{4,20},{8,24},{12,28},{16,0},{20,4},{24,8},{28,12},{1,17},{... | collective-permute-start | bytes 294920 | tf_op jit(solution)/shard_map/ppermute | solution.py:374
  32.8 1.4 %attend.7.refs_3_ = bf16[128,384]{1,0:T(8,128)(2,1)S(1)} custom-call(bf16[384,384]{1,0:T(8,128)(2,1)S(1)} %get-tuple-element.53.refs_3_.refs_0_.refs_1_, bf16[384,384]{1,0:T(8,128)(2,1)S(1)} %get-tuple-element.53.refs_3_.refs_0_.refs_1_, bf16[384,384]{1,0:T(8,128)(2,1)S(1)} %collective-permute-done.5.refs_1_.refs_4_.refs_0_.refs_2_, ...), custom_call_target="tpu_custom_call" | custom-call | flops 301989888 | bytes 2359296 | tf_op jit(solution)/shard_map/attend/pallas_call | solution.py:283
  34.2 1.5 %collective-permute-done.12.refs_0_ = bf16[128,384]{1,0:T(8,128)(2,1)S(1)} collective-permute-done((bf16[128,384]{1,0:T(8,128)(2,1)S(1)}, bf16[128,384]{1,0:T(8,128)(2,1)S(1)}, u32[]{:S(2)}, u32[]{:S(2)}) %collective-permute-start.12) | collective-permute-done | bytes 98336 | tf_op jit(solution)/shard_map/ppermute | solution.py:374
  35.8 1.6 %collective-permute-done.13.refs_1_ = bf16[128,384]{1,0:T(8,128)(2,1)S(1)} collective-permute-done((bf16[128,384]{1,0:T(8,128)(2,1)S(1)}, bf16[128,384]{1,0:T(8,128)(2,1)S(1)}, u32[]{:S(2)}, u32[]{:S(2)}) %collective-permute-start.13) | collective-permute-done | bytes 98336 | tf_op jit(solution)/shard_map/ppermute | solution.py:374
  37.5 0.8 %unpack_heads.1 = bf16[128,1536]{1,0:T(8,128)(2,1)} custom-call(bf16[128,384]{1,0:T(8,128)(2,1)S(1)} %collective-permute-done.12.refs_0_, bf16[128,384]{1,0:T(8,128)(2,1)S(1)} %collective-permute-done.13.refs_1_, bf16[128,384]{1,0:T(8,128)(2,1)S(1)} %collective-permute-done.14.refs_2_, bf16[128,384]{1,0:T(8,128)(2,1)S(1)} %attend.7.refs_3_), custom_call_target="tpu_custom_call" | custom-call | bytes 786432 | tf_op jit(solution)/shard_map/unpack_heads/pallas_call | solution.py:325
  (34 shorter events, 0.9 us)
Async XLA Ops:
  1.5 4.0 %collective-permute-start.1 = (bf16[256,384]{1,0:T(8,128)(2,1)S(1)}, bf16[256,384]{1,0:T(8,128)(2,1)S(1)}, u32[]{:S(2)}, u32[]{:S(2)}) collective-permute-start(bf16[256,384]{1,0:T(8,128)(2,1)S(1)} %slice.51), channel_id=1, source_target_pairs={{0,4},{4,0},{8,12},{12,8},{16,20},{20,16},{24,28},{28,24},{1,5},{5... | collective-permute-start | bytes 589832 | tf_op jit(solution)/shard_map/ppermute | solution.py:380
  2.0 19.8 %collective-permute-start = (bf16[384,384]{1,0:T(8,128)(2,1)S(1)}, bf16[384,384]{1,0:T(8,128)(2,1)S(1)}, u32[]{:S(2)}, u32[]{:S(2)}) collective-permute-start(bf16[384,384]{1,0:T(8,128)(2,1)S(1)} %get-tuple-element.48), channel_id=1, source_target_pairs={{0,24},{4,28},{8,16},{12,20},{16,8},{20,12},{24,0},{28,4},{1,25},{... | collective-permute-start | bytes 884744 | tf_op jit(solution)/shard_map/ppermute | solution.py:366
  5.5 7.4 %collective-permute-start.2 = (bf16[4,2,16,384]{3,2,1,0:T(8,128)(2,1)S(1)}, bf16[4,2,16,384]{3,2,1,0:T(8,128)(2,1)S(1)}, u32[]{:S(2)}, u32[]{:S(2)}) collective-permute-start(bf16[4,2,16,384]{3,2,1,0:T(8,128)(2,1)S(1)} %get-tuple-element.56), channel_id=1, source_target_pairs={{0,1},{1,0},{2,3},{3,2},{4,5},{5,4},{6,7},{7,6},{8,9},{9,8},{10,11... | collective-permute-start | bytes 294920 | tf_op jit(solution)/shard_map/ppermute | solution.py:385
  7.1 8.0 %collective-permute-start.3 = (bf16[4,2,16,384]{3,2,1,0:T(8,128)(2,1)S(1)}, bf16[4,2,16,384]{3,2,1,0:T(8,128)(2,1)S(1)}, u32[]{:S(2)}, u32[]{:S(2)}) collective-permute-start(bf16[4,2,16,384]{3,2,1,0:T(8,128)(2,1)S(1)} %get-tuple-element.58), channel_id=1, source_target_pairs={{0,2},{1,3},{2,0},{3,1},{4,6},{5,7},{6,4},{7,5},{8,10},{9,11},{10,... | collective-permute-start | bytes 294920 | tf_op jit(solution)/shard_map/ppermute | solution.py:385
  10.9 12.4 %collective-permute-start.5 = (bf16[384,384]{1,0:T(8,128)(2,1)S(1)}, bf16[384,384]{1,0:T(8,128)(2,1)S(1)}, u32[]{:S(2)}, u32[]{:S(2)}) collective-permute-start(bf16[384,384]{1,0:T(8,128)(2,1)S(1)} %get-tuple-element.64), channel_id=1, source_target_pairs={{0,8},{4,12},{8,0},{12,4},{16,24},{20,28},{24,16},{28,20},{1,9},{5... | collective-permute-start | bytes 884744 | tf_op jit(solution)/shard_map/ppermute | solution.py:366
  11.6 11.8 %collective-permute-start.6 = (bf16[384,384]{1,0:T(8,128)(2,1)S(1)}, bf16[384,384]{1,0:T(8,128)(2,1)S(1)}, u32[]{:S(2)}, u32[]{:S(2)}) collective-permute-start(bf16[384,384]{1,0:T(8,128)(2,1)S(1)} %get-tuple-element.66), channel_id=1, source_target_pairs={{0,16},{4,20},{8,24},{12,28},{16,0},{20,4},{24,8},{28,12},{1,17},{... | collective-permute-start | bytes 884744 | tf_op jit(solution)/shard_map/ppermute | solution.py:366
  13.0 6.6 %collective-permute-start.4 = (bf16[4,2,16,384]{3,2,1,0:T(8,128)(2,1)S(1)}, bf16[4,2,16,384]{3,2,1,0:T(8,128)(2,1)S(1)}, u32[]{:S(2)}, u32[]{:S(2)}) collective-permute-start(bf16[4,2,16,384]{3,2,1,0:T(8,128)(2,1)S(1)} %get-tuple-element.59), channel_id=1, source_target_pairs={{0,3},{1,2},{2,1},{3,0},{4,7},{5,6},{6,5},{7,4},{8,11},{9,10},{10,... | collective-permute-start | bytes 294920 | tf_op jit(solution)/shard_map/ppermute | solution.py:385
  19.6 6.7 %collective-permute-start.7 = (bf16[128,384]{1,0:T(8,128)(2,1)S(1)}, bf16[128,384]{1,0:T(8,128)(2,1)S(1)}, u32[]{:S(2)}, u32[]{:S(2)}) collective-permute-start(bf16[128,384]{1,0:T(8,128)(2,1)S(1)} %interleave.4), channel_id=1, source_target_pairs={{0,24},{4,28},{8,16},{12,20},{16,8},{20,12},{24,0},{28,4},{1,25},{... | collective-permute-start | bytes 294920 | tf_op jit(solution)/shard_map/ppermute | solution.py:366
  21.2 5.1 %collective-permute-start.8 = (bf16[128,384]{1,0:T(8,128)(2,1)S(1)}, bf16[128,384]{1,0:T(8,128)(2,1)S(1)}, u32[]{:S(2)}, u32[]{:S(2)}) collective-permute-start(bf16[128,384]{1,0:T(8,128)(2,1)S(1)} %interleave.5), channel_id=1, source_target_pairs={{0,8},{4,12},{8,0},{12,4},{16,24},{20,28},{24,16},{28,20},{1,9},{5... | collective-permute-start | bytes 294920 | tf_op jit(solution)/shard_map/ppermute | solution.py:366
  21.8 4.7 %collective-permute-start.9 = (bf16[128,384]{1,0:T(8,128)(2,1)S(1)}, bf16[128,384]{1,0:T(8,128)(2,1)S(1)}, u32[]{:S(2)}, u32[]{:S(2)}) collective-permute-start(bf16[128,384]{1,0:T(8,128)(2,1)S(1)} %interleave.6), channel_id=1, source_target_pairs={{0,16},{4,20},{8,24},{12,28},{16,0},{20,4},{24,8},{28,12},{1,17},{... | collective-permute-start | bytes 294920 | tf_op jit(solution)/shard_map/ppermute | solution.py:366
  24.1 0.7 %copy-start = (s32[16,16]{1,0:T(8,128)S(1)}, s32[16,16]{1,0:T(8,128)}, u32[]{:S(2)}) copy-start(s32[16,16]{1,0:T(8,128)} %param.15) | copy-start | bytes 3076
  24.2 2.4 %collective-permute-start.11 = (bf16[3,256,384]{2,1,0:T(8,128)(2,1)S(1)}, bf16[3,256,384]{2,1,0:T(8,128)(2,1)S(1)}, u32[]{:S(2)}, u32[]{:S(2)}) collective-permute-start(bf16[3,256,384]{2,1,0:T(8,128)(2,1)S(1)} %join.3), channel_id=1, source_target_pairs={{0,4},{4,0},{8,12},{12,8},{16,20},{20,16},{24,28},{28,24},{1,5},{5... | collective-permute-start | bytes 1769480 | tf_op jit(solution)/shard_map/ppermute | solution.py:380
  26.6 1.8 %collective-permute-start.10 = (bf16[4,128,384]{2,1,0:T(8,128)(2,1)S(1)}, bf16[4,128,384]{2,1,0:T(8,128)(2,1)S(1)}, u32[]{:S(2)}, u32[]{:S(2)}) collective-permute-start(bf16[4,128,384]{2,1,0:T(8,128)(2,1)S(1)} %join.2), channel_id=1, source_target_pairs={{0,4},{4,0},{8,12},{12,8},{16,20},{20,16},{24,28},{28,24},{1,5},{5... | collective-permute-start | bytes 1179656 | tf_op jit(solution)/shard_map/ppermute | solution.py:380
  29.2 6.6 %collective-permute-start.12 = (bf16[128,384]{1,0:T(8,128)(2,1)S(1)}, bf16[128,384]{1,0:T(8,128)(2,1)S(1)}, u32[]{:S(2)}, u32[]{:S(2)}) collective-permute-start(bf16[128,384]{1,0:T(8,128)(2,1)S(1)} %get-tuple-element.88), channel_id=1, source_target_pairs={{0,24},{4,28},{8,16},{12,20},{16,8},{20,12},{24,0},{28,4},{1,25},{... | collective-permute-start | bytes 294920 | tf_op jit(solution)/shard_map/ppermute | solution.py:374
  30.7 6.7 %collective-permute-start.13 = (bf16[128,384]{1,0:T(8,128)(2,1)S(1)}, bf16[128,384]{1,0:T(8,128)(2,1)S(1)}, u32[]{:S(2)}, u32[]{:S(2)}) collective-permute-start(bf16[128,384]{1,0:T(8,128)(2,1)S(1)} %get-tuple-element.89), channel_id=1, source_target_pairs={{0,8},{4,12},{8,0},{12,4},{16,24},{20,28},{24,16},{28,20},{1,9},{5... | collective-permute-start | bytes 294920 | tf_op jit(solution)/shard_map/ppermute | solution.py:374
  32.1 5.3 %collective-permute-start.14 = (bf16[128,384]{1,0:T(8,128)(2,1)S(1)}, bf16[128,384]{1,0:T(8,128)(2,1)S(1)}, u32[]{:S(2)}, u32[]{:S(2)}) collective-permute-start(bf16[128,384]{1,0:T(8,128)(2,1)S(1)} %get-tuple-element.90), channel_id=1, source_target_pairs={{0,16},{4,20},{8,24},{12,28},{16,0},{20,4},{24,8},{28,12},{1,17},{... | collective-permute-start | bytes 294920 | tf_op jit(solution)/shard_map/ppermute | solution.py:374

commit v2 on v0

--- a/solution.py
+++ b/solution.py
@@ -350,6 +350,8 @@
         return lax.ppermute(x, "head", [(h, partner(h, t, head_count)) for h in range(head_count)])
 
     members = range(1, gather)
+    every = range(groups)
+    steps = [*every[-1:], *every[1:-1], *every[:1]] if groups > 1 else [0]
     kv_own, stored = prepare(
         query_new,
         key_new,
@@ -378,7 +380,7 @@
     block_mask, group, member, head_index, _ = lax.optimization_barrier(
         (block_mask, group, member, head_index, kv[1:])
     )
-    cache = [to_group(interleave([x[t] for x in by_head]), t) for t in range(groups)]
+    cache = [to_group(interleave([x[t] for x in by_head]), t) for t in steps]
     if groups > 1:
         swap = join(kv[1:], 2 * tok_rows)
         kv_other += [to_member(swap, s) for s in members]
@@ -389,13 +391,13 @@
     q_pick = (q_block[:, None] == jnp.arange(block_mask.shape[0])[None, :]).astype(jnp.float32)
     row_mask = jnp.dot(q_pick, block_mask.astype(jnp.float32))
 
-    def bias_of(steps):
+    def bias_of(swaps):
         device = jnp.stack(
             [
                 (origin(group, t, groups) * gather + origin(member, s, gather)) * head_count
                 + origin(head_index, z, head_count)
-                for s in steps
-                for t in range(groups)
+                for s in swaps
+                for t in steps
                 for z in range(head_count)
             ]
         )
@@ -404,8 +406,6 @@
         seen = jnp.dot(row_mask, pick.astype(jnp.float32))
         return jnp.where(seen > 0.5, 0.0, MASKED).astype(jnp.float32)
 
-    every = range(groups)
-    steps = [*every[-1:], *every[1:-1], *every[:1]] if groups > 1 else [0]
     bias = [bias_of([0])] + ([bias_of(members)] if gather > 1 else [])
     away = steps[:-1]
     if groups > 1:

time: 38.5 us -> 37.6 us (0.977)
  waiting for transfers between devices: 7.55 us -> 6.62 us
    ppermute x6, waiting for transfers between devices: 1.15 us -> 0.22 us  [to_group(): return lax.ppermute(x, 'seq', pairs)]
  transfers between devices with their start and end apart: 15 -> 15, of which waited for: 5 -> 5; matrix products, arithmetic and copies ran while one was open for 3% -> 3% of each run, Pallas kernels for 11% -> 12%
where the time goes in v2:
time: 37.6 us; the launch traced here: 37.3 us
  starting transfers between devices  21 us (56%)
  Pallas kernels  7.76 us (21%)
  waiting for transfers between devices  6.62 us (18%)
  local copies, waits for them, and re-layouts  0.97 us (3%)
  matrix products  0.44 us (1%)
    ppermute x6, starting transfers between devices, to_group(): return lax.ppermute(x, 'seq', pairs)  9.13 us
    ppermute x3, starting transfers between devices, to_head(): lax.ppermute(x, 'head', [(h, partner(h, t, head_count)) for h in range(he...  7.66 us
    pallas_call x4, Pallas kernels, attend(): pl.pallas_call(functools.partial(attend_kernel, tuple(pieces), tuple(((le...  5.06 us
    ppermute x3, starting transfers between devices, from_group(): return lax.ppermute(x, 'seq', pairs)  3.55 us
    ppermute x3, waiting for transfers between devices, from_group(): return lax.ppermute(x, 'seq', pairs)  3.25 us
    ppermute x3, waiting for transfers between devices, to_head(): lax.ppermute(x, 'head', [(h, partner(h, t, head_count)) for h in range(he...  3.14 us
    pallas_call x1, Pallas kernels, prepare(): pl.pallas_call(functools.partial(prepare_kernel, groups, gather, shards),...  1.8 us
    pallas_call x1, Pallas kernels, unpack(): pl.pallas_call(functools.partial(unpack_kernel, tuple(steps), gather, wid...  0.77 us
  transfers between devices with their start and end apart: 15, of which 5 were waited for; matrix products, arithmetic and copies ran while one was open for 3% of the time, Pallas kernels for 12%

profile of v2, /device:TPU:0, one launch (start us, length us, event | category | flops | bytes accessed | tf_op | source)
XLA Modules:
  0.0 37.3 jit_solution(9677246411513574521)
XLA Ops:
  0.0 1.8 %prepare.1 = (bf16[384,384]{1,0:T(8,128)(2,1)S(1)}, bf16[384,384]{1,0:T(8,128)(2,1)S(1)}, bf16[384,384]{1,0:T(8,128)(2,1)S(1)}, bf16[384,384]{1,0:T(8,128)(2,1)S...) custom-call(bf16[128,1536]{1,0:T(8,128)(2,1)} %refs_0_.1, ...), custom_call_target="tpu_custom_call" | custom-call | flops 393216 | bytes 3145728 | tf_op jit(solution)/shard_map/prepare/pallas_call | solution.py:92
  1.8 0.5 %collective-permute-start.1 = (bf16[256,384]{1,0:T(8,128)(2,1)S(1)}, bf16[256,384]{1,0:T(8,128)(2,1)S(1)}, u32[]{:S(2)}, u32[]{:S(2)}) collective-permute-start(bf16[256,384]{1,0:T(8,128)(2,1)S(1)} %slice.51), channel_id=1, source_target_pairs={{0,4},{4,0},{8,12},{12,8},{16,20},{20,16},{24,28},{28,24},{1,5},{5... | collective-permute-start | bytes 589832 | tf_op jit(solution)/shard_map/ppermute | solution.py:345
  2.4 3.5 %collective-permute-start = (bf16[384,384]{1,0:T(8,128)(2,1)S(1)}, bf16[384,384]{1,0:T(8,128)(2,1)S(1)}, u32[]{:S(2)}, u32[]{:S(2)}) collective-permute-start(bf16[384,384]{1,0:T(8,128)(2,1)S(1)} %get-tuple-element.47), channel_id=1, source_target_pairs={{0,24},{4,28},{8,16},{12,20},{16,8},{20,12},{24,0},{28,4},{1,25},{... | collective-permute-start | bytes 884744 | tf_op jit(solution)/shard_map/ppermute | solution.py:331
  5.9 1.6 %collective-permute-start.2 = (bf16[4,2,16,384]{3,2,1,0:T(8,128)(2,1)S(1)}, bf16[4,2,16,384]{3,2,1,0:T(8,128)(2,1)S(1)}, u32[]{:S(2)}, u32[]{:S(2)}) collective-permute-start(bf16[4,2,16,384]{3,2,1,0:T(8,128)(2,1)S(1)} %get-tuple-element.57), channel_id=1, source_target_pairs={{0,1},{1,0},{2,3},{3,2},{4,5},{5,4},{6,7},{7,6},{8,9},{9,8},{10,11... | collective-permute-start | bytes 294920 | tf_op jit(solution)/shard_map/ppermute | solution.py:350
  7.5 2.7 %collective-permute-start.3 = (bf16[4,2,16,384]{3,2,1,0:T(8,128)(2,1)S(1)}, bf16[4,2,16,384]{3,2,1,0:T(8,128)(2,1)S(1)}, u32[]{:S(2)}, u32[]{:S(2)}) collective-permute-start(bf16[4,2,16,384]{3,2,1,0:T(8,128)(2,1)S(1)} %get-tuple-element.59), channel_id=1, source_target_pairs={{0,2},{1,3},{2,0},{3,1},{4,6},{5,7},{6,4},{7,5},{8,10},{9,11},{10,... | collective-permute-start | bytes 294920 | tf_op jit(solution)/shard_map/ppermute | solution.py:350
  10.1 0.5 %collective-permute-start.5 = (bf16[384,384]{1,0:T(8,128)(2,1)S(1)}, bf16[384,384]{1,0:T(8,128)(2,1)S(1)}, u32[]{:S(2)}, u32[]{:S(2)}) collective-permute-start(bf16[384,384]{1,0:T(8,128)(2,1)S(1)} %get-tuple-element.62), channel_id=1, source_target_pairs={{0,8},{4,12},{8,0},{12,4},{16,24},{20,28},{24,16},{28,20},{1,9},{5... | collective-permute-start | bytes 884744 | tf_op jit(solution)/shard_map/ppermute | solution.py:331
  10.7 1.4 %collective-permute-start.6 = (bf16[384,384]{1,0:T(8,128)(2,1)S(1)}, bf16[384,384]{1,0:T(8,128)(2,1)S(1)}, u32[]{:S(2)}, u32[]{:S(2)}) collective-permute-start(bf16[384,384]{1,0:T(8,128)(2,1)S(1)} %get-tuple-element.64), channel_id=1, source_target_pairs={{0,16},{4,20},{8,24},{12,28},{16,0},{20,4},{24,8},{28,12},{1,17},{... | collective-permute-start | bytes 884744 | tf_op jit(solution)/shard_map/ppermute | solution.py:331
  12.1 3.4 %collective-permute-start.4 = (bf16[4,2,16,384]{3,2,1,0:T(8,128)(2,1)S(1)}, bf16[4,2,16,384]{3,2,1,0:T(8,128)(2,1)S(1)}, u32[]{:S(2)}, u32[]{:S(2)}) collective-permute-start(bf16[4,2,16,384]{3,2,1,0:T(8,128)(2,1)S(1)} %get-tuple-element.60), channel_id=1, source_target_pairs={{0,3},{1,2},{2,1},{3,0},{4,7},{5,6},{6,5},{7,4},{8,11},{9,10},{10,... | collective-permute-start | bytes 294920 | tf_op jit(solution)/shard_map/ppermute | solution.py:350
  15.5 3.1 %collective-permute-done.4 = bf16[4,2,16,384]{3,2,1,0:T(8,128)(2,1)S(1)} collective-permute-done((bf16[4,2,16,384]{3,2,1,0:T(8,128)(2,1)S(1)}, bf16[4,2,16,384]{3,2,1,0:T(8,128)(2,1)S(1)}, u32[]{:S(2)}, u32[]{:S(2)}) %collective-permute-start.4) | collective-permute-done | bytes 98336 | tf_op jit(solution)/shard_map/ppermute | solution.py:350
  18.7 1.6 %collective-permute-start.7 = (bf16[128,384]{1,0:T(8,128)(2,1)S(1)}, bf16[128,384]{1,0:T(8,128)(2,1)S(1)}, u32[]{:S(2)}, u32[]{:S(2)}) collective-permute-start(bf16[128,384]{1,0:T(8,128)(2,1)S(1)} %interleave.4), channel_id=1, source_target_pairs={{0,24},{4,28},{8,16},{12,20},{16,8},{20,12},{24,0},{28,4},{1,25},{... | collective-permute-start | bytes 294920 | tf_op jit(solution)/shard_map/ppermute | solution.py:331
  20.3 0.6 %collective-permute-start.8 = (bf16[128,384]{1,0:T(8,128)(2,1)S(1)}, bf16[128,384]{1,0:T(8,128)(2,1)S(1)}, u32[]{:S(2)}, u32[]{:S(2)}) collective-permute-start(bf16[128,384]{1,0:T(8,128)(2,1)S(1)} %interleave.5), channel_id=1, source_target_pairs={{0,8},{4,12},{8,0},{12,4},{16,24},{20,28},{24,16},{28,20},{1,9},{5... | collective-permute-start | bytes 294920 | tf_op jit(solution)/shard_map/ppermute | solution.py:331
  21.0 1.5 %collective-permute-start.9 = (bf16[128,384]{1,0:T(8,128)(2,1)S(1)}, bf16[128,384]{1,0:T(8,128)(2,1)S(1)}, u32[]{:S(2)}, u32[]{:S(2)}) collective-permute-start(bf16[128,384]{1,0:T(8,128)(2,1)S(1)} %interleave.6), channel_id=1, source_target_pairs={{0,16},{4,20},{8,24},{12,28},{16,0},{20,4},{24,8},{28,12},{1,17},{... | collective-permute-start | bytes 294920 | tf_op jit(solution)/shard_map/ppermute | solution.py:331
  22.5 0.1 stack.155
  22.6 0.1 stack.138
  22.9 0.1 add.233
  23.1 0.1 add.253
  23.3 0.1 add.277
  23.4 0.4 %copy-done = s32[16,16]{1,0:T(8,128)S(1)} copy-done((s32[16,16]{1,0:T(8,128)S(1)}, s32[16,16]{1,0:T(8,128)}, u32[]{:S(2)}) %copy-start) | copy-done | bytes 1048
  23.9 0.2 fusion.4
  24.1 0.1 fusion.1.refs_7_.refs_9_
  24.2 0.1 fusion.refs_4_.refs_13_
  24.3 1.1 %attend.4 = (f32[384,384]{1,0:T(8,128)S(1)}, f32[384,384]{1,0:T(8,128)S(1)}, f32[384,384]{1,0:T(8,128)S(1)}) custom-call(bf16[384,384]{1,0:T(8,128)(2,1)S(1)} %collective-permute-done.refs_0_.refs_6_.refs_2_.refs_4_, bf16[384,384]{1,0:T(8,128)(2,1)S(1)} %collective-permute-done.5.refs_1_.refs_4_.refs_0_.refs_2_, ...), custom_call_target="tpu_custom_call" | custom-call | flops 301989888 | bytes 786432 | tf_op jit(solution)/shard_map/attend/pallas_call | solution.py:248
  25.4 0.2 collective-permute-done.9.refs_2_.refs_5_.refs_7_
  25.8 1.7 %attend.5 = (f32[384,384]{1,0:T(8,128)S(1)}, f32[384,384]{1,0:T(8,128)S(1)}, f32[384,384]{1,0:T(8,128)S(1)}) custom-call(bf16[384,384]{1,0:T(8,128)(2,1)S(1)} %collective-permute-done.refs_0_.refs_6_.refs_2_.refs_4_, bf16[384,384]{1,0:T(8,128)(2,1)S(1)} %collective-permute-done.5.refs_1_.refs_4_.refs_0_.refs_2_, ...), custom_call_target="tpu_custom_call" | custom-call | flops 452984832 | bytes 1179648 | tf_op jit(solution)/shard_map/attend/pallas_call | solution.py:248
  27.5 0.8 %attend.6 = (bf16[128,384]{1,0:T(8,128)(2,1)S(1)}, bf16[128,384]{1,0:T(8,128)(2,1)S(1)}, bf16[128,384]{1,0:T(8,128)(2,1)S(1)}) custom-call(bf16[384,384]{1,0:T(8,128)(2,1)S(1)} %collective-permute-done.refs_0_.refs_6_.refs_2_.refs_4_, bf16[384,384]{1,0:T(8,128)(2,1)S(1)} %collective-permute-done.5.refs_1_.refs_4_.refs_0_.refs_2_, ...), custom_call_target="tpu_custom_call" | custom-call | flops 150994944 | bytes 393216 | tf_op jit(solution)/shard_map/attend/pallas_call | solution.py:248
  28.3 1.5 %collective-permute-start.12 = (bf16[128,384]{1,0:T(8,128)(2,1)S(1)}, bf16[128,384]{1,0:T(8,128)(2,1)S(1)}, u32[]{:S(2)}, u32[]{:S(2)}) collective-permute-start(bf16[128,384]{1,0:T(8,128)(2,1)S(1)} %get-tuple-element.86), channel_id=1, source_target_pairs={{0,24},{4,28},{8,16},{12,20},{16,8},{20,12},{24,0},{28,4},{1,25},{... | collective-permute-start | bytes 294920 | tf_op jit(solution)/shard_map/ppermute | solution.py:339
  29.8 1.4 %collective-permute-start.13 = (bf16[128,384]{1,0:T(8,128)(2,1)S(1)}, bf16[128,384]{1,0:T(8,128)(2,1)S(1)}, u32[]{:S(2)}, u32[]{:S(2)}) collective-permute-start(bf16[128,384]{1,0:T(8,128)(2,1)S(1)} %get-tuple-element.87), channel_id=1, source_target_pairs={{0,8},{4,12},{8,0},{12,4},{16,24},{20,28},{24,16},{28,20},{1,9},{5... | collective-permute-start | bytes 294920 | tf_op jit(solution)/shard_map/ppermute | solution.py:339
  31.2 0.6 %collective-permute-start.14 = (bf16[128,384]{1,0:T(8,128)(2,1)S(1)}, bf16[128,384]{1,0:T(8,128)(2,1)S(1)}, u32[]{:S(2)}, u32[]{:S(2)}) collective-permute-start(bf16[128,384]{1,0:T(8,128)(2,1)S(1)} %get-tuple-element.88), channel_id=1, source_target_pairs={{0,16},{4,20},{8,24},{12,28},{16,0},{20,4},{24,8},{28,12},{1,17},{... | collective-permute-start | bytes 294920 | tf_op jit(solution)/shard_map/ppermute | solution.py:339
  31.9 1.4 %attend.7.refs_3_ = bf16[128,384]{1,0:T(8,128)(2,1)S(1)} custom-call(bf16[384,384]{1,0:T(8,128)(2,1)S(1)} %get-tuple-element.54.refs_3_.refs_0_.refs_1_, bf16[384,384]{1,0:T(8,128)(2,1)S(1)} %get-tuple-element.54.refs_3_.refs_0_.refs_1_, bf16[384,384]{1,0:T(8,128)(2,1)S(1)} %collective-permute-done.5.refs_1_.refs_4_.refs_0_.refs_2_, ...), custom_call_target="tpu_custom_call" | custom-call | flops 301989888 | bytes 2359296 | tf_op jit(solution)/shard_map/attend/pallas_call | solution.py:248
  33.3 1.5 %collective-permute-done.12.refs_0_ = bf16[128,384]{1,0:T(8,128)(2,1)S(1)} collective-permute-done((bf16[128,384]{1,0:T(8,128)(2,1)S(1)}, bf16[128,384]{1,0:T(8,128)(2,1)S(1)}, u32[]{:S(2)}, u32[]{:S(2)}) %collective-permute-start.12) | collective-permute-done | bytes 98336 | tf_op jit(solution)/shard_map/ppermute | solution.py:339
  34.9 1.6 %collective-permute-done.13.refs_1_ = bf16[128,384]{1,0:T(8,128)(2,1)S(1)} collective-permute-done((bf16[128,384]{1,0:T(8,128)(2,1)S(1)}, bf16[128,384]{1,0:T(8,128)(2,1)S(1)}, u32[]{:S(2)}, u32[]{:S(2)}) %collective-permute-start.13) | collective-permute-done | bytes 98336 | tf_op jit(solution)/shard_map/ppermute | solution.py:339
  36.6 0.8 %unpack_heads.1 = bf16[128,1536]{1,0:T(8,128)(2,1)} custom-call(bf16[128,384]{1,0:T(8,128)(2,1)S(1)} %collective-permute-done.12.refs_0_, bf16[128,384]{1,0:T(8,128)(2,1)S(1)} %collective-permute-done.13.refs_1_, bf16[128,384]{1,0:T(8,128)(2,1)S(1)} %collective-permute-done.14.refs_2_, bf16[128,384]{1,0:T(8,128)(2,1)S(1)} %attend.7.refs_3_), custom_call_target="tpu_custom_call" | custom-call | bytes 786432 | tf_op jit(solution)/shard_map/unpack_heads/pallas_call | solution.py:290
  (33 shorter events, 0.8 us)
Async XLA Ops:
  1.8 4.0 %collective-permute-start.1 = (bf16[256,384]{1,0:T(8,128)(2,1)S(1)}, bf16[256,384]{1,0:T(8,128)(2,1)S(1)}, u32[]{:S(2)}, u32[]{:S(2)}) collective-permute-start(bf16[256,384]{1,0:T(8,128)(2,1)S(1)} %slice.51), channel_id=1, source_target_pairs={{0,4},{4,0},{8,12},{12,8},{16,20},{20,16},{24,28},{28,24},{1,5},{5... | collective-permute-start | bytes 589832 | tf_op jit(solution)/shard_map/ppermute | solution.py:345
  2.4 18.6 %collective-permute-start = (bf16[384,384]{1,0:T(8,128)(2,1)S(1)}, bf16[384,384]{1,0:T(8,128)(2,1)S(1)}, u32[]{:S(2)}, u32[]{:S(2)}) collective-permute-start(bf16[384,384]{1,0:T(8,128)(2,1)S(1)} %get-tuple-element.47), channel_id=1, source_target_pairs={{0,24},{4,28},{8,16},{12,20},{16,8},{20,12},{24,0},{28,4},{1,25},{... | collective-permute-start | bytes 884744 | tf_op jit(solution)/shard_map/ppermute | solution.py:331
  5.9 6.2 %collective-permute-start.2 = (bf16[4,2,16,384]{3,2,1,0:T(8,128)(2,1)S(1)}, bf16[4,2,16,384]{3,2,1,0:T(8,128)(2,1)S(1)}, u32[]{:S(2)}, u32[]{:S(2)}) collective-permute-start(bf16[4,2,16,384]{3,2,1,0:T(8,128)(2,1)S(1)} %get-tuple-element.57), channel_id=1, source_target_pairs={{0,1},{1,0},{2,3},{3,2},{4,5},{5,4},{6,7},{7,6},{8,9},{9,8},{10,11... | collective-permute-start | bytes 294920 | tf_op jit(solution)/shard_map/ppermute | solution.py:350
  7.5 8.0 %collective-permute-start.3 = (bf16[4,2,16,384]{3,2,1,0:T(8,128)(2,1)S(1)}, bf16[4,2,16,384]{3,2,1,0:T(8,128)(2,1)S(1)}, u32[]{:S(2)}, u32[]{:S(2)}) collective-permute-start(bf16[4,2,16,384]{3,2,1,0:T(8,128)(2,1)S(1)} %get-tuple-element.59), channel_id=1, source_target_pairs={{0,2},{1,3},{2,0},{3,1},{4,6},{5,7},{6,4},{7,5},{8,10},{9,11},{10,... | collective-permute-start | bytes 294920 | tf_op jit(solution)/shard_map/ppermute | solution.py:350
  10.1 12.3 %collective-permute-start.5 = (bf16[384,384]{1,0:T(8,128)(2,1)S(1)}, bf16[384,384]{1,0:T(8,128)(2,1)S(1)}, u32[]{:S(2)}, u32[]{:S(2)}) collective-permute-start(bf16[384,384]{1,0:T(8,128)(2,1)S(1)} %get-tuple-element.62), channel_id=1, source_target_pairs={{0,8},{4,12},{8,0},{12,4},{16,24},{20,28},{24,16},{28,20},{1,9},{5... | collective-permute-start | bytes 884744 | tf_op jit(solution)/shard_map/ppermute | solution.py:331
  10.7 11.8 %collective-permute-start.6 = (bf16[384,384]{1,0:T(8,128)(2,1)S(1)}, bf16[384,384]{1,0:T(8,128)(2,1)S(1)}, u32[]{:S(2)}, u32[]{:S(2)}) collective-permute-start(bf16[384,384]{1,0:T(8,128)(2,1)S(1)} %get-tuple-element.64), channel_id=1, source_target_pairs={{0,16},{4,20},{8,24},{12,28},{16,0},{20,4},{24,8},{28,12},{1,17},{... | collective-permute-start | bytes 884744 | tf_op jit(solution)/shard_map/ppermute | solution.py:331
  12.1 6.6 %collective-permute-start.4 = (bf16[4,2,16,384]{3,2,1,0:T(8,128)(2,1)S(1)}, bf16[4,2,16,384]{3,2,1,0:T(8,128)(2,1)S(1)}, u32[]{:S(2)}, u32[]{:S(2)}) collective-permute-start(bf16[4,2,16,384]{3,2,1,0:T(8,128)(2,1)S(1)} %get-tuple-element.60), channel_id=1, source_target_pairs={{0,3},{1,2},{2,1},{3,0},{4,7},{5,6},{6,5},{7,4},{8,11},{9,10},{10,... | collective-permute-start | bytes 294920 | tf_op jit(solution)/shard_map/ppermute | solution.py:350
  18.7 6.7 %collective-permute-start.7 = (bf16[128,384]{1,0:T(8,128)(2,1)S(1)}, bf16[128,384]{1,0:T(8,128)(2,1)S(1)}, u32[]{:S(2)}, u32[]{:S(2)}) collective-permute-start(bf16[128,384]{1,0:T(8,128)(2,1)S(1)} %interleave.4), channel_id=1, source_target_pairs={{0,24},{4,28},{8,16},{12,20},{16,8},{20,12},{24,0},{28,4},{1,25},{... | collective-permute-start | bytes 294920 | tf_op jit(solution)/shard_map/ppermute | solution.py:331
  20.3 5.1 %collective-permute-start.8 = (bf16[128,384]{1,0:T(8,128)(2,1)S(1)}, bf16[128,384]{1,0:T(8,128)(2,1)S(1)}, u32[]{:S(2)}, u32[]{:S(2)}) collective-permute-start(bf16[128,384]{1,0:T(8,128)(2,1)S(1)} %interleave.5), channel_id=1, source_target_pairs={{0,8},{4,12},{8,0},{12,4},{16,24},{20,28},{24,16},{28,20},{1,9},{5... | collective-permute-start | bytes 294920 | tf_op jit(solution)/shard_map/ppermute | solution.py:331
  21.0 4.7 %collective-permute-start.9 = (bf16[128,384]{1,0:T(8,128)(2,1)S(1)}, bf16[128,384]{1,0:T(8,128)(2,1)S(1)}, u32[]{:S(2)}, u32[]{:S(2)}) collective-permute-start(bf16[128,384]{1,0:T(8,128)(2,1)S(1)} %interleave.6), channel_id=1, source_target_pairs={{0,16},{4,20},{8,24},{12,28},{16,0},{20,4},{24,8},{28,12},{1,17},{... | collective-permute-start | bytes 294920 | tf_op jit(solution)/shard_map/ppermute | solution.py:331
  23.2 0.7 %copy-start = (s32[16,16]{1,0:T(8,128)S(1)}, s32[16,16]{1,0:T(8,128)}, u32[]{:S(2)}) copy-start(s32[16,16]{1,0:T(8,128)} %param.15) | copy-start | bytes 3076
  23.4 2.4 %collective-permute-start.11 = (bf16[3,256,384]{2,1,0:T(8,128)(2,1)S(1)}, bf16[3,256,384]{2,1,0:T(8,128)(2,1)S(1)}, u32[]{:S(2)}, u32[]{:S(2)}) collective-permute-start(bf16[3,256,384]{2,1,0:T(8,128)(2,1)S(1)} %join.3), channel_id=1, source_target_pairs={{0,4},{4,0},{8,12},{12,8},{16,20},{20,16},{24,28},{28,24},{1,5},{5... | collective-permute-start | bytes 1769480 | tf_op jit(solution)/shard_map/ppermute | solution.py:345
  25.7 1.8 %collective-permute-start.10 = (bf16[4,128,384]{2,1,0:T(8,128)(2,1)S(1)}, bf16[4,128,384]{2,1,0:T(8,128)(2,1)S(1)}, u32[]{:S(2)}, u32[]{:S(2)}) collective-permute-start(bf16[4,128,384]{2,1,0:T(8,128)(2,1)S(1)} %join.2), channel_id=1, source_target_pairs={{0,4},{4,0},{8,12},{12,8},{16,20},{20,16},{24,28},{28,24},{1,5},{5... | collective-permute-start | bytes 1179656 | tf_op jit(solution)/shard_map/ppermute | solution.py:345
  28.3 6.6 %collective-permute-start.12 = (bf16[128,384]{1,0:T(8,128)(2,1)S(1)}, bf16[128,384]{1,0:T(8,128)(2,1)S(1)}, u32[]{:S(2)}, u32[]{:S(2)}) collective-permute-start(bf16[128,384]{1,0:T(8,128)(2,1)S(1)} %get-tuple-element.86), channel_id=1, source_target_pairs={{0,24},{4,28},{8,16},{12,20},{16,8},{20,12},{24,0},{28,4},{1,25},{... | collective-permute-start | bytes 294920 | tf_op jit(solution)/shard_map/ppermute | solution.py:339
  29.8 6.7 %collective-permute-start.13 = (bf16[128,384]{1,0:T(8,128)(2,1)S(1)}, bf16[128,384]{1,0:T(8,128)(2,1)S(1)}, u32[]{:S(2)}, u32[]{:S(2)}) collective-permute-start(bf16[128,384]{1,0:T(8,128)(2,1)S(1)} %get-tuple-element.87), channel_id=1, source_target_pairs={{0,8},{4,12},{8,0},{12,4},{16,24},{20,28},{24,16},{28,20},{1,9},{5... | collective-permute-start | bytes 294920 | tf_op jit(solution)/shard_map/ppermute | solution.py:339
  31.2 5.3 %collective-permute-start.14 = (bf16[128,384]{1,0:T(8,128)(2,1)S(1)}, bf16[128,384]{1,0:T(8,128)(2,1)S(1)}, u32[]{:S(2)}, u32[]{:S(2)}) collective-permute-start(bf16[128,384]{1,0:T(8,128)(2,1)S(1)} %get-tuple-element.88), channel_id=1, source_target_pairs={{0,16},{4,20},{8,24},{12,28},{16,0},{20,4},{24,8},{28,12},{1,17},{... | collective-permute-start | bytes 294920 | tf_op jit(solution)/shard_map/ppermute | solution.py:339

commit v3 on v2

--- a/solution.py
+++ b/solution.py
@@ -407,7 +407,7 @@
         return jnp.where(seen > 0.5, 0.0, MASKED).astype(jnp.float32)
 
     bias = [bias_of([0])] + ([bias_of(members)] if gather > 1 else [])
-    away = steps[:-1]
+    away, home = every[1:], [*every[1:], 0]
     if groups > 1:
         state = attend(kv, away, [(kv, None)])
         cache, state, bias = lax.optimization_barrier((cache, state, bias))
@@ -423,7 +423,7 @@
             state = attend(kv, away, last, state, True)
         parts.update(zip(away, state))
     parts[0] = attend(kv, [0], [(kv, None), *sets, *last], (), True)[0]
-    return unpack([from_group(parts[t], t) for t in steps], steps, gather)
+    return unpack([from_group(parts[t], t) for t in home], home, gather)
 
 
 def solution(mesh):

time: 37.6 us -> 37.9 us (level)
  transfers between devices with their start and end apart: 15 -> 15, of which waited for: 5 -> 4; matrix products, arithmetic and copies ran while one was open for 3% -> 3% of each run, Pallas kernels for 12% -> 12%
where the time goes in v3:
time: 37.9 us; the launch traced here: 37.7 us
  starting transfers between devices  21 us (55%)
  Pallas kernels  7.77 us (21%)
  waiting for transfers between devices  6.94 us (18%)
  local copies, waits for them, and re-layouts  0.97 us (3%)
  matrix products  0.44 us (1%)
    ppermute x6, starting transfers between devices, to_group(): return lax.ppermute(x, 'seq', pairs)  9.13 us
    ppermute x3, starting transfers between devices, to_head(): lax.ppermute(x, 'head', [(h, partner(h, t, head_count)) for h in range(he...  7.66 us
    pallas_call x4, Pallas kernels, attend(): pl.pallas_call(functools.partial(attend_kernel, tuple(pieces), tuple(((le...  5.06 us
    ppermute x3, waiting for transfers between devices, from_group(): return lax.ppermute(x, 'seq', pairs)  3.57 us
    ppermute x3, starting transfers between devices, from_group(): return lax.ppermute(x, 'seq', pairs)  3.55 us
    ppermute x3, waiting for transfers between devices, to_head(): lax.ppermute(x, 'head', [(h, partner(h, t, head_count)) for h in range(he...  3.14 us
    pallas_call x1, Pallas kernels, prepare(): pl.pallas_call(functools.partial(prepare_kernel, groups, gather, shards),...  1.8 us
    pallas_call x1, Pallas kernels, unpack(): pl.pallas_call(functools.partial(unpack_kernel, tuple(steps), gather, wid...  0.77 us
  transfers between devices with their start and end apart: 15, of which 4 were waited for; matrix products, arithmetic and copies ran while one was open for 3% of the time, Pallas kernels for 12%

profile of v3, /device:TPU:0, one launch (start us, length us, event | category | flops | bytes accessed | tf_op | source)
XLA Modules:
  0.0 37.7 jit_solution(10186583135858071743)
XLA Ops:
  0.0 1.8 %prepare.1 = (bf16[384,384]{1,0:T(8,128)(2,1)S(1)}, bf16[384,384]{1,0:T(8,128)(2,1)S(1)}, bf16[384,384]{1,0:T(8,128)(2,1)S(1)}, bf16[384,384]{1,0:T(8,128)(2,1)S...) custom-call(bf16[128,1536]{1,0:T(8,128)(2,1)} %refs_0_.1, ...), custom_call_target="tpu_custom_call" | custom-call | flops 393216 | bytes 3145728 | tf_op jit(solution)/shard_map/prepare/pallas_call | solution.py:92
  1.8 0.5 %collective-permute-start = (bf16[256,384]{1,0:T(8,128)(2,1)S(1)}, bf16[256,384]{1,0:T(8,128)(2,1)S(1)}, u32[]{:S(2)}, u32[]{:S(2)}) collective-permute-start(bf16[256,384]{1,0:T(8,128)(2,1)S(1)} %slice.51), channel_id=1, source_target_pairs={{0,4},{4,0},{8,12},{12,8},{16,20},{20,16},{24,28},{28,24},{1,5},{5... | collective-permute-start | bytes 589832 | tf_op jit(solution)/shard_map/ppermute | solution.py:345
  2.4 3.5 %collective-permute-start.6 = (bf16[384,384]{1,0:T(8,128)(2,1)S(1)}, bf16[384,384]{1,0:T(8,128)(2,1)S(1)}, u32[]{:S(2)}, u32[]{:S(2)}) collective-permute-start(bf16[384,384]{1,0:T(8,128)(2,1)S(1)} %get-tuple-element.64), channel_id=1, source_target_pairs={{0,24},{4,28},{8,16},{12,20},{16,8},{20,12},{24,0},{28,4},{1,25},{... | collective-permute-start | bytes 884744 | tf_op jit(solution)/shard_map/ppermute | solution.py:331
  5.9 1.6 %collective-permute-start.2 = (bf16[4,2,16,384]{3,2,1,0:T(8,128)(2,1)S(1)}, bf16[4,2,16,384]{3,2,1,0:T(8,128)(2,1)S(1)}, u32[]{:S(2)}, u32[]{:S(2)}) collective-permute-start(bf16[4,2,16,384]{3,2,1,0:T(8,128)(2,1)S(1)} %get-tuple-element.57), channel_id=1, source_target_pairs={{0,1},{1,0},{2,3},{3,2},{4,5},{5,4},{6,7},{7,6},{8,9},{9,8},{10,11... | collective-permute-start | bytes 294920 | tf_op jit(solution)/shard_map/ppermute | solution.py:350
  7.5 2.7 %collective-permute-start.3 = (bf16[4,2,16,384]{3,2,1,0:T(8,128)(2,1)S(1)}, bf16[4,2,16,384]{3,2,1,0:T(8,128)(2,1)S(1)}, u32[]{:S(2)}, u32[]{:S(2)}) collective-permute-start(bf16[4,2,16,384]{3,2,1,0:T(8,128)(2,1)S(1)} %get-tuple-element.59), channel_id=1, source_target_pairs={{0,2},{1,3},{2,0},{3,1},{4,6},{5,7},{6,4},{7,5},{8,10},{9,11},{10,... | collective-permute-start | bytes 294920 | tf_op jit(solution)/shard_map/ppermute | solution.py:350
  10.1 0.5 %collective-permute-start.1 = (bf16[384,384]{1,0:T(8,128)(2,1)S(1)}, bf16[384,384]{1,0:T(8,128)(2,1)S(1)}, u32[]{:S(2)}, u32[]{:S(2)}) collective-permute-start(bf16[384,384]{1,0:T(8,128)(2,1)S(1)} %get-tuple-element.54), channel_id=1, source_target_pairs={{0,8},{4,12},{8,0},{12,4},{16,24},{20,28},{24,16},{28,20},{1,9},{5... | collective-permute-start | bytes 884744 | tf_op jit(solution)/shard_map/ppermute | solution.py:331
  10.7 1.4 %collective-permute-start.5 = (bf16[384,384]{1,0:T(8,128)(2,1)S(1)}, bf16[384,384]{1,0:T(8,128)(2,1)S(1)}, u32[]{:S(2)}, u32[]{:S(2)}) collective-permute-start(bf16[384,384]{1,0:T(8,128)(2,1)S(1)} %get-tuple-element.62), channel_id=1, source_target_pairs={{0,16},{4,20},{8,24},{12,28},{16,0},{20,4},{24,8},{28,12},{1,17},{... | collective-permute-start | bytes 884744 | tf_op jit(solution)/shard_map/ppermute | solution.py:331
  12.1 3.4 %collective-permute-start.4 = (bf16[4,2,16,384]{3,2,1,0:T(8,128)(2,1)S(1)}, bf16[4,2,16,384]{3,2,1,0:T(8,128)(2,1)S(1)}, u32[]{:S(2)}, u32[]{:S(2)}) collective-permute-start(bf16[4,2,16,384]{3,2,1,0:T(8,128)(2,1)S(1)} %get-tuple-element.60), channel_id=1, source_target_pairs={{0,3},{1,2},{2,1},{3,0},{4,7},{5,6},{6,5},{7,4},{8,11},{9,10},{10,... | collective-permute-start | bytes 294920 | tf_op jit(solution)/shard_map/ppermute | solution.py:350
  15.5 3.1 %collective-permute-done.4 = bf16[4,2,16,384]{3,2,1,0:T(8,128)(2,1)S(1)} collective-permute-done((bf16[4,2,16,384]{3,2,1,0:T(8,128)(2,1)S(1)}, bf16[4,2,16,384]{3,2,1,0:T(8,128)(2,1)S(1)}, u32[]{:S(2)}, u32[]{:S(2)}) %collective-permute-start.4) | collective-permute-done | bytes 98336 | tf_op jit(solution)/shard_map/ppermute | solution.py:350
  18.7 1.6 %collective-permute-start.7 = (bf16[128,384]{1,0:T(8,128)(2,1)S(1)}, bf16[128,384]{1,0:T(8,128)(2,1)S(1)}, u32[]{:S(2)}, u32[]{:S(2)}) collective-permute-start(bf16[128,384]{1,0:T(8,128)(2,1)S(1)} %interleave.4), channel_id=1, source_target_pairs={{0,24},{4,28},{8,16},{12,20},{16,8},{20,12},{24,0},{28,4},{1,25},{... | collective-permute-start | bytes 294920 | tf_op jit(solution)/shard_map/ppermute | solution.py:331
  20.3 0.6 %collective-permute-start.8 = (bf16[128,384]{1,0:T(8,128)(2,1)S(1)}, bf16[128,384]{1,0:T(8,128)(2,1)S(1)}, u32[]{:S(2)}, u32[]{:S(2)}) collective-permute-start(bf16[128,384]{1,0:T(8,128)(2,1)S(1)} %interleave.5), channel_id=1, source_target_pairs={{0,8},{4,12},{8,0},{12,4},{16,24},{20,28},{24,16},{28,20},{1,9},{5... | collective-permute-start | bytes 294920 | tf_op jit(solution)/shard_map/ppermute | solution.py:331
  21.0 1.5 %collective-permute-start.9 = (bf16[128,384]{1,0:T(8,128)(2,1)S(1)}, bf16[128,384]{1,0:T(8,128)(2,1)S(1)}, u32[]{:S(2)}, u32[]{:S(2)}) collective-permute-start(bf16[128,384]{1,0:T(8,128)(2,1)S(1)} %interleave.6), channel_id=1, source_target_pairs={{0,16},{4,20},{8,24},{12,28},{16,0},{20,4},{24,8},{28,12},{1,17},{... | collective-permute-start | bytes 294920 | tf_op jit(solution)/shard_map/ppermute | solution.py:331
  22.5 0.1 stack.155
  22.6 0.1 stack.138
  22.9 0.1 add.233
  23.1 0.1 add.253
  23.3 0.1 add.277
  23.4 0.4 %copy-done = s32[16,16]{1,0:T(8,128)S(1)} copy-done((s32[16,16]{1,0:T(8,128)S(1)}, s32[16,16]{1,0:T(8,128)}, u32[]{:S(2)}) %copy-start) | copy-done | bytes 1048
  23.9 0.2 fusion.4
  24.1 0.1 fusion.1.refs_7_.refs_9_
  24.2 0.1 fusion.refs_4_.refs_13_
  24.3 1.1 %attend.4 = (f32[384,384]{1,0:T(8,128)S(1)}, f32[384,384]{1,0:T(8,128)S(1)}, f32[384,384]{1,0:T(8,128)S(1)}) custom-call(bf16[384,384]{1,0:T(8,128)(2,1)S(1)} %collective-permute-done.1.refs_0_.refs_4_.refs_2_, bf16[384,384]{1,0:T(8,128)(2,1)S(1)} %collective-permute-done.5.refs_1_.refs_5_.refs_3_, ...), custom_call_target="tpu_custom_call" | custom-call | flops 301989888 | bytes 786432 | tf_op jit(solution)/shard_map/attend/pallas_call | solution.py:248
  25.4 0.2 collective-permute-done.9.refs_2_.refs_5_.refs_7_
  25.8 1.7 %attend.5 = (f32[384,384]{1,0:T(8,128)S(1)}, f32[384,384]{1,0:T(8,128)S(1)}, f32[384,384]{1,0:T(8,128)S(1)}) custom-call(bf16[384,384]{1,0:T(8,128)(2,1)S(1)} %collective-permute-done.1.refs_0_.refs_4_.refs_2_, bf16[384,384]{1,0:T(8,128)(2,1)S(1)} %collective-permute-done.5.refs_1_.refs_5_.refs_3_, ...), custom_call_target="tpu_custom_call" | custom-call | flops 452984832 | bytes 1179648 | tf_op jit(solution)/shard_map/attend/pallas_call | solution.py:248
  27.5 0.8 %attend.6 = (bf16[128,384]{1,0:T(8,128)(2,1)S(1)}, bf16[128,384]{1,0:T(8,128)(2,1)S(1)}, bf16[128,384]{1,0:T(8,128)(2,1)S(1)}) custom-call(bf16[384,384]{1,0:T(8,128)(2,1)S(1)} %collective-permute-done.1.refs_0_.refs_4_.refs_2_, bf16[384,384]{1,0:T(8,128)(2,1)S(1)} %collective-permute-done.5.refs_1_.refs_5_.refs_3_, ...), custom_call_target="tpu_custom_call" | custom-call | flops 150994944 | bytes 393216 | tf_op jit(solution)/shard_map/attend/pallas_call | solution.py:248
  28.3 1.6 %collective-permute-start.12 = (bf16[128,384]{1,0:T(8,128)(2,1)S(1)}, bf16[128,384]{1,0:T(8,128)(2,1)S(1)}, u32[]{:S(2)}, u32[]{:S(2)}) collective-permute-start(bf16[128,384]{1,0:T(8,128)(2,1)S(1)} %get-tuple-element.86), channel_id=1, source_target_pairs={{0,8},{4,12},{8,0},{12,4},{16,24},{20,28},{24,16},{28,20},{1,9},{5... | collective-permute-start | bytes 294920 | tf_op jit(solution)/shard_map/ppermute | solution.py:339
  29.9 0.5 %collective-permute-start.13 = (bf16[128,384]{1,0:T(8,128)(2,1)S(1)}, bf16[128,384]{1,0:T(8,128)(2,1)S(1)}, u32[]{:S(2)}, u32[]{:S(2)}) collective-permute-start(bf16[128,384]{1,0:T(8,128)(2,1)S(1)} %get-tuple-element.87), channel_id=1, source_target_pairs={{0,16},{4,20},{8,24},{12,28},{16,0},{20,4},{24,8},{28,12},{1,17},{... | collective-permute-start | bytes 294920 | tf_op jit(solution)/shard_map/ppermute | solution.py:339
  30.4 1.5 %collective-permute-start.14 = (bf16[128,384]{1,0:T(8,128)(2,1)S(1)}, bf16[128,384]{1,0:T(8,128)(2,1)S(1)}, u32[]{:S(2)}, u32[]{:S(2)}) collective-permute-start(bf16[128,384]{1,0:T(8,128)(2,1)S(1)} %get-tuple-element.88), channel_id=1, source_target_pairs={{0,24},{4,28},{8,16},{12,20},{16,8},{20,12},{24,0},{28,4},{1,25},{... | collective-permute-start | bytes 294920 | tf_op jit(solution)/shard_map/ppermute | solution.py:339
  31.9 1.4 %attend.7.refs_3_ = bf16[128,384]{1,0:T(8,128)(2,1)S(1)} custom-call(bf16[384,384]{1,0:T(8,128)(2,1)S(1)} %get-tuple-element.53.refs_3_.refs_0_.refs_1_, bf16[384,384]{1,0:T(8,128)(2,1)S(1)} %get-tuple-element.53.refs_3_.refs_0_.refs_1_, bf16[384,384]{1,0:T(8,128)(2,1)S(1)} %collective-permute-done.1.refs_0_.refs_4_.refs_2_, ...), custom_call_target="tpu_custom_call" | custom-call | flops 301989888 | bytes 2359296 | tf_op jit(solution)/shard_map/attend/pallas_call | solution.py:248
  33.3 0.2 collective-permute-done.12.refs_0_
  33.6 3.3 %collective-permute-done.13.refs_1_ = bf16[128,384]{1,0:T(8,128)(2,1)S(1)} collective-permute-done((bf16[128,384]{1,0:T(8,128)(2,1)S(1)}, bf16[128,384]{1,0:T(8,128)(2,1)S(1)}, u32[]{:S(2)}, u32[]{:S(2)}) %collective-permute-start.13) | collective-permute-done | bytes 98336 | tf_op jit(solution)/shard_map/ppermute | solution.py:339
  36.9 0.8 %unpack_heads.1 = bf16[128,1536]{1,0:T(8,128)(2,1)} custom-call(bf16[128,384]{1,0:T(8,128)(2,1)S(1)} %collective-permute-done.12.refs_0_, bf16[128,384]{1,0:T(8,128)(2,1)S(1)} %collective-permute-done.13.refs_1_, bf16[128,384]{1,0:T(8,128)(2,1)S(1)} %collective-permute-done.14.refs_2_, bf16[128,384]{1,0:T(8,128)(2,1)S(1)} %attend.7.refs_3_), custom_call_target="tpu_custom_call" | custom-call | bytes 786432 | tf_op jit(solution)/shard_map/unpack_heads/pallas_call | solution.py:290
  (33 shorter events, 0.7 us)
Async XLA Ops:
  1.8 4.0 %collective-permute-start = (bf16[256,384]{1,0:T(8,128)(2,1)S(1)}, bf16[256,384]{1,0:T(8,128)(2,1)S(1)}, u32[]{:S(2)}, u32[]{:S(2)}) collective-permute-start(bf16[256,384]{1,0:T(8,128)(2,1)S(1)} %slice.51), channel_id=1, source_target_pairs={{0,4},{4,0},{8,12},{12,8},{16,20},{20,16},{24,28},{28,24},{1,5},{5... | collective-permute-start | bytes 589832 | tf_op jit(solution)/shard_map/ppermute | solution.py:345
  2.4 18.6 %collective-permute-start.6 = (bf16[384,384]{1,0:T(8,128)(2,1)S(1)}, bf16[384,384]{1,0:T(8,128)(2,1)S(1)}, u32[]{:S(2)}, u32[]{:S(2)}) collective-permute-start(bf16[384,384]{1,0:T(8,128)(2,1)S(1)} %get-tuple-element.64), channel_id=1, source_target_pairs={{0,24},{4,28},{8,16},{12,20},{16,8},{20,12},{24,0},{28,4},{1,25},{... | collective-permute-start | bytes 884744 | tf_op jit(solution)/shard_map/ppermute | solution.py:331
  5.9 6.2 %collective-permute-start.2 = (bf16[4,2,16,384]{3,2,1,0:T(8,128)(2,1)S(1)}, bf16[4,2,16,384]{3,2,1,0:T(8,128)(2,1)S(1)}, u32[]{:S(2)}, u32[]{:S(2)}) collective-permute-start(bf16[4,2,16,384]{3,2,1,0:T(8,128)(2,1)S(1)} %get-tuple-element.57), channel_id=1, source_target_pairs={{0,1},{1,0},{2,3},{3,2},{4,5},{5,4},{6,7},{7,6},{8,9},{9,8},{10,11... | collective-permute-start | bytes 294920 | tf_op jit(solution)/shard_map/ppermute | solution.py:350
  7.5 8.0 %collective-permute-start.3 = (bf16[4,2,16,384]{3,2,1,0:T(8,128)(2,1)S(1)}, bf16[4,2,16,384]{3,2,1,0:T(8,128)(2,1)S(1)}, u32[]{:S(2)}, u32[]{:S(2)}) collective-permute-start(bf16[4,2,16,384]{3,2,1,0:T(8,128)(2,1)S(1)} %get-tuple-element.59), channel_id=1, source_target_pairs={{0,2},{1,3},{2,0},{3,1},{4,6},{5,7},{6,4},{7,5},{8,10},{9,11},{10,... | collective-permute-start | bytes 294920 | tf_op jit(solution)/shard_map/ppermute | solution.py:350
  10.1 12.3 %collective-permute-start.1 = (bf16[384,384]{1,0:T(8,128)(2,1)S(1)}, bf16[384,384]{1,0:T(8,128)(2,1)S(1)}, u32[]{:S(2)}, u32[]{:S(2)}) collective-permute-start(bf16[384,384]{1,0:T(8,128)(2,1)S(1)} %get-tuple-element.54), channel_id=1, source_target_pairs={{0,8},{4,12},{8,0},{12,4},{16,24},{20,28},{24,16},{28,20},{1,9},{5... | collective-permute-start | bytes 884744 | tf_op jit(solution)/shard_map/ppermute | solution.py:331
  10.7 11.8 %collective-permute-start.5 = (bf16[384,384]{1,0:T(8,128)(2,1)S(1)}, bf16[384,384]{1,0:T(8,128)(2,1)S(1)}, u32[]{:S(2)}, u32[]{:S(2)}) collective-permute-start(bf16[384,384]{1,0:T(8,128)(2,1)S(1)} %get-tuple-element.62), channel_id=1, source_target_pairs={{0,16},{4,20},{8,24},{12,28},{16,0},{20,4},{24,8},{28,12},{1,17},{... | collective-permute-start | bytes 884744 | tf_op jit(solution)/shard_map/ppermute | solution.py:331
  12.1 6.6 %collective-permute-start.4 = (bf16[4,2,16,384]{3,2,1,0:T(8,128)(2,1)S(1)}, bf16[4,2,16,384]{3,2,1,0:T(8,128)(2,1)S(1)}, u32[]{:S(2)}, u32[]{:S(2)}) collective-permute-start(bf16[4,2,16,384]{3,2,1,0:T(8,128)(2,1)S(1)} %get-tuple-element.60), channel_id=1, source_target_pairs={{0,3},{1,2},{2,1},{3,0},{4,7},{5,6},{6,5},{7,4},{8,11},{9,10},{10,... | collective-permute-start | bytes 294920 | tf_op jit(solution)/shard_map/ppermute | solution.py:350
  18.7 6.7 %collective-permute-start.7 = (bf16[128,384]{1,0:T(8,128)(2,1)S(1)}, bf16[128,384]{1,0:T(8,128)(2,1)S(1)}, u32[]{:S(2)}, u32[]{:S(2)}) collective-permute-start(bf16[128,384]{1,0:T(8,128)(2,1)S(1)} %interleave.4), channel_id=1, source_target_pairs={{0,24},{4,28},{8,16},{12,20},{16,8},{20,12},{24,0},{28,4},{1,25},{... | collective-permute-start | bytes 294920 | tf_op jit(solution)/shard_map/ppermute | solution.py:331
  20.3 5.1 %collective-permute-start.8 = (bf16[128,384]{1,0:T(8,128)(2,1)S(1)}, bf16[128,384]{1,0:T(8,128)(2,1)S(1)}, u32[]{:S(2)}, u32[]{:S(2)}) collective-permute-start(bf16[128,384]{1,0:T(8,128)(2,1)S(1)} %interleave.5), channel_id=1, source_target_pairs={{0,8},{4,12},{8,0},{12,4},{16,24},{20,28},{24,16},{28,20},{1,9},{5... | collective-permute-start | bytes 294920 | tf_op jit(solution)/shard_map/ppermute | solution.py:331
  21.0 4.7 %collective-permute-start.9 = (bf16[128,384]{1,0:T(8,128)(2,1)S(1)}, bf16[128,384]{1,0:T(8,128)(2,1)S(1)}, u32[]{:S(2)}, u32[]{:S(2)}) collective-permute-start(bf16[128,384]{1,0:T(8,128)(2,1)S(1)} %interleave.6), channel_id=1, source_target_pairs={{0,16},{4,20},{8,24},{12,28},{16,0},{20,4},{24,8},{28,12},{1,17},{... | collective-permute-start | bytes 294920 | tf_op jit(solution)/shard_map/ppermute | solution.py:331
  23.2 0.7 %copy-start = (s32[16,16]{1,0:T(8,128)S(1)}, s32[16,16]{1,0:T(8,128)}, u32[]{:S(2)}) copy-start(s32[16,16]{1,0:T(8,128)} %param.15) | copy-start | bytes 3076
  23.4 2.4 %collective-permute-start.11 = (bf16[3,256,384]{2,1,0:T(8,128)(2,1)S(1)}, bf16[3,256,384]{2,1,0:T(8,128)(2,1)S(1)}, u32[]{:S(2)}, u32[]{:S(2)}) collective-permute-start(bf16[3,256,384]{2,1,0:T(8,128)(2,1)S(1)} %join.3), channel_id=1, source_target_pairs={{0,4},{4,0},{8,12},{12,8},{16,20},{20,16},{24,28},{28,24},{1,5},{5... | collective-permute-start | bytes 1769480 | tf_op jit(solution)/shard_map/ppermute | solution.py:345
  25.7 1.8 %collective-permute-start.10 = (bf16[4,128,384]{2,1,0:T(8,128)(2,1)S(1)}, bf16[4,128,384]{2,1,0:T(8,128)(2,1)S(1)}, u32[]{:S(2)}, u32[]{:S(2)}) collective-permute-start(bf16[4,128,384]{2,1,0:T(8,128)(2,1)S(1)} %join.2), channel_id=1, source_target_pairs={{0,4},{4,0},{8,12},{12,8},{16,20},{20,16},{24,28},{28,24},{1,5},{5... | collective-permute-start | bytes 1179656 | tf_op jit(solution)/shard_map/ppermute | solution.py:345
  28.3 5.2 %collective-permute-start.12 = (bf16[128,384]{1,0:T(8,128)(2,1)S(1)}, bf16[128,384]{1,0:T(8,128)(2,1)S(1)}, u32[]{:S(2)}, u32[]{:S(2)}) collective-permute-start(bf16[128,384]{1,0:T(8,128)(2,1)S(1)} %get-tuple-element.86), channel_id=1, source_target_pairs={{0,8},{4,12},{8,0},{12,4},{16,24},{20,28},{24,16},{28,20},{1,9},{5... | collective-permute-start | bytes 294920 | tf_op jit(solution)/shard_map/ppermute | solution.py:339
  29.9 7.0 %collective-permute-start.13 = (bf16[128,384]{1,0:T(8,128)(2,1)S(1)}, bf16[128,384]{1,0:T(8,128)(2,1)S(1)}, u32[]{:S(2)}, u32[]{:S(2)}) collective-permute-start(bf16[128,384]{1,0:T(8,128)(2,1)S(1)} %get-tuple-element.87), channel_id=1, source_target_pairs={{0,16},{4,20},{8,24},{12,28},{16,0},{20,4},{24,8},{28,12},{1,17},{... | collective-permute-start | bytes 294920 | tf_op jit(solution)/shard_map/ppermute | solution.py:339
  30.4 6.5 %collective-permute-start.14 = (bf16[128,384]{1,0:T(8,128)(2,1)S(1)}, bf16[128,384]{1,0:T(8,128)(2,1)S(1)}, u32[]{:S(2)}, u32[]{:S(2)}) collective-permute-start(bf16[128,384]{1,0:T(8,128)(2,1)S(1)} %get-tuple-element.88), channel_id=1, source_target_pairs={{0,24},{4,28},{8,16},{12,20},{16,8},{20,12},{24,0},{28,4},{1,25},{... | collective-permute-start | bytes 294920 | tf_op jit(solution)/shard_map/ppermute | solution.py:339

commit v4 on v2

--- a/solution.py
+++ b/solution.py
@@ -52,8 +52,12 @@
     for t in range(groups):
         cols = columns(partner(group, t, groups), width)
         for i, src in enumerate(new_refs):
-            dst = pieces[t].at[pl.ds(i * rows, rows)]
-            copies.append(pltpu.make_async_copy(src.at[:, cols], dst, new_sems.at[t, i]))
+            for j in range(2):
+                part = pl.ds(j * (rows // 2), rows // 2)
+                dst = pieces[t].at[pl.ds(i * rows + j * (rows // 2), rows // 2)]
+                copies.append(
+                    pltpu.make_async_copy(src.at[part, cols], dst, new_sems.at[t, i, j])
+                )
     for copy in loads + copies:
         copy.start()
     for copy in loads:
@@ -96,7 +100,7 @@
         in_specs=[pl.BlockSpec(memory_space=pltpu.HBM)] * len(operands),
         out_specs=vmem(groups + shards),
         scratch_shapes=[pltpu.VMEM(x.shape, x.dtype) for x in (ck, cv, ke, ve)]
-        + [pltpu.SemaphoreType.DMA((4,)), pltpu.SemaphoreType.DMA((groups, 3))],
+        + [pltpu.SemaphoreType.DMA((4,)), pltpu.SemaphoreType.DMA((groups, 3, 2))],
         compiler_params=pltpu.CompilerParams(vmem_limit_bytes=SMALL),
         cost_estimate=pl.CostEstimate(
             flops=4 * ck.size, bytes_accessed=12 * q.size + 8 * ck.size, transcendentals=0
@@ -161,25 +165,30 @@
     return parts[0] if len(parts) == 1 else jnp.concatenate(parts, axis=0)
 
 
-def attend_sets(queries, sets):
+def scores_of(queries, sets, cols):
     scale = math.log2(math.e) / math.sqrt(DH)
     scores = []
-    for keys, _, bias in sets:
+    for refs, half, bias in sets:
         x = lax.dot_general(
-            queries, keys, (((1,), (1,)), ((), ())), preferred_element_type=jnp.float32
+            queries,
+            rows_of(refs, 0, half, cols),
+            (((1,), (1,)), ((), ())),
+            preferred_element_type=jnp.float32,
         )
         scores.append(x * scale if bias is None else x * scale + bias)
+    return scores
+
+
+def weigh(scores):
     peak = functools.reduce(
         jnp.maximum, [jnp.max(x, axis=1, keepdims=True) for x in scores]
     )
-    total, product = 0.0, 0.0
-    for x, (_, values, _) in zip(scores, sets):
+    total, weights = 0.0, []
+    for x in scores:
         raised = jnp.exp2(x - peak)
         total += jnp.sum(raised, axis=1, keepdims=True)
-        product += jnp.dot(
-            raised.astype(jnp.bfloat16), values, preferred_element_type=jnp.float32
-        )
-    return peak, total, product
+        weights.append(raised.astype(jnp.bfloat16))
+    return peak, total, weights
 
 
 def bias_rows(bias_ref, pieces, blocks):
@@ -203,16 +212,17 @@
         refs = refs[count + masked :]
     state, refs = (refs[:3], refs[3:]) if merge else (None, refs)
     width = q_refs[0].shape[1]
-    for at in range(0, width, DH):
-        cols = slice(at, at + DH)
-        queries = rows_of(q_refs, q_start, rows, cols)
-        peak, total, product = attend_sets(
-            queries,
-            [
-                (rows_of(k_refs, 0, half, cols), rows_of(k_refs, half, half, cols), bias)
-                for k_refs, half, bias in sets
-            ],
-        )
+    heads = [slice(at, at + DH) for at in range(0, width, DH)]
+    scores = [
+        scores_of(rows_of(q_refs, q_start, rows, cols), sets, cols) for cols in heads
+    ]
+    weighed = [weigh(x) for x in scores]
+    for cols, (peak, total, weights) in zip(heads, weighed):
+        product = 0.0
+        for x, (refs_of, half, _) in zip(weights, sets):
+            product += jnp.dot(
+                x, rows_of(refs_of, half, half, cols), preferred_element_type=jnp.float32
+            )
         if merge:
             peak_1, total_1, product_1 = [ref[:, cols] for ref in state]
             top = jnp.maximum(peak, peak_1)

time: 37.6 us -> 37.7 us (level)
  waiting for transfers between devices: 6.62 us -> 7.06 us
    pallas_call x4, Pallas kernels: 5.06 us -> 4.61 us  [attend(): pl.pallas_call(functools.partial(attend_kernel, tuple(pieces), tuple(((le...]
    ppermute x3, waiting for transfers between devices: 3.25 us -> 3.63 us  [from_group(): return lax.ppermute(x, 'seq', pairs)]
  transfers between devices with their start and end apart: 15 -> 15, of which waited for: 5 -> 5; matrix products, arithmetic and copies ran while one was open for 3% -> 3% of each run, Pallas kernels for 12% -> 10%
where the time goes in v4:
time: 37.7 us; the launch traced here: 37.5 us
  starting transfers between devices  21 us (56%)
  Pallas kernels  7.51 us (20%)
  waiting for transfers between devices  7.06 us (19%)
  local copies, waits for them, and re-layouts  0.97 us (3%)
  matrix products  0.44 us (1%)
    ppermute x6, starting transfers between devices, to_group(): return lax.ppermute(x, 'seq', pairs)  9.13 us
    ppermute x3, starting transfers between devices, to_head(): lax.ppermute(x, 'head', [(h, partner(h, t, head_count)) for h in range(he...  7.66 us
    pallas_call x4, Pallas kernels, attend(): pl.pallas_call(functools.partial(attend_kernel, tuple(pieces), tuple(((le...  4.61 us
    ppermute x3, waiting for transfers between devices, from_group(): return lax.ppermute(x, 'seq', pairs)  3.63 us
    ppermute x3, starting transfers between devices, from_group(): return lax.ppermute(x, 'seq', pairs)  3.55 us
    ppermute x3, waiting for transfers between devices, to_head(): lax.ppermute(x, 'head', [(h, partner(h, t, head_count)) for h in range(he...  3.14 us
    pallas_call x1, Pallas kernels, prepare(): pl.pallas_call(functools.partial(prepare_kernel, groups, gather, shards),...  1.99 us
    pallas_call x1, Pallas kernels, unpack(): pl.pallas_call(functools.partial(unpack_kernel, tuple(steps), gather, wid...  0.77 us
  transfers between devices with their start and end apart: 15, of which 5 were waited for; matrix products, arithmetic and copies ran while one was open for 3% of the time, Pallas kernels for 10%

profile of v4, /device:TPU:0, one launch (start us, length us, event | category | flops | bytes accessed | tf_op | source)
XLA Modules:
  0.0 37.5 jit_solution(187603900018397206)
XLA Ops:
  0.0 2.0 %prepare.1 = (bf16[384,384]{1,0:T(8,128)(2,1)S(1)}, bf16[384,384]{1,0:T(8,128)(2,1)S(1)}, bf16[384,384]{1,0:T(8,128)(2,1)S(1)}, bf16[384,384]{1,0:T(8,128)(2,1)S...) custom-call(bf16[128,1536]{1,0:T(8,128)(2,1)} %refs_0_.1, ...), custom_call_target="tpu_custom_call" | custom-call | flops 393216 | bytes 3145728 | tf_op jit(solution)/shard_map/prepare/pallas_call | solution.py:96
  2.0 0.5 %collective-permute-start.1 = (bf16[256,384]{1,0:T(8,128)(2,1)S(1)}, bf16[256,384]{1,0:T(8,128)(2,1)S(1)}, u32[]{:S(2)}, u32[]{:S(2)}) collective-permute-start(bf16[256,384]{1,0:T(8,128)(2,1)S(1)} %slice.51), channel_id=1, source_target_pairs={{0,4},{4,0},{8,12},{12,8},{16,20},{20,16},{24,28},{28,24},{1,5},{5... | collective-permute-start | bytes 589832 | tf_op jit(solution)/shard_map/ppermute | solution.py:355
  2.5 3.5 %collective-permute-start = (bf16[384,384]{1,0:T(8,128)(2,1)S(1)}, bf16[384,384]{1,0:T(8,128)(2,1)S(1)}, u32[]{:S(2)}, u32[]{:S(2)}) collective-permute-start(bf16[384,384]{1,0:T(8,128)(2,1)S(1)} %get-tuple-element.47), channel_id=1, source_target_pairs={{0,24},{4,28},{8,16},{12,20},{16,8},{20,12},{24,0},{28,4},{1,25},{... | collective-permute-start | bytes 884744 | tf_op jit(solution)/shard_map/ppermute | solution.py:341
  6.1 1.6 %collective-permute-start.2 = (bf16[4,2,16,384]{3,2,1,0:T(8,128)(2,1)S(1)}, bf16[4,2,16,384]{3,2,1,0:T(8,128)(2,1)S(1)}, u32[]{:S(2)}, u32[]{:S(2)}) collective-permute-start(bf16[4,2,16,384]{3,2,1,0:T(8,128)(2,1)S(1)} %get-tuple-element.57), channel_id=1, source_target_pairs={{0,1},{1,0},{2,3},{3,2},{4,5},{5,4},{6,7},{7,6},{8,9},{9,8},{10,11... | collective-permute-start | bytes 294920 | tf_op jit(solution)/shard_map/ppermute | solution.py:360
  7.7 2.7 %collective-permute-start.3 = (bf16[4,2,16,384]{3,2,1,0:T(8,128)(2,1)S(1)}, bf16[4,2,16,384]{3,2,1,0:T(8,128)(2,1)S(1)}, u32[]{:S(2)}, u32[]{:S(2)}) collective-permute-start(bf16[4,2,16,384]{3,2,1,0:T(8,128)(2,1)S(1)} %get-tuple-element.59), channel_id=1, source_target_pairs={{0,2},{1,3},{2,0},{3,1},{4,6},{5,7},{6,4},{7,5},{8,10},{9,11},{10,... | collective-permute-start | bytes 294920 | tf_op jit(solution)/shard_map/ppermute | solution.py:360
  10.3 0.5 %collective-permute-start.5 = (bf16[384,384]{1,0:T(8,128)(2,1)S(1)}, bf16[384,384]{1,0:T(8,128)(2,1)S(1)}, u32[]{:S(2)}, u32[]{:S(2)}) collective-permute-start(bf16[384,384]{1,0:T(8,128)(2,1)S(1)} %get-tuple-element.62), channel_id=1, source_target_pairs={{0,8},{4,12},{8,0},{12,4},{16,24},{20,28},{24,16},{28,20},{1,9},{5... | collective-permute-start | bytes 884744 | tf_op jit(solution)/shard_map/ppermute | solution.py:341
  10.9 1.4 %collective-permute-start.6 = (bf16[384,384]{1,0:T(8,128)(2,1)S(1)}, bf16[384,384]{1,0:T(8,128)(2,1)S(1)}, u32[]{:S(2)}, u32[]{:S(2)}) collective-permute-start(bf16[384,384]{1,0:T(8,128)(2,1)S(1)} %get-tuple-element.64), channel_id=1, source_target_pairs={{0,16},{4,20},{8,24},{12,28},{16,0},{20,4},{24,8},{28,12},{1,17},{... | collective-permute-start | bytes 884744 | tf_op jit(solution)/shard_map/ppermute | solution.py:341
  12.3 3.4 %collective-permute-start.4 = (bf16[4,2,16,384]{3,2,1,0:T(8,128)(2,1)S(1)}, bf16[4,2,16,384]{3,2,1,0:T(8,128)(2,1)S(1)}, u32[]{:S(2)}, u32[]{:S(2)}) collective-permute-start(bf16[4,2,16,384]{3,2,1,0:T(8,128)(2,1)S(1)} %get-tuple-element.60), channel_id=1, source_target_pairs={{0,3},{1,2},{2,1},{3,0},{4,7},{5,6},{6,5},{7,4},{8,11},{9,10},{10,... | collective-permute-start | bytes 294920 | tf_op jit(solution)/shard_map/ppermute | solution.py:360
  15.7 3.1 %collective-permute-done.4 = bf16[4,2,16,384]{3,2,1,0:T(8,128)(2,1)S(1)} collective-permute-done((bf16[4,2,16,384]{3,2,1,0:T(8,128)(2,1)S(1)}, bf16[4,2,16,384]{3,2,1,0:T(8,128)(2,1)S(1)}, u32[]{:S(2)}, u32[]{:S(2)}) %collective-permute-start.4) | collective-permute-done | bytes 98336 | tf_op jit(solution)/shard_map/ppermute | solution.py:360
  18.9 1.6 %collective-permute-start.7 = (bf16[128,384]{1,0:T(8,128)(2,1)S(1)}, bf16[128,384]{1,0:T(8,128)(2,1)S(1)}, u32[]{:S(2)}, u32[]{:S(2)}) collective-permute-start(bf16[128,384]{1,0:T(8,128)(2,1)S(1)} %interleave.4), channel_id=1, source_target_pairs={{0,24},{4,28},{8,16},{12,20},{16,8},{20,12},{24,0},{28,4},{1,25},{... | collective-permute-start | bytes 294920 | tf_op jit(solution)/shard_map/ppermute | solution.py:341
  20.5 0.6 %collective-permute-start.8 = (bf16[128,384]{1,0:T(8,128)(2,1)S(1)}, bf16[128,384]{1,0:T(8,128)(2,1)S(1)}, u32[]{:S(2)}, u32[]{:S(2)}) collective-permute-start(bf16[128,384]{1,0:T(8,128)(2,1)S(1)} %interleave.5), channel_id=1, source_target_pairs={{0,8},{4,12},{8,0},{12,4},{16,24},{20,28},{24,16},{28,20},{1,9},{5... | collective-permute-start | bytes 294920 | tf_op jit(solution)/shard_map/ppermute | solution.py:341
  21.2 1.4 %collective-permute-start.9 = (bf16[128,384]{1,0:T(8,128)(2,1)S(1)}, bf16[128,384]{1,0:T(8,128)(2,1)S(1)}, u32[]{:S(2)}, u32[]{:S(2)}) collective-permute-start(bf16[128,384]{1,0:T(8,128)(2,1)S(1)} %interleave.6), channel_id=1, source_target_pairs={{0,16},{4,20},{8,24},{12,28},{16,0},{20,4},{24,8},{28,12},{1,17},{... | collective-permute-start | bytes 294920 | tf_op jit(solution)/shard_map/ppermute | solution.py:341
  22.7 0.1 stack.155
  22.8 0.1 stack.138
  23.1 0.1 add.233
  23.3 0.1 add.253
  23.5 0.1 add.277
  23.6 0.4 %copy-done = s32[16,16]{1,0:T(8,128)S(1)} copy-done((s32[16,16]{1,0:T(8,128)S(1)}, s32[16,16]{1,0:T(8,128)}, u32[]{:S(2)}) %copy-start) | copy-done | bytes 1048
  24.1 0.2 fusion.4
  24.3 0.1 fusion.1.refs_7_.refs_9_
  24.4 0.1 fusion.refs_4_.refs_13_
  24.5 1.1 %attend.4 = (f32[384,384]{1,0:T(8,128)S(1)}, f32[384,384]{1,0:T(8,128)S(1)}, f32[384,384]{1,0:T(8,128)S(1)}) custom-call(bf16[384,384]{1,0:T(8,128)(2,1)S(1)} %collective-permute-done.refs_0_.refs_6_.refs_2_.refs_4_, bf16[384,384]{1,0:T(8,128)(2,1)S(1)} %collective-permute-done.5.refs_1_.refs_4_.refs_0_.refs_2_, ...), custom_call_target="tpu_custom_call" | custom-call | flops 301989888 | bytes 786432 | tf_op jit(solution)/shard_map/attend/pallas_call | solution.py:258
  25.6 0.2 collective-permute-done.9.refs_2_.refs_5_.refs_7_
  26.0 1.6 %attend.5 = (f32[384,384]{1,0:T(8,128)S(1)}, f32[384,384]{1,0:T(8,128)S(1)}, f32[384,384]{1,0:T(8,128)S(1)}) custom-call(bf16[384,384]{1,0:T(8,128)(2,1)S(1)} %collective-permute-done.refs_0_.refs_6_.refs_2_.refs_4_, bf16[384,384]{1,0:T(8,128)(2,1)S(1)} %collective-permute-done.5.refs_1_.refs_4_.refs_0_.refs_2_, ...), custom_call_target="tpu_custom_call" | custom-call | flops 452984832 | bytes 1179648 | tf_op jit(solution)/shard_map/attend/pallas_call | solution.py:258
  27.7 0.9 %attend.6 = (bf16[128,384]{1,0:T(8,128)(2,1)S(1)}, bf16[128,384]{1,0:T(8,128)(2,1)S(1)}, bf16[128,384]{1,0:T(8,128)(2,1)S(1)}) custom-call(bf16[384,384]{1,0:T(8,128)(2,1)S(1)} %collective-permute-done.refs_0_.refs_6_.refs_2_.refs_4_, bf16[384,384]{1,0:T(8,128)(2,1)S(1)} %collective-permute-done.5.refs_1_.refs_4_.refs_0_.refs_2_, ...), custom_call_target="tpu_custom_call" | custom-call | flops 150994944 | bytes 393216 | tf_op jit(solution)/shard_map/attend/pallas_call | solution.py:258
  28.5 1.5 %collective-permute-start.12 = (bf16[128,384]{1,0:T(8,128)(2,1)S(1)}, bf16[128,384]{1,0:T(8,128)(2,1)S(1)}, u32[]{:S(2)}, u32[]{:S(2)}) collective-permute-start(bf16[128,384]{1,0:T(8,128)(2,1)S(1)} %get-tuple-element.86), channel_id=1, source_target_pairs={{0,24},{4,28},{8,16},{12,20},{16,8},{20,12},{24,0},{28,4},{1,25},{... | collective-permute-start | bytes 294920 | tf_op jit(solution)/shard_map/ppermute | solution.py:349
  30.0 1.4 %collective-permute-start.13 = (bf16[128,384]{1,0:T(8,128)(2,1)S(1)}, bf16[128,384]{1,0:T(8,128)(2,1)S(1)}, u32[]{:S(2)}, u32[]{:S(2)}) collective-permute-start(bf16[128,384]{1,0:T(8,128)(2,1)S(1)} %get-tuple-element.87), channel_id=1, source_target_pairs={{0,8},{4,12},{8,0},{12,4},{16,24},{20,28},{24,16},{28,20},{1,9},{5... | collective-permute-start | bytes 294920 | tf_op jit(solution)/shard_map/ppermute | solution.py:349
  31.4 0.6 %collective-permute-start.14 = (bf16[128,384]{1,0:T(8,128)(2,1)S(1)}, bf16[128,384]{1,0:T(8,128)(2,1)S(1)}, u32[]{:S(2)}, u32[]{:S(2)}) collective-permute-start(bf16[128,384]{1,0:T(8,128)(2,1)S(1)} %get-tuple-element.88), channel_id=1, source_target_pairs={{0,16},{4,20},{8,24},{12,28},{16,0},{20,4},{24,8},{28,12},{1,17},{... | collective-permute-start | bytes 294920 | tf_op jit(solution)/shard_map/ppermute | solution.py:349
  32.1 1.0 %attend.7.refs_3_ = bf16[128,384]{1,0:T(8,128)(2,1)S(1)} custom-call(bf16[384,384]{1,0:T(8,128)(2,1)S(1)} %get-tuple-element.54.refs_3_.refs_0_.refs_1_, bf16[384,384]{1,0:T(8,128)(2,1)S(1)} %get-tuple-element.54.refs_3_.refs_0_.refs_1_, bf16[384,384]{1,0:T(8,128)(2,1)S(1)} %collective-permute-done.5.refs_1_.refs_4_.refs_0_.refs_2_, ...), custom_call_target="tpu_custom_call" | custom-call | flops 301989888 | bytes 2359296 | tf_op jit(solution)/shard_map/attend/pallas_call | solution.py:258
  33.1 2.0 %collective-permute-done.12.refs_0_ = bf16[128,384]{1,0:T(8,128)(2,1)S(1)} collective-permute-done((bf16[128,384]{1,0:T(8,128)(2,1)S(1)}, bf16[128,384]{1,0:T(8,128)(2,1)S(1)}, u32[]{:S(2)}, u32[]{:S(2)}) %collective-permute-start.12) | collective-permute-done | bytes 98336 | tf_op jit(solution)/shard_map/ppermute | solution.py:349
  35.1 1.6 %collective-permute-done.13.refs_1_ = bf16[128,384]{1,0:T(8,128)(2,1)S(1)} collective-permute-done((bf16[128,384]{1,0:T(8,128)(2,1)S(1)}, bf16[128,384]{1,0:T(8,128)(2,1)S(1)}, u32[]{:S(2)}, u32[]{:S(2)}) %collective-permute-start.13) | collective-permute-done | bytes 98336 | tf_op jit(solution)/shard_map/ppermute | solution.py:349
  36.8 0.8 %unpack_heads.1 = bf16[128,1536]{1,0:T(8,128)(2,1)} custom-call(bf16[128,384]{1,0:T(8,128)(2,1)S(1)} %collective-permute-done.12.refs_0_, bf16[128,384]{1,0:T(8,128)(2,1)S(1)} %collective-permute-done.13.refs_1_, bf16[128,384]{1,0:T(8,128)(2,1)S(1)} %collective-permute-done.14.refs_2_, bf16[128,384]{1,0:T(8,128)(2,1)S(1)} %attend.7.refs_3_), custom_call_target="tpu_custom_call" | custom-call | bytes 786432 | tf_op jit(solution)/shard_map/unpack_heads/pallas_call | solution.py:300
  (33 shorter events, 0.8 us)
Async XLA Ops:
  2.0 4.0 %collective-permute-start.1 = (bf16[256,384]{1,0:T(8,128)(2,1)S(1)}, bf16[256,384]{1,0:T(8,128)(2,1)S(1)}, u32[]{:S(2)}, u32[]{:S(2)}) collective-permute-start(bf16[256,384]{1,0:T(8,128)(2,1)S(1)} %slice.51), channel_id=1, source_target_pairs={{0,4},{4,0},{8,12},{12,8},{16,20},{20,16},{24,28},{28,24},{1,5},{5... | collective-permute-start | bytes 589832 | tf_op jit(solution)/shard_map/ppermute | solution.py:355
  2.5 18.6 %collective-permute-start = (bf16[384,384]{1,0:T(8,128)(2,1)S(1)}, bf16[384,384]{1,0:T(8,128)(2,1)S(1)}, u32[]{:S(2)}, u32[]{:S(2)}) collective-permute-start(bf16[384,384]{1,0:T(8,128)(2,1)S(1)} %get-tuple-element.47), channel_id=1, source_target_pairs={{0,24},{4,28},{8,16},{12,20},{16,8},{20,12},{24,0},{28,4},{1,25},{... | collective-permute-start | bytes 884744 | tf_op jit(solution)/shard_map/ppermute | solution.py:341
  6.1 6.2 %collective-permute-start.2 = (bf16[4,2,16,384]{3,2,1,0:T(8,128)(2,1)S(1)}, bf16[4,2,16,384]{3,2,1,0:T(8,128)(2,1)S(1)}, u32[]{:S(2)}, u32[]{:S(2)}) collective-permute-start(bf16[4,2,16,384]{3,2,1,0:T(8,128)(2,1)S(1)} %get-tuple-element.57), channel_id=1, source_target_pairs={{0,1},{1,0},{2,3},{3,2},{4,5},{5,4},{6,7},{7,6},{8,9},{9,8},{10,11... | collective-permute-start | bytes 294920 | tf_op jit(solution)/shard_map/ppermute | solution.py:360
  7.7 8.0 %collective-permute-start.3 = (bf16[4,2,16,384]{3,2,1,0:T(8,128)(2,1)S(1)}, bf16[4,2,16,384]{3,2,1,0:T(8,128)(2,1)S(1)}, u32[]{:S(2)}, u32[]{:S(2)}) collective-permute-start(bf16[4,2,16,384]{3,2,1,0:T(8,128)(2,1)S(1)} %get-tuple-element.59), channel_id=1, source_target_pairs={{0,2},{1,3},{2,0},{3,1},{4,6},{5,7},{6,4},{7,5},{8,10},{9,11},{10,... | collective-permute-start | bytes 294920 | tf_op jit(solution)/shard_map/ppermute | solution.py:360
  10.3 12.3 %collective-permute-start.5 = (bf16[384,384]{1,0:T(8,128)(2,1)S(1)}, bf16[384,384]{1,0:T(8,128)(2,1)S(1)}, u32[]{:S(2)}, u32[]{:S(2)}) collective-permute-start(bf16[384,384]{1,0:T(8,128)(2,1)S(1)} %get-tuple-element.62), channel_id=1, source_target_pairs={{0,8},{4,12},{8,0},{12,4},{16,24},{20,28},{24,16},{28,20},{1,9},{5... | collective-permute-start | bytes 884744 | tf_op jit(solution)/shard_map/ppermute | solution.py:341
  10.9 11.8 %collective-permute-start.6 = (bf16[384,384]{1,0:T(8,128)(2,1)S(1)}, bf16[384,384]{1,0:T(8,128)(2,1)S(1)}, u32[]{:S(2)}, u32[]{:S(2)}) collective-permute-start(bf16[384,384]{1,0:T(8,128)(2,1)S(1)} %get-tuple-element.64), channel_id=1, source_target_pairs={{0,16},{4,20},{8,24},{12,28},{16,0},{20,4},{24,8},{28,12},{1,17},{... | collective-permute-start | bytes 884744 | tf_op jit(solution)/shard_map/ppermute | solution.py:341
  12.3 6.6 %collective-permute-start.4 = (bf16[4,2,16,384]{3,2,1,0:T(8,128)(2,1)S(1)}, bf16[4,2,16,384]{3,2,1,0:T(8,128)(2,1)S(1)}, u32[]{:S(2)}, u32[]{:S(2)}) collective-permute-start(bf16[4,2,16,384]{3,2,1,0:T(8,128)(2,1)S(1)} %get-tuple-element.60), channel_id=1, source_target_pairs={{0,3},{1,2},{2,1},{3,0},{4,7},{5,6},{6,5},{7,4},{8,11},{9,10},{10,... | collective-permute-start | bytes 294920 | tf_op jit(solution)/shard_map/ppermute | solution.py:360
  18.9 6.7 %collective-permute-start.7 = (bf16[128,384]{1,0:T(8,128)(2,1)S(1)}, bf16[128,384]{1,0:T(8,128)(2,1)S(1)}, u32[]{:S(2)}, u32[]{:S(2)}) collective-permute-start(bf16[128,384]{1,0:T(8,128)(2,1)S(1)} %interleave.4), channel_id=1, source_target_pairs={{0,24},{4,28},{8,16},{12,20},{16,8},{20,12},{24,0},{28,4},{1,25},{... | collective-permute-start | bytes 294920 | tf_op jit(solution)/shard_map/ppermute | solution.py:341
  20.5 5.1 %collective-permute-start.8 = (bf16[128,384]{1,0:T(8,128)(2,1)S(1)}, bf16[128,384]{1,0:T(8,128)(2,1)S(1)}, u32[]{:S(2)}, u32[]{:S(2)}) collective-permute-start(bf16[128,384]{1,0:T(8,128)(2,1)S(1)} %interleave.5), channel_id=1, source_target_pairs={{0,8},{4,12},{8,0},{12,4},{16,24},{20,28},{24,16},{28,20},{1,9},{5... | collective-permute-start | bytes 294920 | tf_op jit(solution)/shard_map/ppermute | solution.py:341
  21.2 4.7 %collective-permute-start.9 = (bf16[128,384]{1,0:T(8,128)(2,1)S(1)}, bf16[128,384]{1,0:T(8,128)(2,1)S(1)}, u32[]{:S(2)}, u32[]{:S(2)}) collective-permute-start(bf16[128,384]{1,0:T(8,128)(2,1)S(1)} %interleave.6), channel_id=1, source_target_pairs={{0,16},{4,20},{8,24},{12,28},{16,0},{20,4},{24,8},{28,12},{1,17},{... | collective-permute-start | bytes 294920 | tf_op jit(solution)/shard_map/ppermute | solution.py:341
  23.4 0.7 %copy-start = (s32[16,16]{1,0:T(8,128)S(1)}, s32[16,16]{1,0:T(8,128)}, u32[]{:S(2)}) copy-start(s32[16,16]{1,0:T(8,128)} %param.15) | copy-start | bytes 3076
  23.5 2.4 %collective-permute-start.11 = (bf16[3,256,384]{2,1,0:T(8,128)(2,1)S(1)}, bf16[3,256,384]{2,1,0:T(8,128)(2,1)S(1)}, u32[]{:S(2)}, u32[]{:S(2)}) collective-permute-start(bf16[3,256,384]{2,1,0:T(8,128)(2,1)S(1)} %join.3), channel_id=1, source_target_pairs={{0,4},{4,0},{8,12},{12,8},{16,20},{20,16},{24,28},{28,24},{1,5},{5... | collective-permute-start | bytes 1769480 | tf_op jit(solution)/shard_map/ppermute | solution.py:355
  25.9 1.8 %collective-permute-start.10 = (bf16[4,128,384]{2,1,0:T(8,128)(2,1)S(1)}, bf16[4,128,384]{2,1,0:T(8,128)(2,1)S(1)}, u32[]{:S(2)}, u32[]{:S(2)}) collective-permute-start(bf16[4,128,384]{2,1,0:T(8,128)(2,1)S(1)} %join.2), channel_id=1, source_target_pairs={{0,4},{4,0},{8,12},{12,8},{16,20},{20,16},{24,28},{28,24},{1,5},{5... | collective-permute-start | bytes 1179656 | tf_op jit(solution)/shard_map/ppermute | solution.py:355
  28.5 6.6 %collective-permute-start.12 = (bf16[128,384]{1,0:T(8,128)(2,1)S(1)}, bf16[128,384]{1,0:T(8,128)(2,1)S(1)}, u32[]{:S(2)}, u32[]{:S(2)}) collective-permute-start(bf16[128,384]{1,0:T(8,128)(2,1)S(1)} %get-tuple-element.86), channel_id=1, source_target_pairs={{0,24},{4,28},{8,16},{12,20},{16,8},{20,12},{24,0},{28,4},{1,25},{... | collective-permute-start | bytes 294920 | tf_op jit(solution)/shard_map/ppermute | solution.py:349
  30.0 6.6 %collective-permute-start.13 = (bf16[128,384]{1,0:T(8,128)(2,1)S(1)}, bf16[128,384]{1,0:T(8,128)(2,1)S(1)}, u32[]{:S(2)}, u32[]{:S(2)}) collective-permute-start(bf16[128,384]{1,0:T(8,128)(2,1)S(1)} %get-tuple-element.87), channel_id=1, source_target_pairs={{0,8},{4,12},{8,0},{12,4},{16,24},{20,28},{24,16},{28,20},{1,9},{5... | collective-permute-start | bytes 294920 | tf_op jit(solution)/shard_map/ppermute | solution.py:349
  31.4 5.3 %collective-permute-start.14 = (bf16[128,384]{1,0:T(8,128)(2,1)S(1)}, bf16[128,384]{1,0:T(8,128)(2,1)S(1)}, u32[]{:S(2)}, u32[]{:S(2)}) collective-permute-start(bf16[128,384]{1,0:T(8,128)(2,1)S(1)} %get-tuple-element.88), channel_id=1, source_target_pairs={{0,16},{4,20},{8,24},{12,28},{16,0},{20,4},{24,8},{28,12},{1,17},{... | collective-permute-start | bytes 294920 | tf_op jit(solution)/shard_map/ppermute | solution.py:349

commit v5 on v2

--- a/solution.py
+++ b/solution.py
@@ -38,9 +38,9 @@
 
 
 def prepare_kernel(groups, gather, shards, *refs):
-    new_refs, cache_refs, outs, scratch = refs[:3], refs[3:7], refs[7:-6], refs[-6:]
+    new_refs, cache_refs, outs, scratch = refs[:3], refs[3:7], refs[7:-7], refs[-7:]
     pieces, cached = outs[:groups], outs[groups:]
-    ck_buf, cv_buf, ke_buf, ve_buf, cache_sems, new_sems = scratch
+    ck_buf, cv_buf, ke_buf, ve_buf, new_buf, cache_sems, new_sems = scratch
     group, shard = lax.axis_index("seq") // gather, lax.axis_index("head")
 
     loads = [
@@ -49,11 +49,12 @@
     ]
     rows, width = pieces[0].shape[0] // 3, pieces[0].shape[1]
     copies = []
-    for t in range(groups):
-        cols = columns(partner(group, t, groups), width)
-        for i, src in enumerate(new_refs):
-            dst = pieces[t].at[pl.ds(i * rows, rows)]
-            copies.append(pltpu.make_async_copy(src.at[:, cols], dst, new_sems.at[t, i]))
+    for i, src in enumerate(new_refs):
+        for j in range(2):
+            part = pl.ds(j * (rows // 2), rows // 2)
+            copies.append(
+                pltpu.make_async_copy(src.at[part], new_buf.at[i, part], new_sems.at[i, j])
+            )
     for copy in loads + copies:
         copy.start()
     for copy in loads:
@@ -82,8 +83,12 @@
                 mantissa = buf[:, columns(part, width)].astype(jnp.float32)
                 scaled = mantissa * factor[which * cache_rows : (which + 1) * cache_rows]
                 cached[s][t, which] = scaled.astype(jnp.bfloat16)
-    for copy in copies:
-        copy.wait()
+    for i in range(3):
+        for copy in copies[2 * i : 2 * i + 2]:
+            copy.wait()
+        for t in range(groups):
+            cols = columns(partner(group, t, groups), width)
+            pieces[t][pl.ds(i * rows, rows)] = new_buf[i, :, cols]
 
 
 def prepare(q, k, v, ck, cv, ke, ve, groups, gather, shards):
@@ -96,7 +101,8 @@
         in_specs=[pl.BlockSpec(memory_space=pltpu.HBM)] * len(operands),
         out_specs=vmem(groups + shards),
         scratch_shapes=[pltpu.VMEM(x.shape, x.dtype) for x in (ck, cv, ke, ve)]
-        + [pltpu.SemaphoreType.DMA((4,)), pltpu.SemaphoreType.DMA((groups, 3))],
+        + [pltpu.VMEM((3, *q.shape), q.dtype)]
+        + [pltpu.SemaphoreType.DMA((4,)), pltpu.SemaphoreType.DMA((3, 2))],
         compiler_params=pltpu.CompilerParams(vmem_limit_bytes=SMALL),
         cost_estimate=pl.CostEstimate(
             flops=4 * ck.size, bytes_accessed=12 * q.size + 8 * ck.size, transcendentals=0

time: 37.6 us -> 37.5 us (level)
  no operation moved by 1% of the time
where the time goes in v5:
time: 37.5 us; the launch traced here: 37.3 us
  starting transfers between devices  21 us (56%)
  Pallas kernels  7.71 us (21%)
  waiting for transfers between devices  6.62 us (18%)
  local copies, waits for them, and re-layouts  0.97 us (3%)
  matrix products  0.44 us (1%)
    ppermute x6, starting transfers between devices, to_group(): return lax.ppermute(x, 'seq', pairs)  9.13 us
    ppermute x3, starting transfers between devices, to_head(): lax.ppermute(x, 'head', [(h, partner(h, t, head_count)) for h in range(he...  7.66 us
    pallas_call x4, Pallas kernels, attend(): pl.pallas_call(functools.partial(attend_kernel, tuple(pieces), tuple(((le...  5.06 us
    ppermute x3, starting transfers between devices, from_group(): return lax.ppermute(x, 'seq', pairs)  3.55 us
    ppermute x3, waiting for transfers between devices, from_group(): return lax.ppermute(x, 'seq', pairs)  3.25 us
    ppermute x3, waiting for transfers between devices, to_head(): lax.ppermute(x, 'head', [(h, partner(h, t, head_count)) for h in range(he...  3.15 us
    pallas_call x1, Pallas kernels, prepare(): pl.pallas_call(functools.partial(prepare_kernel, groups, gather, shards),...  1.74 us
    pallas_call x1, Pallas kernels, unpack(): pl.pallas_call(functools.partial(unpack_kernel, tuple(steps), gather, wid...  0.77 us
  transfers between devices with their start and end apart: 15, of which 5 were waited for; matrix products, arithmetic and copies ran while one was open for 3% of the time, Pallas kernels for 12%

profile of v5, /device:TPU:0, one launch (start us, length us, event | category | flops | bytes accessed | tf_op | source)
XLA Modules:
  0.0 37.3 jit_solution(5348211631636690043)
XLA Ops:
  0.0 1.7 %prepare.1 = (bf16[384,384]{1,0:T(8,128)(2,1)S(1)}, bf16[384,384]{1,0:T(8,128)(2,1)S(1)}, bf16[384,384]{1,0:T(8,128)(2,1)S(1)}, bf16[384,384]{1,0:T(8,128)(2,1)S...) custom-call(bf16[128,1536]{1,0:T(8,128)(2,1)} %refs_0_.1, ...), custom_call_target="tpu_custom_call" | custom-call | flops 393216 | bytes 3145728 | tf_op jit(solution)/shard_map/prepare/pallas_call | solution.py:97
  1.8 0.5 %collective-permute-start.1 = (bf16[256,384]{1,0:T(8,128)(2,1)S(1)}, bf16[256,384]{1,0:T(8,128)(2,1)S(1)}, u32[]{:S(2)}, u32[]{:S(2)}) collective-permute-start(bf16[256,384]{1,0:T(8,128)(2,1)S(1)} %slice.51), channel_id=1, source_target_pairs={{0,4},{4,0},{8,12},{12,8},{16,20},{20,16},{24,28},{28,24},{1,5},{5... | collective-permute-start | bytes 589832 | tf_op jit(solution)/shard_map/ppermute | solution.py:351
  2.3 3.5 %collective-permute-start = (bf16[384,384]{1,0:T(8,128)(2,1)S(1)}, bf16[384,384]{1,0:T(8,128)(2,1)S(1)}, u32[]{:S(2)}, u32[]{:S(2)}) collective-permute-start(bf16[384,384]{1,0:T(8,128)(2,1)S(1)} %get-tuple-element.47), channel_id=1, source_target_pairs={{0,24},{4,28},{8,16},{12,20},{16,8},{20,12},{24,0},{28,4},{1,25},{... | collective-permute-start | bytes 884744 | tf_op jit(solution)/shard_map/ppermute | solution.py:337
  5.8 1.6 %collective-permute-start.2 = (bf16[4,2,16,384]{3,2,1,0:T(8,128)(2,1)S(1)}, bf16[4,2,16,384]{3,2,1,0:T(8,128)(2,1)S(1)}, u32[]{:S(2)}, u32[]{:S(2)}) collective-permute-start(bf16[4,2,16,384]{3,2,1,0:T(8,128)(2,1)S(1)} %get-tuple-element.57), channel_id=1, source_target_pairs={{0,1},{1,0},{2,3},{3,2},{4,5},{5,4},{6,7},{7,6},{8,9},{9,8},{10,11... | collective-permute-start | bytes 294920 | tf_op jit(solution)/shard_map/ppermute | solution.py:356
  7.4 2.7 %collective-permute-start.3 = (bf16[4,2,16,384]{3,2,1,0:T(8,128)(2,1)S(1)}, bf16[4,2,16,384]{3,2,1,0:T(8,128)(2,1)S(1)}, u32[]{:S(2)}, u32[]{:S(2)}) collective-permute-start(bf16[4,2,16,384]{3,2,1,0:T(8,128)(2,1)S(1)} %get-tuple-element.59), channel_id=1, source_target_pairs={{0,2},{1,3},{2,0},{3,1},{4,6},{5,7},{6,4},{7,5},{8,10},{9,11},{10,... | collective-permute-start | bytes 294920 | tf_op jit(solution)/shard_map/ppermute | solution.py:356
  10.1 0.5 %collective-permute-start.5 = (bf16[384,384]{1,0:T(8,128)(2,1)S(1)}, bf16[384,384]{1,0:T(8,128)(2,1)S(1)}, u32[]{:S(2)}, u32[]{:S(2)}) collective-permute-start(bf16[384,384]{1,0:T(8,128)(2,1)S(1)} %get-tuple-element.62), channel_id=1, source_target_pairs={{0,8},{4,12},{8,0},{12,4},{16,24},{20,28},{24,16},{28,20},{1,9},{5... | collective-permute-start | bytes 884744 | tf_op jit(solution)/shard_map/ppermute | solution.py:337
  10.6 1.4 %collective-permute-start.6 = (bf16[384,384]{1,0:T(8,128)(2,1)S(1)}, bf16[384,384]{1,0:T(8,128)(2,1)S(1)}, u32[]{:S(2)}, u32[]{:S(2)}) collective-permute-start(bf16[384,384]{1,0:T(8,128)(2,1)S(1)} %get-tuple-element.64), channel_id=1, source_target_pairs={{0,16},{4,20},{8,24},{12,28},{16,0},{20,4},{24,8},{28,12},{1,17},{... | collective-permute-start | bytes 884744 | tf_op jit(solution)/shard_map/ppermute | solution.py:337
  12.0 3.4 %collective-permute-start.4 = (bf16[4,2,16,384]{3,2,1,0:T(8,128)(2,1)S(1)}, bf16[4,2,16,384]{3,2,1,0:T(8,128)(2,1)S(1)}, u32[]{:S(2)}, u32[]{:S(2)}) collective-permute-start(bf16[4,2,16,384]{3,2,1,0:T(8,128)(2,1)S(1)} %get-tuple-element.60), channel_id=1, source_target_pairs={{0,3},{1,2},{2,1},{3,0},{4,7},{5,6},{6,5},{7,4},{8,11},{9,10},{10,... | collective-permute-start | bytes 294920 | tf_op jit(solution)/shard_map/ppermute | solution.py:356
  15.5 3.1 %collective-permute-done.4 = bf16[4,2,16,384]{3,2,1,0:T(8,128)(2,1)S(1)} collective-permute-done((bf16[4,2,16,384]{3,2,1,0:T(8,128)(2,1)S(1)}, bf16[4,2,16,384]{3,2,1,0:T(8,128)(2,1)S(1)}, u32[]{:S(2)}, u32[]{:S(2)}) %collective-permute-start.4) | collective-permute-done | bytes 98336 | tf_op jit(solution)/shard_map/ppermute | solution.py:356
  18.6 1.6 %collective-permute-start.7 = (bf16[128,384]{1,0:T(8,128)(2,1)S(1)}, bf16[128,384]{1,0:T(8,128)(2,1)S(1)}, u32[]{:S(2)}, u32[]{:S(2)}) collective-permute-start(bf16[128,384]{1,0:T(8,128)(2,1)S(1)} %interleave.4), channel_id=1, source_target_pairs={{0,24},{4,28},{8,16},{12,20},{16,8},{20,12},{24,0},{28,4},{1,25},{... | collective-permute-start | bytes 294920 | tf_op jit(solution)/shard_map/ppermute | solution.py:337
  20.3 0.6 %collective-permute-start.8 = (bf16[128,384]{1,0:T(8,128)(2,1)S(1)}, bf16[128,384]{1,0:T(8,128)(2,1)S(1)}, u32[]{:S(2)}, u32[]{:S(2)}) collective-permute-start(bf16[128,384]{1,0:T(8,128)(2,1)S(1)} %interleave.5), channel_id=1, source_target_pairs={{0,8},{4,12},{8,0},{12,4},{16,24},{20,28},{24,16},{28,20},{1,9},{5... | collective-permute-start | bytes 294920 | tf_op jit(solution)/shard_map/ppermute | solution.py:337
  20.9 1.5 %collective-permute-start.9 = (bf16[128,384]{1,0:T(8,128)(2,1)S(1)}, bf16[128,384]{1,0:T(8,128)(2,1)S(1)}, u32[]{:S(2)}, u32[]{:S(2)}) collective-permute-start(bf16[128,384]{1,0:T(8,128)(2,1)S(1)} %interleave.6), channel_id=1, source_target_pairs={{0,16},{4,20},{8,24},{12,28},{16,0},{20,4},{24,8},{28,12},{1,17},{... | collective-permute-start | bytes 294920 | tf_op jit(solution)/shard_map/ppermute | solution.py:337
  22.5 0.1 stack.155
  22.6 0.1 stack.138
  22.9 0.1 add.233
  23.0 0.1 add.253
  23.2 0.1 add.277
  23.4 0.4 %copy-done = s32[16,16]{1,0:T(8,128)S(1)} copy-done((s32[16,16]{1,0:T(8,128)S(1)}, s32[16,16]{1,0:T(8,128)}, u32[]{:S(2)}) %copy-start) | copy-done | bytes 1048
  23.8 0.2 fusion.4
  24.0 0.1 fusion.1.refs_7_.refs_9_
  24.1 0.1 fusion.refs_4_.refs_13_
  24.3 1.1 %attend.4 = (f32[384,384]{1,0:T(8,128)S(1)}, f32[384,384]{1,0:T(8,128)S(1)}, f32[384,384]{1,0:T(8,128)S(1)}) custom-call(bf16[384,384]{1,0:T(8,128)(2,1)S(1)} %collective-permute-done.refs_0_.refs_6_.refs_2_.refs_4_, bf16[384,384]{1,0:T(8,128)(2,1)S(1)} %collective-permute-done.5.refs_1_.refs_4_.refs_0_.refs_2_, ...), custom_call_target="tpu_custom_call" | custom-call | flops 301989888 | bytes 786432 | tf_op jit(solution)/shard_map/attend/pallas_call | solution.py:254
  25.4 0.2 collective-permute-done.9.refs_2_.refs_5_.refs_7_
  25.7 1.7 %attend.5 = (f32[384,384]{1,0:T(8,128)S(1)}, f32[384,384]{1,0:T(8,128)S(1)}, f32[384,384]{1,0:T(8,128)S(1)}) custom-call(bf16[384,384]{1,0:T(8,128)(2,1)S(1)} %collective-permute-done.refs_0_.refs_6_.refs_2_.refs_4_, bf16[384,384]{1,0:T(8,128)(2,1)S(1)} %collective-permute-done.5.refs_1_.refs_4_.refs_0_.refs_2_, ...), custom_call_target="tpu_custom_call" | custom-call | flops 452984832 | bytes 1179648 | tf_op jit(solution)/shard_map/attend/pallas_call | solution.py:254
  27.4 0.8 %attend.6 = (bf16[128,384]{1,0:T(8,128)(2,1)S(1)}, bf16[128,384]{1,0:T(8,128)(2,1)S(1)}, bf16[128,384]{1,0:T(8,128)(2,1)S(1)}) custom-call(bf16[384,384]{1,0:T(8,128)(2,1)S(1)} %collective-permute-done.refs_0_.refs_6_.refs_2_.refs_4_, bf16[384,384]{1,0:T(8,128)(2,1)S(1)} %collective-permute-done.5.refs_1_.refs_4_.refs_0_.refs_2_, ...), custom_call_target="tpu_custom_call" | custom-call | flops 150994944 | bytes 393216 | tf_op jit(solution)/shard_map/attend/pallas_call | solution.py:254
  28.3 1.5 %collective-permute-start.12 = (bf16[128,384]{1,0:T(8,128)(2,1)S(1)}, bf16[128,384]{1,0:T(8,128)(2,1)S(1)}, u32[]{:S(2)}, u32[]{:S(2)}) collective-permute-start(bf16[128,384]{1,0:T(8,128)(2,1)S(1)} %get-tuple-element.86), channel_id=1, source_target_pairs={{0,24},{4,28},{8,16},{12,20},{16,8},{20,12},{24,0},{28,4},{1,25},{... | collective-permute-start | bytes 294920 | tf_op jit(solution)/shard_map/ppermute | solution.py:345
  29.8 1.4 %collective-permute-start.13 = (bf16[128,384]{1,0:T(8,128)(2,1)S(1)}, bf16[128,384]{1,0:T(8,128)(2,1)S(1)}, u32[]{:S(2)}, u32[]{:S(2)}) collective-permute-start(bf16[128,384]{1,0:T(8,128)(2,1)S(1)} %get-tuple-element.87), channel_id=1, source_target_pairs={{0,8},{4,12},{8,0},{12,4},{16,24},{20,28},{24,16},{28,20},{1,9},{5... | collective-permute-start | bytes 294920 | tf_op jit(solution)/shard_map/ppermute | solution.py:345
  31.2 0.6 %collective-permute-start.14 = (bf16[128,384]{1,0:T(8,128)(2,1)S(1)}, bf16[128,384]{1,0:T(8,128)(2,1)S(1)}, u32[]{:S(2)}, u32[]{:S(2)}) collective-permute-start(bf16[128,384]{1,0:T(8,128)(2,1)S(1)} %get-tuple-element.88), channel_id=1, source_target_pairs={{0,16},{4,20},{8,24},{12,28},{16,0},{20,4},{24,8},{28,12},{1,17},{... | collective-permute-start | bytes 294920 | tf_op jit(solution)/shard_map/ppermute | solution.py:345
  31.8 1.4 %attend.7.refs_3_ = bf16[128,384]{1,0:T(8,128)(2,1)S(1)} custom-call(bf16[384,384]{1,0:T(8,128)(2,1)S(1)} %get-tuple-element.54.refs_3_.refs_0_.refs_1_, bf16[384,384]{1,0:T(8,128)(2,1)S(1)} %get-tuple-element.54.refs_3_.refs_0_.refs_1_, bf16[384,384]{1,0:T(8,128)(2,1)S(1)} %collective-permute-done.5.refs_1_.refs_4_.refs_0_.refs_2_, ...), custom_call_target="tpu_custom_call" | custom-call | flops 301989888 | bytes 2359296 | tf_op jit(solution)/shard_map/attend/pallas_call | solution.py:254
  33.3 1.6 %collective-permute-done.12.refs_0_ = bf16[128,384]{1,0:T(8,128)(2,1)S(1)} collective-permute-done((bf16[128,384]{1,0:T(8,128)(2,1)S(1)}, bf16[128,384]{1,0:T(8,128)(2,1)S(1)}, u32[]{:S(2)}, u32[]{:S(2)}) %collective-permute-start.12) | collective-permute-done | bytes 98336 | tf_op jit(solution)/shard_map/ppermute | solution.py:345
  34.8 1.6 %collective-permute-done.13.refs_1_ = bf16[128,384]{1,0:T(8,128)(2,1)S(1)} collective-permute-done((bf16[128,384]{1,0:T(8,128)(2,1)S(1)}, bf16[128,384]{1,0:T(8,128)(2,1)S(1)}, u32[]{:S(2)}, u32[]{:S(2)}) %collective-permute-start.13) | collective-permute-done | bytes 98336 | tf_op jit(solution)/shard_map/ppermute | solution.py:345
  36.5 0.8 %unpack_heads.1 = bf16[128,1536]{1,0:T(8,128)(2,1)} custom-call(bf16[128,384]{1,0:T(8,128)(2,1)S(1)} %collective-permute-done.12.refs_0_, bf16[128,384]{1,0:T(8,128)(2,1)S(1)} %collective-permute-done.13.refs_1_, bf16[128,384]{1,0:T(8,128)(2,1)S(1)} %collective-permute-done.14.refs_2_, bf16[128,384]{1,0:T(8,128)(2,1)S(1)} %attend.7.refs_3_), custom_call_target="tpu_custom_call" | custom-call | bytes 786432 | tf_op jit(solution)/shard_map/unpack_heads/pallas_call | solution.py:296
  (33 shorter events, 0.8 us)
Async XLA Ops:
  1.8 4.0 %collective-permute-start.1 = (bf16[256,384]{1,0:T(8,128)(2,1)S(1)}, bf16[256,384]{1,0:T(8,128)(2,1)S(1)}, u32[]{:S(2)}, u32[]{:S(2)}) collective-permute-start(bf16[256,384]{1,0:T(8,128)(2,1)S(1)} %slice.51), channel_id=1, source_target_pairs={{0,4},{4,0},{8,12},{12,8},{16,20},{20,16},{24,28},{28,24},{1,5},{5... | collective-permute-start | bytes 589832 | tf_op jit(solution)/shard_map/ppermute | solution.py:351
  2.3 18.6 %collective-permute-start = (bf16[384,384]{1,0:T(8,128)(2,1)S(1)}, bf16[384,384]{1,0:T(8,128)(2,1)S(1)}, u32[]{:S(2)}, u32[]{:S(2)}) collective-permute-start(bf16[384,384]{1,0:T(8,128)(2,1)S(1)} %get-tuple-element.47), channel_id=1, source_target_pairs={{0,24},{4,28},{8,16},{12,20},{16,8},{20,12},{24,0},{28,4},{1,25},{... | collective-permute-start | bytes 884744 | tf_op jit(solution)/shard_map/ppermute | solution.py:337
  5.8 6.2 %collective-permute-start.2 = (bf16[4,2,16,384]{3,2,1,0:T(8,128)(2,1)S(1)}, bf16[4,2,16,384]{3,2,1,0:T(8,128)(2,1)S(1)}, u32[]{:S(2)}, u32[]{:S(2)}) collective-permute-start(bf16[4,2,16,384]{3,2,1,0:T(8,128)(2,1)S(1)} %get-tuple-element.57), channel_id=1, source_target_pairs={{0,1},{1,0},{2,3},{3,2},{4,5},{5,4},{6,7},{7,6},{8,9},{9,8},{10,11... | collective-permute-start | bytes 294920 | tf_op jit(solution)/shard_map/ppermute | solution.py:356
  7.4 8.0 %collective-permute-start.3 = (bf16[4,2,16,384]{3,2,1,0:T(8,128)(2,1)S(1)}, bf16[4,2,16,384]{3,2,1,0:T(8,128)(2,1)S(1)}, u32[]{:S(2)}, u32[]{:S(2)}) collective-permute-start(bf16[4,2,16,384]{3,2,1,0:T(8,128)(2,1)S(1)} %get-tuple-element.59), channel_id=1, source_target_pairs={{0,2},{1,3},{2,0},{3,1},{4,6},{5,7},{6,4},{7,5},{8,10},{9,11},{10,... | collective-permute-start | bytes 294920 | tf_op jit(solution)/shard_map/ppermute | solution.py:356
  10.1 12.3 %collective-permute-start.5 = (bf16[384,384]{1,0:T(8,128)(2,1)S(1)}, bf16[384,384]{1,0:T(8,128)(2,1)S(1)}, u32[]{:S(2)}, u32[]{:S(2)}) collective-permute-start(bf16[384,384]{1,0:T(8,128)(2,1)S(1)} %get-tuple-element.62), channel_id=1, source_target_pairs={{0,8},{4,12},{8,0},{12,4},{16,24},{20,28},{24,16},{28,20},{1,9},{5... | collective-permute-start | bytes 884744 | tf_op jit(solution)/shard_map/ppermute | solution.py:337
  10.6 11.8 %collective-permute-start.6 = (bf16[384,384]{1,0:T(8,128)(2,1)S(1)}, bf16[384,384]{1,0:T(8,128)(2,1)S(1)}, u32[]{:S(2)}, u32[]{:S(2)}) collective-permute-start(bf16[384,384]{1,0:T(8,128)(2,1)S(1)} %get-tuple-element.64), channel_id=1, source_target_pairs={{0,16},{4,20},{8,24},{12,28},{16,0},{20,4},{24,8},{28,12},{1,17},{... | collective-permute-start | bytes 884744 | tf_op jit(solution)/shard_map/ppermute | solution.py:337
  12.0 6.6 %collective-permute-start.4 = (bf16[4,2,16,384]{3,2,1,0:T(8,128)(2,1)S(1)}, bf16[4,2,16,384]{3,2,1,0:T(8,128)(2,1)S(1)}, u32[]{:S(2)}, u32[]{:S(2)}) collective-permute-start(bf16[4,2,16,384]{3,2,1,0:T(8,128)(2,1)S(1)} %get-tuple-element.60), channel_id=1, source_target_pairs={{0,3},{1,2},{2,1},{3,0},{4,7},{5,6},{6,5},{7,4},{8,11},{9,10},{10,... | collective-permute-start | bytes 294920 | tf_op jit(solution)/shard_map/ppermute | solution.py:356
  18.6 6.7 %collective-permute-start.7 = (bf16[128,384]{1,0:T(8,128)(2,1)S(1)}, bf16[128,384]{1,0:T(8,128)(2,1)S(1)}, u32[]{:S(2)}, u32[]{:S(2)}) collective-permute-start(bf16[128,384]{1,0:T(8,128)(2,1)S(1)} %interleave.4), channel_id=1, source_target_pairs={{0,24},{4,28},{8,16},{12,20},{16,8},{20,12},{24,0},{28,4},{1,25},{... | collective-permute-start | bytes 294920 | tf_op jit(solution)/shard_map/ppermute | solution.py:337
  20.3 5.1 %collective-permute-start.8 = (bf16[128,384]{1,0:T(8,128)(2,1)S(1)}, bf16[128,384]{1,0:T(8,128)(2,1)S(1)}, u32[]{:S(2)}, u32[]{:S(2)}) collective-permute-start(bf16[128,384]{1,0:T(8,128)(2,1)S(1)} %interleave.5), channel_id=1, source_target_pairs={{0,8},{4,12},{8,0},{12,4},{16,24},{20,28},{24,16},{28,20},{1,9},{5... | collective-permute-start | bytes 294920 | tf_op jit(solution)/shard_map/ppermute | solution.py:337
  20.9 4.7 %collective-permute-start.9 = (bf16[128,384]{1,0:T(8,128)(2,1)S(1)}, bf16[128,384]{1,0:T(8,128)(2,1)S(1)}, u32[]{:S(2)}, u32[]{:S(2)}) collective-permute-start(bf16[128,384]{1,0:T(8,128)(2,1)S(1)} %interleave.6), channel_id=1, source_target_pairs={{0,16},{4,20},{8,24},{12,28},{16,0},{20,4},{24,8},{28,12},{1,17},{... | collective-permute-start | bytes 294920 | tf_op jit(solution)/shard_map/ppermute | solution.py:337
  23.1 0.7 %copy-start = (s32[16,16]{1,0:T(8,128)S(1)}, s32[16,16]{1,0:T(8,128)}, u32[]{:S(2)}) copy-start(s32[16,16]{1,0:T(8,128)} %param.15) | copy-start | bytes 3076
  23.3 2.4 %collective-permute-start.11 = (bf16[3,256,384]{2,1,0:T(8,128)(2,1)S(1)}, bf16[3,256,384]{2,1,0:T(8,128)(2,1)S(1)}, u32[]{:S(2)}, u32[]{:S(2)}) collective-permute-start(bf16[3,256,384]{2,1,0:T(8,128)(2,1)S(1)} %join.3), channel_id=1, source_target_pairs={{0,4},{4,0},{8,12},{12,8},{16,20},{20,16},{24,28},{28,24},{1,5},{5... | collective-permute-start | bytes 1769480 | tf_op jit(solution)/shard_map/ppermute | solution.py:351
  25.6 1.8 %collective-permute-start.10 = (bf16[4,128,384]{2,1,0:T(8,128)(2,1)S(1)}, bf16[4,128,384]{2,1,0:T(8,128)(2,1)S(1)}, u32[]{:S(2)}, u32[]{:S(2)}) collective-permute-start(bf16[4,128,384]{2,1,0:T(8,128)(2,1)S(1)} %join.2), channel_id=1, source_target_pairs={{0,4},{4,0},{8,12},{12,8},{16,20},{20,16},{24,28},{28,24},{1,5},{5... | collective-permute-start | bytes 1179656 | tf_op jit(solution)/shard_map/ppermute | solution.py:351
  28.3 6.6 %collective-permute-start.12 = (bf16[128,384]{1,0:T(8,128)(2,1)S(1)}, bf16[128,384]{1,0:T(8,128)(2,1)S(1)}, u32[]{:S(2)}, u32[]{:S(2)}) collective-permute-start(bf16[128,384]{1,0:T(8,128)(2,1)S(1)} %get-tuple-element.86), channel_id=1, source_target_pairs={{0,24},{4,28},{8,16},{12,20},{16,8},{20,12},{24,0},{28,4},{1,25},{... | collective-permute-start | bytes 294920 | tf_op jit(solution)/shard_map/ppermute | solution.py:345
  29.8 6.7 %collective-permute-start.13 = (bf16[128,384]{1,0:T(8,128)(2,1)S(1)}, bf16[128,384]{1,0:T(8,128)(2,1)S(1)}, u32[]{:S(2)}, u32[]{:S(2)}) collective-permute-start(bf16[128,384]{1,0:T(8,128)(2,1)S(1)} %get-tuple-element.87), channel_id=1, source_target_pairs={{0,8},{4,12},{8,0},{12,4},{16,24},{20,28},{24,16},{28,20},{1,9},{5... | collective-permute-start | bytes 294920 | tf_op jit(solution)/shard_map/ppermute | solution.py:345
  31.2 5.3 %collective-permute-start.14 = (bf16[128,384]{1,0:T(8,128)(2,1)S(1)}, bf16[128,384]{1,0:T(8,128)(2,1)S(1)}, u32[]{:S(2)}, u32[]{:S(2)}) collective-permute-start(bf16[128,384]{1,0:T(8,128)(2,1)S(1)} %get-tuple-element.88), channel_id=1, source_target_pairs={{0,16},{4,20},{8,24},{12,28},{16,0},{20,4},{24,8},{28,12},{1,17},{... | collective-permute-start | bytes 294920 | tf_op jit(solution)/shard_map/ppermute | solution.py:345

commit v6 on v4

--- a/solution.py
+++ b/solution.py
@@ -38,9 +38,9 @@
 
 
 def prepare_kernel(groups, gather, shards, *refs):
-    new_refs, cache_refs, outs, scratch = refs[:3], refs[3:7], refs[7:-6], refs[-6:]
+    new_refs, cache_refs, outs, scratch = refs[:3], refs[3:7], refs[7:-7], refs[-7:]
     pieces, cached = outs[:groups], outs[groups:]
-    ck_buf, cv_buf, ke_buf, ve_buf, cache_sems, new_sems = scratch
+    ck_buf, cv_buf, ke_buf, ve_buf, new_buf, cache_sems, new_sems = scratch
     group, shard = lax.axis_index("seq") // gather, lax.axis_index("head")
 
     loads = [
@@ -49,15 +49,12 @@
     ]
     rows, width = pieces[0].shape[0] // 3, pieces[0].shape[1]
     copies = []
-    for t in range(groups):
-        cols = columns(partner(group, t, groups), width)
-        for i, src in enumerate(new_refs):
-            for j in range(2):
-                part = pl.ds(j * (rows // 2), rows // 2)
-                dst = pieces[t].at[pl.ds(i * rows + j * (rows // 2), rows // 2)]
-                copies.append(
-                    pltpu.make_async_copy(src.at[part, cols], dst, new_sems.at[t, i, j])
-                )
+    for i, src in enumerate(new_refs):
+        for j in range(2):
+            part = pl.ds(j * (rows // 2), rows // 2)
+            copies.append(
+                pltpu.make_async_copy(src.at[part], new_buf.at[i, part], new_sems.at[i, j])
+            )
     for copy in loads + copies:
         copy.start()
     for copy in loads:
@@ -86,8 +83,12 @@
                 mantissa = buf[:, columns(part, width)].astype(jnp.float32)
                 scaled = mantissa * factor[which * cache_rows : (which + 1) * cache_rows]
                 cached[s][t, which] = scaled.astype(jnp.bfloat16)
-    for copy in copies:
-        copy.wait()
+    for i in range(3):
+        for copy in copies[2 * i : 2 * i + 2]:
+            copy.wait()
+        for t in range(groups):
+            cols = columns(partner(group, t, groups), width)
+            pieces[t][pl.ds(i * rows, rows)] = new_buf[i, :, cols]
 
 
 def prepare(q, k, v, ck, cv, ke, ve, groups, gather, shards):
@@ -100,7 +101,8 @@
         in_specs=[pl.BlockSpec(memory_space=pltpu.HBM)] * len(operands),
         out_specs=vmem(groups + shards),
         scratch_shapes=[pltpu.VMEM(x.shape, x.dtype) for x in (ck, cv, ke, ve)]
-        + [pltpu.SemaphoreType.DMA((4,)), pltpu.SemaphoreType.DMA((groups, 3, 2))],
+        + [pltpu.VMEM((3, *q.shape), q.dtype)]
+        + [pltpu.SemaphoreType.DMA((4,)), pltpu.SemaphoreType.DMA((3, 2))],
         compiler_params=pltpu.CompilerParams(vmem_limit_bytes=SMALL),
         cost_estimate=pl.CostEstimate(
             flops=4 * ck.size, bytes_accessed=12 * q.size + 8 * ck.size, transcendentals=0

time: 37.7 us -> 37.5 us (level)
  no operation moved by 1% of the time
where the time goes in v6:
time: 37.5 us; the launch traced here: 37.3 us
  starting transfers between devices  21 us (56%)
  Pallas kernels  7.26 us (19%)
  waiting for transfers between devices  7.05 us (19%)
  local copies, waits for them, and re-layouts  0.97 us (3%)
  matrix products  0.44 us (1%)
    ppermute x6, starting transfers between devices, to_group(): return lax.ppermute(x, 'seq', pairs)  9.13 us
    ppermute x3, starting transfers between devices, to_head(): lax.ppermute(x, 'head', [(h, partner(h, t, head_count)) for h in range(he...  7.66 us
    pallas_call x4, Pallas kernels, attend(): pl.pallas_call(functools.partial(attend_kernel, tuple(pieces), tuple(((le...  4.61 us
    ppermute x3, waiting for transfers between devices, from_group(): return lax.ppermute(x, 'seq', pairs)  3.63 us
    ppermute x3, starting transfers between devices, from_group(): return lax.ppermute(x, 'seq', pairs)  3.55 us
    ppermute x3, waiting for transfers between devices, to_head(): lax.ppermute(x, 'head', [(h, partner(h, t, head_count)) for h in range(he...  3.15 us
    pallas_call x1, Pallas kernels, prepare(): pl.pallas_call(functools.partial(prepare_kernel, groups, gather, shards),...  1.74 us
    pallas_call x1, Pallas kernels, unpack(): pl.pallas_call(functools.partial(unpack_kernel, tuple(steps), gather, wid...  0.77 us
  transfers between devices with their start and end apart: 15, of which 5 were waited for; matrix products, arithmetic and copies ran while one was open for 3% of the time, Pallas kernels for 10%

profile of v6, /device:TPU:0, one launch (start us, length us, event | category | flops | bytes accessed | tf_op | source)
XLA Modules:
  0.0 37.3 jit_solution(17906911950725308805)
XLA Ops:
  0.0 1.7 %prepare.1 = (bf16[384,384]{1,0:T(8,128)(2,1)S(1)}, bf16[384,384]{1,0:T(8,128)(2,1)S(1)}, bf16[384,384]{1,0:T(8,128)(2,1)S(1)}, bf16[384,384]{1,0:T(8,128)(2,1)S...) custom-call(bf16[128,1536]{1,0:T(8,128)(2,1)} %refs_0_.1, ...), custom_call_target="tpu_custom_call" | custom-call | flops 393216 | bytes 3145728 | tf_op jit(solution)/shard_map/prepare/pallas_call | solution.py:97
  1.8 0.5 %collective-permute-start.1 = (bf16[256,384]{1,0:T(8,128)(2,1)S(1)}, bf16[256,384]{1,0:T(8,128)(2,1)S(1)}, u32[]{:S(2)}, u32[]{:S(2)}) collective-permute-start(bf16[256,384]{1,0:T(8,128)(2,1)S(1)} %slice.51), channel_id=1, source_target_pairs={{0,4},{4,0},{8,12},{12,8},{16,20},{20,16},{24,28},{28,24},{1,5},{5... | collective-permute-start | bytes 589832 | tf_op jit(solution)/shard_map/ppermute | solution.py:357
  2.3 3.5 %collective-permute-start = (bf16[384,384]{1,0:T(8,128)(2,1)S(1)}, bf16[384,384]{1,0:T(8,128)(2,1)S(1)}, u32[]{:S(2)}, u32[]{:S(2)}) collective-permute-start(bf16[384,384]{1,0:T(8,128)(2,1)S(1)} %get-tuple-element.47), channel_id=1, source_target_pairs={{0,24},{4,28},{8,16},{12,20},{16,8},{20,12},{24,0},{28,4},{1,25},{... | collective-permute-start | bytes 884744 | tf_op jit(solution)/shard_map/ppermute | solution.py:343
  5.8 1.6 %collective-permute-start.2 = (bf16[4,2,16,384]{3,2,1,0:T(8,128)(2,1)S(1)}, bf16[4,2,16,384]{3,2,1,0:T(8,128)(2,1)S(1)}, u32[]{:S(2)}, u32[]{:S(2)}) collective-permute-start(bf16[4,2,16,384]{3,2,1,0:T(8,128)(2,1)S(1)} %get-tuple-element.57), channel_id=1, source_target_pairs={{0,1},{1,0},{2,3},{3,2},{4,5},{5,4},{6,7},{7,6},{8,9},{9,8},{10,11... | collective-permute-start | bytes 294920 | tf_op jit(solution)/shard_map/ppermute | solution.py:362
  7.4 2.7 %collective-permute-start.3 = (bf16[4,2,16,384]{3,2,1,0:T(8,128)(2,1)S(1)}, bf16[4,2,16,384]{3,2,1,0:T(8,128)(2,1)S(1)}, u32[]{:S(2)}, u32[]{:S(2)}) collective-permute-start(bf16[4,2,16,384]{3,2,1,0:T(8,128)(2,1)S(1)} %get-tuple-element.59), channel_id=1, source_target_pairs={{0,2},{1,3},{2,0},{3,1},{4,6},{5,7},{6,4},{7,5},{8,10},{9,11},{10,... | collective-permute-start | bytes 294920 | tf_op jit(solution)/shard_map/ppermute | solution.py:362
  10.1 0.5 %collective-permute-start.5 = (bf16[384,384]{1,0:T(8,128)(2,1)S(1)}, bf16[384,384]{1,0:T(8,128)(2,1)S(1)}, u32[]{:S(2)}, u32[]{:S(2)}) collective-permute-start(bf16[384,384]{1,0:T(8,128)(2,1)S(1)} %get-tuple-element.62), channel_id=1, source_target_pairs={{0,8},{4,12},{8,0},{12,4},{16,24},{20,28},{24,16},{28,20},{1,9},{5... | collective-permute-start | bytes 884744 | tf_op jit(solution)/shard_map/ppermute | solution.py:343
  10.6 1.4 %collective-permute-start.6 = (bf16[384,384]{1,0:T(8,128)(2,1)S(1)}, bf16[384,384]{1,0:T(8,128)(2,1)S(1)}, u32[]{:S(2)}, u32[]{:S(2)}) collective-permute-start(bf16[384,384]{1,0:T(8,128)(2,1)S(1)} %get-tuple-element.64), channel_id=1, source_target_pairs={{0,16},{4,20},{8,24},{12,28},{16,0},{20,4},{24,8},{28,12},{1,17},{... | collective-permute-start | bytes 884744 | tf_op jit(solution)/shard_map/ppermute | solution.py:343
  12.0 3.4 %collective-permute-start.4 = (bf16[4,2,16,384]{3,2,1,0:T(8,128)(2,1)S(1)}, bf16[4,2,16,384]{3,2,1,0:T(8,128)(2,1)S(1)}, u32[]{:S(2)}, u32[]{:S(2)}) collective-permute-start(bf16[4,2,16,384]{3,2,1,0:T(8,128)(2,1)S(1)} %get-tuple-element.60), channel_id=1, source_target_pairs={{0,3},{1,2},{2,1},{3,0},{4,7},{5,6},{6,5},{7,4},{8,11},{9,10},{10,... | collective-permute-start | bytes 294920 | tf_op jit(solution)/shard_map/ppermute | solution.py:362
  15.5 3.1 %collective-permute-done.4 = bf16[4,2,16,384]{3,2,1,0:T(8,128)(2,1)S(1)} collective-permute-done((bf16[4,2,16,384]{3,2,1,0:T(8,128)(2,1)S(1)}, bf16[4,2,16,384]{3,2,1,0:T(8,128)(2,1)S(1)}, u32[]{:S(2)}, u32[]{:S(2)}) %collective-permute-start.4) | collective-permute-done | bytes 98336 | tf_op jit(solution)/shard_map/ppermute | solution.py:362
  18.6 1.6 %collective-permute-start.7 = (bf16[128,384]{1,0:T(8,128)(2,1)S(1)}, bf16[128,384]{1,0:T(8,128)(2,1)S(1)}, u32[]{:S(2)}, u32[]{:S(2)}) collective-permute-start(bf16[128,384]{1,0:T(8,128)(2,1)S(1)} %interleave.4), channel_id=1, source_target_pairs={{0,24},{4,28},{8,16},{12,20},{16,8},{20,12},{24,0},{28,4},{1,25},{... | collective-permute-start | bytes 294920 | tf_op jit(solution)/shard_map/ppermute | solution.py:343
  20.3 0.6 %collective-permute-start.8 = (bf16[128,384]{1,0:T(8,128)(2,1)S(1)}, bf16[128,384]{1,0:T(8,128)(2,1)S(1)}, u32[]{:S(2)}, u32[]{:S(2)}) collective-permute-start(bf16[128,384]{1,0:T(8,128)(2,1)S(1)} %interleave.5), channel_id=1, source_target_pairs={{0,8},{4,12},{8,0},{12,4},{16,24},{20,28},{24,16},{28,20},{1,9},{5... | collective-permute-start | bytes 294920 | tf_op jit(solution)/shard_map/ppermute | solution.py:343
  20.9 1.5 %collective-permute-start.9 = (bf16[128,384]{1,0:T(8,128)(2,1)S(1)}, bf16[128,384]{1,0:T(8,128)(2,1)S(1)}, u32[]{:S(2)}, u32[]{:S(2)}) collective-permute-start(bf16[128,384]{1,0:T(8,128)(2,1)S(1)} %interleave.6), channel_id=1, source_target_pairs={{0,16},{4,20},{8,24},{12,28},{16,0},{20,4},{24,8},{28,12},{1,17},{... | collective-permute-start | bytes 294920 | tf_op jit(solution)/shard_map/ppermute | solution.py:343
  22.5 0.1 stack.155
  22.6 0.1 stack.138
  22.9 0.1 add.233
  23.0 0.1 add.253
  23.2 0.1 add.277
  23.4 0.4 %copy-done = s32[16,16]{1,0:T(8,128)S(1)} copy-done((s32[16,16]{1,0:T(8,128)S(1)}, s32[16,16]{1,0:T(8,128)}, u32[]{:S(2)}) %copy-start) | copy-done | bytes 1048
  23.8 0.2 fusion.4
  24.0 0.1 fusion.1.refs_7_.refs_9_
  24.1 0.1 fusion.refs_4_.refs_13_
  24.3 1.1 %attend.4 = (f32[384,384]{1,0:T(8,128)S(1)}, f32[384,384]{1,0:T(8,128)S(1)}, f32[384,384]{1,0:T(8,128)S(1)}) custom-call(bf16[384,384]{1,0:T(8,128)(2,1)S(1)} %collective-permute-done.refs_0_.refs_6_.refs_2_.refs_4_, bf16[384,384]{1,0:T(8,128)(2,1)S(1)} %collective-permute-done.5.refs_1_.refs_4_.refs_0_.refs_2_, ...), custom_call_target="tpu_custom_call" | custom-call | flops 301989888 | bytes 786432 | tf_op jit(solution)/shard_map/attend/pallas_call | solution.py:260
  25.4 0.2 collective-permute-done.9.refs_2_.refs_5_.refs_7_
  25.7 1.6 %attend.5 = (f32[384,384]{1,0:T(8,128)S(1)}, f32[384,384]{1,0:T(8,128)S(1)}, f32[384,384]{1,0:T(8,128)S(1)}) custom-call(bf16[384,384]{1,0:T(8,128)(2,1)S(1)} %collective-permute-done.refs_0_.refs_6_.refs_2_.refs_4_, bf16[384,384]{1,0:T(8,128)(2,1)S(1)} %collective-permute-done.5.refs_1_.refs_4_.refs_0_.refs_2_, ...), custom_call_target="tpu_custom_call" | custom-call | flops 452984832 | bytes 1179648 | tf_op jit(solution)/shard_map/attend/pallas_call | solution.py:260
  27.4 0.9 %attend.6 = (bf16[128,384]{1,0:T(8,128)(2,1)S(1)}, bf16[128,384]{1,0:T(8,128)(2,1)S(1)}, bf16[128,384]{1,0:T(8,128)(2,1)S(1)}) custom-call(bf16[384,384]{1,0:T(8,128)(2,1)S(1)} %collective-permute-done.refs_0_.refs_6_.refs_2_.refs_4_, bf16[384,384]{1,0:T(8,128)(2,1)S(1)} %collective-permute-done.5.refs_1_.refs_4_.refs_0_.refs_2_, ...), custom_call_target="tpu_custom_call" | custom-call | flops 150994944 | bytes 393216 | tf_op jit(solution)/shard_map/attend/pallas_call | solution.py:260
  28.3 1.5 %collective-permute-start.12 = (bf16[128,384]{1,0:T(8,128)(2,1)S(1)}, bf16[128,384]{1,0:T(8,128)(2,1)S(1)}, u32[]{:S(2)}, u32[]{:S(2)}) collective-permute-start(bf16[128,384]{1,0:T(8,128)(2,1)S(1)} %get-tuple-element.86), channel_id=1, source_target_pairs={{0,24},{4,28},{8,16},{12,20},{16,8},{20,12},{24,0},{28,4},{1,25},{... | collective-permute-start | bytes 294920 | tf_op jit(solution)/shard_map/ppermute | solution.py:351
  29.8 1.4 %collective-permute-start.13 = (bf16[128,384]{1,0:T(8,128)(2,1)S(1)}, bf16[128,384]{1,0:T(8,128)(2,1)S(1)}, u32[]{:S(2)}, u32[]{:S(2)}) collective-permute-start(bf16[128,384]{1,0:T(8,128)(2,1)S(1)} %get-tuple-element.87), channel_id=1, source_target_pairs={{0,8},{4,12},{8,0},{12,4},{16,24},{20,28},{24,16},{28,20},{1,9},{5... | collective-permute-start | bytes 294920 | tf_op jit(solution)/shard_map/ppermute | solution.py:351
  31.2 0.6 %collective-permute-start.14 = (bf16[128,384]{1,0:T(8,128)(2,1)S(1)}, bf16[128,384]{1,0:T(8,128)(2,1)S(1)}, u32[]{:S(2)}, u32[]{:S(2)}) collective-permute-start(bf16[128,384]{1,0:T(8,128)(2,1)S(1)} %get-tuple-element.88), channel_id=1, source_target_pairs={{0,16},{4,20},{8,24},{12,28},{16,0},{20,4},{24,8},{28,12},{1,17},{... | collective-permute-start | bytes 294920 | tf_op jit(solution)/shard_map/ppermute | solution.py:351
  31.8 1.0 %attend.7.refs_3_ = bf16[128,384]{1,0:T(8,128)(2,1)S(1)} custom-call(bf16[384,384]{1,0:T(8,128)(2,1)S(1)} %get-tuple-element.54.refs_3_.refs_0_.refs_1_, bf16[384,384]{1,0:T(8,128)(2,1)S(1)} %get-tuple-element.54.refs_3_.refs_0_.refs_1_, bf16[384,384]{1,0:T(8,128)(2,1)S(1)} %collective-permute-done.5.refs_1_.refs_4_.refs_0_.refs_2_, ...), custom_call_target="tpu_custom_call" | custom-call | flops 301989888 | bytes 2359296 | tf_op jit(solution)/shard_map/attend/pallas_call | solution.py:260
  32.9 2.0 %collective-permute-done.12.refs_0_ = bf16[128,384]{1,0:T(8,128)(2,1)S(1)} collective-permute-done((bf16[128,384]{1,0:T(8,128)(2,1)S(1)}, bf16[128,384]{1,0:T(8,128)(2,1)S(1)}, u32[]{:S(2)}, u32[]{:S(2)}) %collective-permute-start.12) | collective-permute-done | bytes 98336 | tf_op jit(solution)/shard_map/ppermute | solution.py:351
  34.8 1.6 %collective-permute-done.13.refs_1_ = bf16[128,384]{1,0:T(8,128)(2,1)S(1)} collective-permute-done((bf16[128,384]{1,0:T(8,128)(2,1)S(1)}, bf16[128,384]{1,0:T(8,128)(2,1)S(1)}, u32[]{:S(2)}, u32[]{:S(2)}) %collective-permute-start.13) | collective-permute-done | bytes 98336 | tf_op jit(solution)/shard_map/ppermute | solution.py:351
  36.5 0.8 %unpack_heads.1 = bf16[128,1536]{1,0:T(8,128)(2,1)} custom-call(bf16[128,384]{1,0:T(8,128)(2,1)S(1)} %collective-permute-done.12.refs_0_, bf16[128,384]{1,0:T(8,128)(2,1)S(1)} %collective-permute-done.13.refs_1_, bf16[128,384]{1,0:T(8,128)(2,1)S(1)} %collective-permute-done.14.refs_2_, bf16[128,384]{1,0:T(8,128)(2,1)S(1)} %attend.7.refs_3_), custom_call_target="tpu_custom_call" | custom-call | bytes 786432 | tf_op jit(solution)/shard_map/unpack_heads/pallas_call | solution.py:302
  (33 shorter events, 0.8 us)
Async XLA Ops:
  1.8 4.0 %collective-permute-start.1 = (bf16[256,384]{1,0:T(8,128)(2,1)S(1)}, bf16[256,384]{1,0:T(8,128)(2,1)S(1)}, u32[]{:S(2)}, u32[]{:S(2)}) collective-permute-start(bf16[256,384]{1,0:T(8,128)(2,1)S(1)} %slice.51), channel_id=1, source_target_pairs={{0,4},{4,0},{8,12},{12,8},{16,20},{20,16},{24,28},{28,24},{1,5},{5... | collective-permute-start | bytes 589832 | tf_op jit(solution)/shard_map/ppermute | solution.py:357
  2.3 18.6 %collective-permute-start = (bf16[384,384]{1,0:T(8,128)(2,1)S(1)}, bf16[384,384]{1,0:T(8,128)(2,1)S(1)}, u32[]{:S(2)}, u32[]{:S(2)}) collective-permute-start(bf16[384,384]{1,0:T(8,128)(2,1)S(1)} %get-tuple-element.47), channel_id=1, source_target_pairs={{0,24},{4,28},{8,16},{12,20},{16,8},{20,12},{24,0},{28,4},{1,25},{... | collective-permute-start | bytes 884744 | tf_op jit(solution)/shard_map/ppermute | solution.py:343
  5.8 6.2 %collective-permute-start.2 = (bf16[4,2,16,384]{3,2,1,0:T(8,128)(2,1)S(1)}, bf16[4,2,16,384]{3,2,1,0:T(8,128)(2,1)S(1)}, u32[]{:S(2)}, u32[]{:S(2)}) collective-permute-start(bf16[4,2,16,384]{3,2,1,0:T(8,128)(2,1)S(1)} %get-tuple-element.57), channel_id=1, source_target_pairs={{0,1},{1,0},{2,3},{3,2},{4,5},{5,4},{6,7},{7,6},{8,9},{9,8},{10,11... | collective-permute-start | bytes 294920 | tf_op jit(solution)/shard_map/ppermute | solution.py:362
  7.4 8.0 %collective-permute-start.3 = (bf16[4,2,16,384]{3,2,1,0:T(8,128)(2,1)S(1)}, bf16[4,2,16,384]{3,2,1,0:T(8,128)(2,1)S(1)}, u32[]{:S(2)}, u32[]{:S(2)}) collective-permute-start(bf16[4,2,16,384]{3,2,1,0:T(8,128)(2,1)S(1)} %get-tuple-element.59), channel_id=1, source_target_pairs={{0,2},{1,3},{2,0},{3,1},{4,6},{5,7},{6,4},{7,5},{8,10},{9,11},{10,... | collective-permute-start | bytes 294920 | tf_op jit(solution)/shard_map/ppermute | solution.py:362
  10.1 12.3 %collective-permute-start.5 = (bf16[384,384]{1,0:T(8,128)(2,1)S(1)}, bf16[384,384]{1,0:T(8,128)(2,1)S(1)}, u32[]{:S(2)}, u32[]{:S(2)}) collective-permute-start(bf16[384,384]{1,0:T(8,128)(2,1)S(1)} %get-tuple-element.62), channel_id=1, source_target_pairs={{0,8},{4,12},{8,0},{12,4},{16,24},{20,28},{24,16},{28,20},{1,9},{5... | collective-permute-start | bytes 884744 | tf_op jit(solution)/shard_map/ppermute | solution.py:343
  10.6 11.8 %collective-permute-start.6 = (bf16[384,384]{1,0:T(8,128)(2,1)S(1)}, bf16[384,384]{1,0:T(8,128)(2,1)S(1)}, u32[]{:S(2)}, u32[]{:S(2)}) collective-permute-start(bf16[384,384]{1,0:T(8,128)(2,1)S(1)} %get-tuple-element.64), channel_id=1, source_target_pairs={{0,16},{4,20},{8,24},{12,28},{16,0},{20,4},{24,8},{28,12},{1,17},{... | collective-permute-start | bytes 884744 | tf_op jit(solution)/shard_map/ppermute | solution.py:343
  12.0 6.6 %collective-permute-start.4 = (bf16[4,2,16,384]{3,2,1,0:T(8,128)(2,1)S(1)}, bf16[4,2,16,384]{3,2,1,0:T(8,128)(2,1)S(1)}, u32[]{:S(2)}, u32[]{:S(2)}) collective-permute-start(bf16[4,2,16,384]{3,2,1,0:T(8,128)(2,1)S(1)} %get-tuple-element.60), channel_id=1, source_target_pairs={{0,3},{1,2},{2,1},{3,0},{4,7},{5,6},{6,5},{7,4},{8,11},{9,10},{10,... | collective-permute-start | bytes 294920 | tf_op jit(solution)/shard_map/ppermute | solution.py:362
  18.6 6.7 %collective-permute-start.7 = (bf16[128,384]{1,0:T(8,128)(2,1)S(1)}, bf16[128,384]{1,0:T(8,128)(2,1)S(1)}, u32[]{:S(2)}, u32[]{:S(2)}) collective-permute-start(bf16[128,384]{1,0:T(8,128)(2,1)S(1)} %interleave.4), channel_id=1, source_target_pairs={{0,24},{4,28},{8,16},{12,20},{16,8},{20,12},{24,0},{28,4},{1,25},{... | collective-permute-start | bytes 294920 | tf_op jit(solution)/shard_map/ppermute | solution.py:343
  20.3 5.1 %collective-permute-start.8 = (bf16[128,384]{1,0:T(8,128)(2,1)S(1)}, bf16[128,384]{1,0:T(8,128)(2,1)S(1)}, u32[]{:S(2)}, u32[]{:S(2)}) collective-permute-start(bf16[128,384]{1,0:T(8,128)(2,1)S(1)} %interleave.5), channel_id=1, source_target_pairs={{0,8},{4,12},{8,0},{12,4},{16,24},{20,28},{24,16},{28,20},{1,9},{5... | collective-permute-start | bytes 294920 | tf_op jit(solution)/shard_map/ppermute | solution.py:343
  20.9 4.7 %collective-permute-start.9 = (bf16[128,384]{1,0:T(8,128)(2,1)S(1)}, bf16[128,384]{1,0:T(8,128)(2,1)S(1)}, u32[]{:S(2)}, u32[]{:S(2)}) collective-permute-start(bf16[128,384]{1,0:T(8,128)(2,1)S(1)} %interleave.6), channel_id=1, source_target_pairs={{0,16},{4,20},{8,24},{12,28},{16,0},{20,4},{24,8},{28,12},{1,17},{... | collective-permute-start | bytes 294920 | tf_op jit(solution)/shard_map/ppermute | solution.py:343
  23.1 0.7 %copy-start = (s32[16,16]{1,0:T(8,128)S(1)}, s32[16,16]{1,0:T(8,128)}, u32[]{:S(2)}) copy-start(s32[16,16]{1,0:T(8,128)} %param.15) | copy-start | bytes 3076
  23.3 2.4 %collective-permute-start.11 = (bf16[3,256,384]{2,1,0:T(8,128)(2,1)S(1)}, bf16[3,256,384]{2,1,0:T(8,128)(2,1)S(1)}, u32[]{:S(2)}, u32[]{:S(2)}) collective-permute-start(bf16[3,256,384]{2,1,0:T(8,128)(2,1)S(1)} %join.3), channel_id=1, source_target_pairs={{0,4},{4,0},{8,12},{12,8},{16,20},{20,16},{24,28},{28,24},{1,5},{5... | collective-permute-start | bytes 1769480 | tf_op jit(solution)/shard_map/ppermute | solution.py:357
  25.6 1.8 %collective-permute-start.10 = (bf16[4,128,384]{2,1,0:T(8,128)(2,1)S(1)}, bf16[4,128,384]{2,1,0:T(8,128)(2,1)S(1)}, u32[]{:S(2)}, u32[]{:S(2)}) collective-permute-start(bf16[4,128,384]{2,1,0:T(8,128)(2,1)S(1)} %join.2), channel_id=1, source_target_pairs={{0,4},{4,0},{8,12},{12,8},{16,20},{20,16},{24,28},{28,24},{1,5},{5... | collective-permute-start | bytes 1179656 | tf_op jit(solution)/shard_map/ppermute | solution.py:357
  28.3 6.6 %collective-permute-start.12 = (bf16[128,384]{1,0:T(8,128)(2,1)S(1)}, bf16[128,384]{1,0:T(8,128)(2,1)S(1)}, u32[]{:S(2)}, u32[]{:S(2)}) collective-permute-start(bf16[128,384]{1,0:T(8,128)(2,1)S(1)} %get-tuple-element.86), channel_id=1, source_target_pairs={{0,24},{4,28},{8,16},{12,20},{16,8},{20,12},{24,0},{28,4},{1,25},{... | collective-permute-start | bytes 294920 | tf_op jit(solution)/shard_map/ppermute | solution.py:351
  29.8 6.7 %collective-permute-start.13 = (bf16[128,384]{1,0:T(8,128)(2,1)S(1)}, bf16[128,384]{1,0:T(8,128)(2,1)S(1)}, u32[]{:S(2)}, u32[]{:S(2)}) collective-permute-start(bf16[128,384]{1,0:T(8,128)(2,1)S(1)} %get-tuple-element.87), channel_id=1, source_target_pairs={{0,8},{4,12},{8,0},{12,4},{16,24},{20,28},{24,16},{28,20},{1,9},{5... | collective-permute-start | bytes 294920 | tf_op jit(solution)/shard_map/ppermute | solution.py:351
  31.2 5.3 %collective-permute-start.14 = (bf16[128,384]{1,0:T(8,128)(2,1)S(1)}, bf16[128,384]{1,0:T(8,128)(2,1)S(1)}, u32[]{:S(2)}, u32[]{:S(2)}) collective-permute-start(bf16[128,384]{1,0:T(8,128)(2,1)S(1)} %get-tuple-element.88), channel_id=1, source_target_pairs={{0,16},{4,20},{8,24},{12,28},{16,0},{20,4},{24,8},{28,12},{1,17},{... | collective-permute-start | bytes 294920 | tf_op jit(solution)/shard_map/ppermute | solution.py:351

commit v7 on v6

--- a/solution.py
+++ b/solution.py
@@ -215,10 +215,14 @@
     state, refs = (refs[:3], refs[3:]) if merge else (None, refs)
     width = q_refs[0].shape[1]
     heads = [slice(at, at + DH) for at in range(0, width, DH)]
-    scores = [
-        scores_of(rows_of(q_refs, q_start, rows, cols), sets, cols) for cols in heads
-    ]
-    weighed = [weigh(x) for x in scores]
+    weighed = []
+    together = heads if len(sets) > 1 or not merge else heads[:1]
+    for n in range(0, len(heads), len(together)):
+        scores = [
+            scores_of(rows_of(q_refs, q_start, rows, cols), sets, cols)
+            for cols in heads[n : n + len(together)]
+        ]
+        weighed += [weigh(x) for x in scores]
     for cols, (peak, total, weights) in zip(heads, weighed):
         product = 0.0
         for x, (refs_of, half, _) in zip(weights, sets):

time: 37.5 us -> 37.5 us (level)
  no operation moved by 1% of the time
where the time goes in v7:
time: 37.5 us; the launch traced here: 37.3 us
  starting transfers between devices  21 us (56%)
  Pallas kernels  7.26 us (19%)
  waiting for transfers between devices  7.05 us (19%)
  local copies, waits for them, and re-layouts  0.97 us (3%)
  matrix products  0.44 us (1%)
    ppermute x6, starting transfers between devices, to_group(): return lax.ppermute(x, 'seq', pairs)  9.13 us
    ppermute x3, starting transfers between devices, to_head(): lax.ppermute(x, 'head', [(h, partner(h, t, head_count)) for h in range(he...  7.66 us
    pallas_call x4, Pallas kernels, attend(): pl.pallas_call(functools.partial(attend_kernel, tuple(pieces), tuple(((le...  4.61 us
    ppermute x3, waiting for transfers between devices, from_group(): return lax.ppermute(x, 'seq', pairs)  3.63 us
    ppermute x3, starting transfers between devices, from_group(): return lax.ppermute(x, 'seq', pairs)  3.55 us
    ppermute x3, waiting for transfers between devices, to_head(): lax.ppermute(x, 'head', [(h, partner(h, t, head_count)) for h in range(he...  3.15 us
    pallas_call x1, Pallas kernels, prepare(): pl.pallas_call(functools.partial(prepare_kernel, groups, gather, shards),...  1.74 us
    pallas_call x1, Pallas kernels, unpack(): pl.pallas_call(functools.partial(unpack_kernel, tuple(steps), gather, wid...  0.77 us
  transfers between devices with their start and end apart: 15, of which 5 were waited for; matrix products, arithmetic and copies ran while one was open for 3% of the time, Pallas kernels for 10%

profile of v7, /device:TPU:0, one launch (start us, length us, event | category | flops | bytes accessed | tf_op | source)
XLA Modules:
  0.0 37.3 jit_solution(17906911950725308805)
XLA Ops:
  0.0 1.7 %prepare.1 = (bf16[384,384]{1,0:T(8,128)(2,1)S(1)}, bf16[384,384]{1,0:T(8,128)(2,1)S(1)}, bf16[384,384]{1,0:T(8,128)(2,1)S(1)}, bf16[384,384]{1,0:T(8,128)(2,1)S...) custom-call(bf16[128,1536]{1,0:T(8,128)(2,1)} %refs_0_.1, ...), custom_call_target="tpu_custom_call" | custom-call | flops 393216 | bytes 3145728 | tf_op jit(solution)/shard_map/prepare/pallas_call | solution.py:97
  1.8 0.5 %collective-permute-start.1 = (bf16[256,384]{1,0:T(8,128)(2,1)S(1)}, bf16[256,384]{1,0:T(8,128)(2,1)S(1)}, u32[]{:S(2)}, u32[]{:S(2)}) collective-permute-start(bf16[256,384]{1,0:T(8,128)(2,1)S(1)} %slice.51), channel_id=1, source_target_pairs={{0,4},{4,0},{8,12},{12,8},{16,20},{20,16},{24,28},{28,24},{1,5},{5... | collective-permute-start | bytes 589832 | tf_op jit(solution)/shard_map/ppermute | solution.py:361
  2.3 3.5 %collective-permute-start = (bf16[384,384]{1,0:T(8,128)(2,1)S(1)}, bf16[384,384]{1,0:T(8,128)(2,1)S(1)}, u32[]{:S(2)}, u32[]{:S(2)}) collective-permute-start(bf16[384,384]{1,0:T(8,128)(2,1)S(1)} %get-tuple-element.47), channel_id=1, source_target_pairs={{0,24},{4,28},{8,16},{12,20},{16,8},{20,12},{24,0},{28,4},{1,25},{... | collective-permute-start | bytes 884744 | tf_op jit(solution)/shard_map/ppermute | solution.py:347
  5.8 1.6 %collective-permute-start.2 = (bf16[4,2,16,384]{3,2,1,0:T(8,128)(2,1)S(1)}, bf16[4,2,16,384]{3,2,1,0:T(8,128)(2,1)S(1)}, u32[]{:S(2)}, u32[]{:S(2)}) collective-permute-start(bf16[4,2,16,384]{3,2,1,0:T(8,128)(2,1)S(1)} %get-tuple-element.57), channel_id=1, source_target_pairs={{0,1},{1,0},{2,3},{3,2},{4,5},{5,4},{6,7},{7,6},{8,9},{9,8},{10,11... | collective-permute-start | bytes 294920 | tf_op jit(solution)/shard_map/ppermute | solution.py:366
  7.4 2.7 %collective-permute-start.3 = (bf16[4,2,16,384]{3,2,1,0:T(8,128)(2,1)S(1)}, bf16[4,2,16,384]{3,2,1,0:T(8,128)(2,1)S(1)}, u32[]{:S(2)}, u32[]{:S(2)}) collective-permute-start(bf16[4,2,16,384]{3,2,1,0:T(8,128)(2,1)S(1)} %get-tuple-element.59), channel_id=1, source_target_pairs={{0,2},{1,3},{2,0},{3,1},{4,6},{5,7},{6,4},{7,5},{8,10},{9,11},{10,... | collective-permute-start | bytes 294920 | tf_op jit(solution)/shard_map/ppermute | solution.py:366
  10.1 0.5 %collective-permute-start.5 = (bf16[384,384]{1,0:T(8,128)(2,1)S(1)}, bf16[384,384]{1,0:T(8,128)(2,1)S(1)}, u32[]{:S(2)}, u32[]{:S(2)}) collective-permute-start(bf16[384,384]{1,0:T(8,128)(2,1)S(1)} %get-tuple-element.62), channel_id=1, source_target_pairs={{0,8},{4,12},{8,0},{12,4},{16,24},{20,28},{24,16},{28,20},{1,9},{5... | collective-permute-start | bytes 884744 | tf_op jit(solution)/shard_map/ppermute | solution.py:347
  10.6 1.4 %collective-permute-start.6 = (bf16[384,384]{1,0:T(8,128)(2,1)S(1)}, bf16[384,384]{1,0:T(8,128)(2,1)S(1)}, u32[]{:S(2)}, u32[]{:S(2)}) collective-permute-start(bf16[384,384]{1,0:T(8,128)(2,1)S(1)} %get-tuple-element.64), channel_id=1, source_target_pairs={{0,16},{4,20},{8,24},{12,28},{16,0},{20,4},{24,8},{28,12},{1,17},{... | collective-permute-start | bytes 884744 | tf_op jit(solution)/shard_map/ppermute | solution.py:347
  12.0 3.4 %collective-permute-start.4 = (bf16[4,2,16,384]{3,2,1,0:T(8,128)(2,1)S(1)}, bf16[4,2,16,384]{3,2,1,0:T(8,128)(2,1)S(1)}, u32[]{:S(2)}, u32[]{:S(2)}) collective-permute-start(bf16[4,2,16,384]{3,2,1,0:T(8,128)(2,1)S(1)} %get-tuple-element.60), channel_id=1, source_target_pairs={{0,3},{1,2},{2,1},{3,0},{4,7},{5,6},{6,5},{7,4},{8,11},{9,10},{10,... | collective-permute-start | bytes 294920 | tf_op jit(solution)/shard_map/ppermute | solution.py:366
  15.5 3.1 %collective-permute-done.4 = bf16[4,2,16,384]{3,2,1,0:T(8,128)(2,1)S(1)} collective-permute-done((bf16[4,2,16,384]{3,2,1,0:T(8,128)(2,1)S(1)}, bf16[4,2,16,384]{3,2,1,0:T(8,128)(2,1)S(1)}, u32[]{:S(2)}, u32[]{:S(2)}) %collective-permute-start.4) | collective-permute-done | bytes 98336 | tf_op jit(solution)/shard_map/ppermute | solution.py:366
  18.6 1.6 %collective-permute-start.7 = (bf16[128,384]{1,0:T(8,128)(2,1)S(1)}, bf16[128,384]{1,0:T(8,128)(2,1)S(1)}, u32[]{:S(2)}, u32[]{:S(2)}) collective-permute-start(bf16[128,384]{1,0:T(8,128)(2,1)S(1)} %interleave.4), channel_id=1, source_target_pairs={{0,24},{4,28},{8,16},{12,20},{16,8},{20,12},{24,0},{28,4},{1,25},{... | collective-permute-start | bytes 294920 | tf_op jit(solution)/shard_map/ppermute | solution.py:347
  20.3 0.6 %collective-permute-start.8 = (bf16[128,384]{1,0:T(8,128)(2,1)S(1)}, bf16[128,384]{1,0:T(8,128)(2,1)S(1)}, u32[]{:S(2)}, u32[]{:S(2)}) collective-permute-start(bf16[128,384]{1,0:T(8,128)(2,1)S(1)} %interleave.5), channel_id=1, source_target_pairs={{0,8},{4,12},{8,0},{12,4},{16,24},{20,28},{24,16},{28,20},{1,9},{5... | collective-permute-start | bytes 294920 | tf_op jit(solution)/shard_map/ppermute | solution.py:347
  20.9 1.5 %collective-permute-start.9 = (bf16[128,384]{1,0:T(8,128)(2,1)S(1)}, bf16[128,384]{1,0:T(8,128)(2,1)S(1)}, u32[]{:S(2)}, u32[]{:S(2)}) collective-permute-start(bf16[128,384]{1,0:T(8,128)(2,1)S(1)} %interleave.6), channel_id=1, source_target_pairs={{0,16},{4,20},{8,24},{12,28},{16,0},{20,4},{24,8},{28,12},{1,17},{... | collective-permute-start | bytes 294920 | tf_op jit(solution)/shard_map/ppermute | solution.py:347
  22.5 0.1 stack.155
  22.6 0.1 stack.138
  22.9 0.1 add.233
  23.0 0.1 add.253
  23.2 0.1 add.277
  23.4 0.4 %copy-done = s32[16,16]{1,0:T(8,128)S(1)} copy-done((s32[16,16]{1,0:T(8,128)S(1)}, s32[16,16]{1,0:T(8,128)}, u32[]{:S(2)}) %copy-start) | copy-done | bytes 1048
  23.8 0.2 fusion.4
  24.0 0.1 fusion.1.refs_7_.refs_9_
  24.1 0.1 fusion.refs_4_.refs_13_
  24.3 1.1 %attend.4 = (f32[384,384]{1,0:T(8,128)S(1)}, f32[384,384]{1,0:T(8,128)S(1)}, f32[384,384]{1,0:T(8,128)S(1)}) custom-call(bf16[384,384]{1,0:T(8,128)(2,1)S(1)} %collective-permute-done.refs_0_.refs_6_.refs_2_.refs_4_, bf16[384,384]{1,0:T(8,128)(2,1)S(1)} %collective-permute-done.5.refs_1_.refs_4_.refs_0_.refs_2_, ...), custom_call_target="tpu_custom_call" | custom-call | flops 301989888 | bytes 786432 | tf_op jit(solution)/shard_map/attend/pallas_call | solution.py:264
  25.4 0.2 collective-permute-done.9.refs_2_.refs_5_.refs_7_
  25.7 1.6 %attend.5 = (f32[384,384]{1,0:T(8,128)S(1)}, f32[384,384]{1,0:T(8,128)S(1)}, f32[384,384]{1,0:T(8,128)S(1)}) custom-call(bf16[384,384]{1,0:T(8,128)(2,1)S(1)} %collective-permute-done.refs_0_.refs_6_.refs_2_.refs_4_, bf16[384,384]{1,0:T(8,128)(2,1)S(1)} %collective-permute-done.5.refs_1_.refs_4_.refs_0_.refs_2_, ...), custom_call_target="tpu_custom_call" | custom-call | flops 452984832 | bytes 1179648 | tf_op jit(solution)/shard_map/attend/pallas_call | solution.py:264
  27.4 0.9 %attend.6 = (bf16[128,384]{1,0:T(8,128)(2,1)S(1)}, bf16[128,384]{1,0:T(8,128)(2,1)S(1)}, bf16[128,384]{1,0:T(8,128)(2,1)S(1)}) custom-call(bf16[384,384]{1,0:T(8,128)(2,1)S(1)} %collective-permute-done.refs_0_.refs_6_.refs_2_.refs_4_, bf16[384,384]{1,0:T(8,128)(2,1)S(1)} %collective-permute-done.5.refs_1_.refs_4_.refs_0_.refs_2_, ...), custom_call_target="tpu_custom_call" | custom-call | flops 150994944 | bytes 393216 | tf_op jit(solution)/shard_map/attend/pallas_call | solution.py:264
  28.3 1.5 %collective-permute-start.12 = (bf16[128,384]{1,0:T(8,128)(2,1)S(1)}, bf16[128,384]{1,0:T(8,128)(2,1)S(1)}, u32[]{:S(2)}, u32[]{:S(2)}) collective-permute-start(bf16[128,384]{1,0:T(8,128)(2,1)S(1)} %get-tuple-element.86), channel_id=1, source_target_pairs={{0,24},{4,28},{8,16},{12,20},{16,8},{20,12},{24,0},{28,4},{1,25},{... | collective-permute-start | bytes 294920 | tf_op jit(solution)/shard_map/ppermute | solution.py:355
  29.8 1.4 %collective-permute-start.13 = (bf16[128,384]{1,0:T(8,128)(2,1)S(1)}, bf16[128,384]{1,0:T(8,128)(2,1)S(1)}, u32[]{:S(2)}, u32[]{:S(2)}) collective-permute-start(bf16[128,384]{1,0:T(8,128)(2,1)S(1)} %get-tuple-element.87), channel_id=1, source_target_pairs={{0,8},{4,12},{8,0},{12,4},{16,24},{20,28},{24,16},{28,20},{1,9},{5... | collective-permute-start | bytes 294920 | tf_op jit(solution)/shard_map/ppermute | solution.py:355
  31.2 0.6 %collective-permute-start.14 = (bf16[128,384]{1,0:T(8,128)(2,1)S(1)}, bf16[128,384]{1,0:T(8,128)(2,1)S(1)}, u32[]{:S(2)}, u32[]{:S(2)}) collective-permute-start(bf16[128,384]{1,0:T(8,128)(2,1)S(1)} %get-tuple-element.88), channel_id=1, source_target_pairs={{0,16},{4,20},{8,24},{12,28},{16,0},{20,4},{24,8},{28,12},{1,17},{... | collective-permute-start | bytes 294920 | tf_op jit(solution)/shard_map/ppermute | solution.py:355
  31.8 1.0 %attend.7.refs_3_ = bf16[128,384]{1,0:T(8,128)(2,1)S(1)} custom-call(bf16[384,384]{1,0:T(8,128)(2,1)S(1)} %get-tuple-element.54.refs_3_.refs_0_.refs_1_, bf16[384,384]{1,0:T(8,128)(2,1)S(1)} %get-tuple-element.54.refs_3_.refs_0_.refs_1_, bf16[384,384]{1,0:T(8,128)(2,1)S(1)} %collective-permute-done.5.refs_1_.refs_4_.refs_0_.refs_2_, ...), custom_call_target="tpu_custom_call" | custom-call | flops 301989888 | bytes 2359296 | tf_op jit(solution)/shard_map/attend/pallas_call | solution.py:264
  32.9 2.0 %collective-permute-done.12.refs_0_ = bf16[128,384]{1,0:T(8,128)(2,1)S(1)} collective-permute-done((bf16[128,384]{1,0:T(8,128)(2,1)S(1)}, bf16[128,384]{1,0:T(8,128)(2,1)S(1)}, u32[]{:S(2)}, u32[]{:S(2)}) %collective-permute-start.12) | collective-permute-done | bytes 98336 | tf_op jit(solution)/shard_map/ppermute | solution.py:355
  34.8 1.6 %collective-permute-done.13.refs_1_ = bf16[128,384]{1,0:T(8,128)(2,1)S(1)} collective-permute-done((bf16[128,384]{1,0:T(8,128)(2,1)S(1)}, bf16[128,384]{1,0:T(8,128)(2,1)S(1)}, u32[]{:S(2)}, u32[]{:S(2)}) %collective-permute-start.13) | collective-permute-done | bytes 98336 | tf_op jit(solution)/shard_map/ppermute | solution.py:355
  36.5 0.8 %unpack_heads.1 = bf16[128,1536]{1,0:T(8,128)(2,1)} custom-call(bf16[128,384]{1,0:T(8,128)(2,1)S(1)} %collective-permute-done.12.refs_0_, bf16[128,384]{1,0:T(8,128)(2,1)S(1)} %collective-permute-done.13.refs_1_, bf16[128,384]{1,0:T(8,128)(2,1)S(1)} %collective-permute-done.14.refs_2_, bf16[128,384]{1,0:T(8,128)(2,1)S(1)} %attend.7.refs_3_), custom_call_target="tpu_custom_call" | custom-call | bytes 786432 | tf_op jit(solution)/shard_map/unpack_heads/pallas_call | solution.py:306
  (33 shorter events, 0.8 us)
Async XLA Ops:
  1.8 4.0 %collective-permute-start.1 = (bf16[256,384]{1,0:T(8,128)(2,1)S(1)}, bf16[256,384]{1,0:T(8,128)(2,1)S(1)}, u32[]{:S(2)}, u32[]{:S(2)}) collective-permute-start(bf16[256,384]{1,0:T(8,128)(2,1)S(1)} %slice.51), channel_id=1, source_target_pairs={{0,4},{4,0},{8,12},{12,8},{16,20},{20,16},{24,28},{28,24},{1,5},{5... | collective-permute-start | bytes 589832 | tf_op jit(solution)/shard_map/ppermute | solution.py:361
  2.3 18.6 %collective-permute-start = (bf16[384,384]{1,0:T(8,128)(2,1)S(1)}, bf16[384,384]{1,0:T(8,128)(2,1)S(1)}, u32[]{:S(2)}, u32[]{:S(2)}) collective-permute-start(bf16[384,384]{1,0:T(8,128)(2,1)S(1)} %get-tuple-element.47), channel_id=1, source_target_pairs={{0,24},{4,28},{8,16},{12,20},{16,8},{20,12},{24,0},{28,4},{1,25},{... | collective-permute-start | bytes 884744 | tf_op jit(solution)/shard_map/ppermute | solution.py:347
  5.8 6.2 %collective-permute-start.2 = (bf16[4,2,16,384]{3,2,1,0:T(8,128)(2,1)S(1)}, bf16[4,2,16,384]{3,2,1,0:T(8,128)(2,1)S(1)}, u32[]{:S(2)}, u32[]{:S(2)}) collective-permute-start(bf16[4,2,16,384]{3,2,1,0:T(8,128)(2,1)S(1)} %get-tuple-element.57), channel_id=1, source_target_pairs={{0,1},{1,0},{2,3},{3,2},{4,5},{5,4},{6,7},{7,6},{8,9},{9,8},{10,11... | collective-permute-start | bytes 294920 | tf_op jit(solution)/shard_map/ppermute | solution.py:366
  7.4 8.0 %collective-permute-start.3 = (bf16[4,2,16,384]{3,2,1,0:T(8,128)(2,1)S(1)}, bf16[4,2,16,384]{3,2,1,0:T(8,128)(2,1)S(1)}, u32[]{:S(2)}, u32[]{:S(2)}) collective-permute-start(bf16[4,2,16,384]{3,2,1,0:T(8,128)(2,1)S(1)} %get-tuple-element.59), channel_id=1, source_target_pairs={{0,2},{1,3},{2,0},{3,1},{4,6},{5,7},{6,4},{7,5},{8,10},{9,11},{10,... | collective-permute-start | bytes 294920 | tf_op jit(solution)/shard_map/ppermute | solution.py:366
  10.1 12.3 %collective-permute-start.5 = (bf16[384,384]{1,0:T(8,128)(2,1)S(1)}, bf16[384,384]{1,0:T(8,128)(2,1)S(1)}, u32[]{:S(2)}, u32[]{:S(2)}) collective-permute-start(bf16[384,384]{1,0:T(8,128)(2,1)S(1)} %get-tuple-element.62), channel_id=1, source_target_pairs={{0,8},{4,12},{8,0},{12,4},{16,24},{20,28},{24,16},{28,20},{1,9},{5... | collective-permute-start | bytes 884744 | tf_op jit(solution)/shard_map/ppermute | solution.py:347
  10.6 11.8 %collective-permute-start.6 = (bf16[384,384]{1,0:T(8,128)(2,1)S(1)}, bf16[384,384]{1,0:T(8,128)(2,1)S(1)}, u32[]{:S(2)}, u32[]{:S(2)}) collective-permute-start(bf16[384,384]{1,0:T(8,128)(2,1)S(1)} %get-tuple-element.64), channel_id=1, source_target_pairs={{0,16},{4,20},{8,24},{12,28},{16,0},{20,4},{24,8},{28,12},{1,17},{... | collective-permute-start | bytes 884744 | tf_op jit(solution)/shard_map/ppermute | solution.py:347
  12.0 6.6 %collective-permute-start.4 = (bf16[4,2,16,384]{3,2,1,0:T(8,128)(2,1)S(1)}, bf16[4,2,16,384]{3,2,1,0:T(8,128)(2,1)S(1)}, u32[]{:S(2)}, u32[]{:S(2)}) collective-permute-start(bf16[4,2,16,384]{3,2,1,0:T(8,128)(2,1)S(1)} %get-tuple-element.60), channel_id=1, source_target_pairs={{0,3},{1,2},{2,1},{3,0},{4,7},{5,6},{6,5},{7,4},{8,11},{9,10},{10,... | collective-permute-start | bytes 294920 | tf_op jit(solution)/shard_map/ppermute | solution.py:366
  18.6 6.7 %collective-permute-start.7 = (bf16[128,384]{1,0:T(8,128)(2,1)S(1)}, bf16[128,384]{1,0:T(8,128)(2,1)S(1)}, u32[]{:S(2)}, u32[]{:S(2)}) collective-permute-start(bf16[128,384]{1,0:T(8,128)(2,1)S(1)} %interleave.4), channel_id=1, source_target_pairs={{0,24},{4,28},{8,16},{12,20},{16,8},{20,12},{24,0},{28,4},{1,25},{... | collective-permute-start | bytes 294920 | tf_op jit(solution)/shard_map/ppermute | solution.py:347
  20.3 5.1 %collective-permute-start.8 = (bf16[128,384]{1,0:T(8,128)(2,1)S(1)}, bf16[128,384]{1,0:T(8,128)(2,1)S(1)}, u32[]{:S(2)}, u32[]{:S(2)}) collective-permute-start(bf16[128,384]{1,0:T(8,128)(2,1)S(1)} %interleave.5), channel_id=1, source_target_pairs={{0,8},{4,12},{8,0},{12,4},{16,24},{20,28},{24,16},{28,20},{1,9},{5... | collective-permute-start | bytes 294920 | tf_op jit(solution)/shard_map/ppermute | solution.py:347
  20.9 4.7 %collective-permute-start.9 = (bf16[128,384]{1,0:T(8,128)(2,1)S(1)}, bf16[128,384]{1,0:T(8,128)(2,1)S(1)}, u32[]{:S(2)}, u32[]{:S(2)}) collective-permute-start(bf16[128,384]{1,0:T(8,128)(2,1)S(1)} %interleave.6), channel_id=1, source_target_pairs={{0,16},{4,20},{8,24},{12,28},{16,0},{20,4},{24,8},{28,12},{1,17},{... | collective-permute-start | bytes 294920 | tf_op jit(solution)/shard_map/ppermute | solution.py:347
  23.1 0.7 %copy-start = (s32[16,16]{1,0:T(8,128)S(1)}, s32[16,16]{1,0:T(8,128)}, u32[]{:S(2)}) copy-start(s32[16,16]{1,0:T(8,128)} %param.15) | copy-start | bytes 3076
  23.3 2.4 %collective-permute-start.11 = (bf16[3,256,384]{2,1,0:T(8,128)(2,1)S(1)}, bf16[3,256,384]{2,1,0:T(8,128)(2,1)S(1)}, u32[]{:S(2)}, u32[]{:S(2)}) collective-permute-start(bf16[3,256,384]{2,1,0:T(8,128)(2,1)S(1)} %join.3), channel_id=1, source_target_pairs={{0,4},{4,0},{8,12},{12,8},{16,20},{20,16},{24,28},{28,24},{1,5},{5... | collective-permute-start | bytes 1769480 | tf_op jit(solution)/shard_map/ppermute | solution.py:361
  25.6 1.8 %collective-permute-start.10 = (bf16[4,128,384]{2,1,0:T(8,128)(2,1)S(1)}, bf16[4,128,384]{2,1,0:T(8,128)(2,1)S(1)}, u32[]{:S(2)}, u32[]{:S(2)}) collective-permute-start(bf16[4,128,384]{2,1,0:T(8,128)(2,1)S(1)} %join.2), channel_id=1, source_target_pairs={{0,4},{4,0},{8,12},{12,8},{16,20},{20,16},{24,28},{28,24},{1,5},{5... | collective-permute-start | bytes 1179656 | tf_op jit(solution)/shard_map/ppermute | solution.py:361
  28.3 6.6 %collective-permute-start.12 = (bf16[128,384]{1,0:T(8,128)(2,1)S(1)}, bf16[128,384]{1,0:T(8,128)(2,1)S(1)}, u32[]{:S(2)}, u32[]{:S(2)}) collective-permute-start(bf16[128,384]{1,0:T(8,128)(2,1)S(1)} %get-tuple-element.86), channel_id=1, source_target_pairs={{0,24},{4,28},{8,16},{12,20},{16,8},{20,12},{24,0},{28,4},{1,25},{... | collective-permute-start | bytes 294920 | tf_op jit(solution)/shard_map/ppermute | solution.py:355
  29.8 6.7 %collective-permute-start.13 = (bf16[128,384]{1,0:T(8,128)(2,1)S(1)}, bf16[128,384]{1,0:T(8,128)(2,1)S(1)}, u32[]{:S(2)}, u32[]{:S(2)}) collective-permute-start(bf16[128,384]{1,0:T(8,128)(2,1)S(1)} %get-tuple-element.87), channel_id=1, source_target_pairs={{0,8},{4,12},{8,0},{12,4},{16,24},{20,28},{24,16},{28,20},{1,9},{5... | collective-permute-start | bytes 294920 | tf_op jit(solution)/shard_map/ppermute | solution.py:355
  31.2 5.3 %collective-permute-start.14 = (bf16[128,384]{1,0:T(8,128)(2,1)S(1)}, bf16[128,384]{1,0:T(8,128)(2,1)S(1)}, u32[]{:S(2)}, u32[]{:S(2)}) collective-permute-start(bf16[128,384]{1,0:T(8,128)(2,1)S(1)} %get-tuple-element.88), channel_id=1, source_target_pairs={{0,16},{4,20},{8,24},{12,28},{16,0},{20,4},{24,8},{28,12},{1,17},{... | collective-permute-start | bytes 294920 | tf_op jit(solution)/shard_map/ppermute | solution.py:355
